TPU v7x, 128 devices: a whole 4x4x4 slice. The times are simulated.
128 devices in a mesh: section: 2 (over core), edata: 4 (over y), expert: 16 (over x, z).
Axes of the slice: x: 4, y: 4, z: 4, core: 2. Of those that a mesh axis runs over, the one named last changes fastest.
Arguments:
- hidden_in: bfloat16 [2, 8192, 2048], P('section', ('edata', 'expert')), may hold values from -6 to 6
- out_grad: bfloat16 [2, 8192, 2048], P('section', ('edata', 'expert')), may hold values from -16 to 16
- routes: int32 [2, 8192, 8], P('section', ('edata', 'expert')), may hold values from 0 to 15, all different within a row; in each aligned block of 128 rows (0 to 127, 128 to 255, ..., all dimensions but the last counted through in order) at most 72 rows name the same one
- gates: float32 [2, 8192, 8], P('section', ('edata', 'expert')), may hold values from 0.05 to 0.5
- w_gate_up: bfloat16 [2, 16, 2048, 1536], P('section', 'expert'), may hold values from -0.125 to 0.125
- w_down: bfloat16 [2, 16, 768, 2048], P('section', 'expert'), may hold values from -0.21875 to 0.21875
Outputs:
- upstream_grad: bfloat16 [2, 8192, 2048], P('section', ('edata', 'expert'))
- gate_up_grad: bfloat16 [2, 16, 2048, 1536], P('section', 'expert', 'edata')
- down_grad: bfloat16 [2, 16, 768, 2048], P('section', 'expert', None, 'edata')
Inputs may be any that keep to these rules, and one draw needn't show every extreme that they name: `routes`: the 8 experts of a token are distinct. In the 128 tokens of one device no expert is chosen more than 72 times, a bound that some block reaches.
All inputs are finite; a program needn't handle non-finite values.
Results may differ from a plain program's by a relative error of at most 0.0058.
Values may be sent and summed in bfloat16 or wider, within the bound.
No kernel may reach another device: no remote copies, remote signals or barrier semaphores. Data moves between devices by JAX's collectives and lax.ppermute only.
A program may use at most 192 MiB of HBM per device.

v0:
```python
import jax
import jax.numpy as jnp
from jax import lax
from jax.sharding import PartitionSpec as P


def passed_along(block, axis, distance):
    devices = range(lax.axis_size(axis))
    route = [((i - distance) % len(devices), i) for i in devices]
    return lax.ppermute(block, axis, route)


def project_rows(xrows, wgu):
    return jnp.dot(xrows, wgu, preferred_element_type=jnp.float32)


def finish_rows(ab, srows, wgu, wdown, hidden):
    first = ab[:, :hidden]
    second = ab[:, hidden:]
    sig = jax.nn.sigmoid(first)
    hrows = (first * sig * second).astype(jnp.bfloat16)
    dh = jnp.dot(srows, wdown.T, preferred_element_type=jnp.float32)
    dfirst = dh * second * sig * (1.0 + first * (1.0 - sig))
    dsecond = dh * first * sig
    dab = jnp.concatenate([dfirst, dsecond], axis=1).astype(jnp.bfloat16)
    slot_grad = jnp.dot(dab, wgu.T, preferred_element_type=jnp.float32).astype(jnp.bfloat16)
    return (slot_grad, hrows, dab)


def body(hidden_in, out_grad, routes, gates, w_gate_up, w_down):
    tok = hidden_in.shape[1]
    width = hidden_in.shape[2]
    topk = routes.shape[2]
    local = w_down.shape[1]
    hidden = w_down.shape[2]
    owners = lax.axis_size("expert")
    experts = local * owners
    capacity = min(tok, tok * topk * 9 // (8 * experts))
    slots = tok * topk
    flat = routes[0].reshape(slots)
    onehot = (flat[:, None] == jnp.arange(experts, dtype=jnp.int32)[None, :]).astype(jnp.int32)
    before = jnp.cumsum(onehot, axis=0) - onehot
    place = jnp.sum(before * onehot, axis=1)
    target = flat * capacity + place
    table = (
        jnp.full((experts * capacity,), slots, jnp.int32)
        .at[target]
        .set(jnp.arange(slots, dtype=jnp.int32))
    )
    x_pad = jnp.concatenate([hidden_in[0], jnp.zeros((1, width), jnp.bfloat16)], axis=0)
    x_buf = x_pad[table // topk].reshape(experts, capacity, width)
    scaled = (gates[0][:, :, None] * out_grad[0][:, None, :].astype(jnp.float32)).astype(
        jnp.bfloat16
    )
    s_pad = jnp.concatenate(
        [scaled.reshape(slots, width), jnp.zeros((1, width), jnp.bfloat16)], axis=0
    )
    s_buf = s_pad[table].reshape(experts, capacity, width)
    x_recv, s_recv = (
        lax.all_to_all(x_buf, "expert", split_axis=0, concat_axis=0, tiled=True),
        lax.all_to_all(s_buf, "expert", split_axis=0, concat_axis=0, tiled=True),
    )
    x_recv = x_recv.reshape(owners, local, capacity, width)
    projected = [project_rows(x_recv[:, 0].reshape(owners * capacity, width), w_gate_up[0, 0])]
    s_recv = s_recv.reshape(owners, local, capacity, width)
    e = 0
    xrows = x_recv[:, e].reshape(owners * capacity, width)
    srows = s_recv[:, e].reshape(owners * capacity, width)
    slot_grad, hrows, dab = finish_rows(projected[e], srows, w_gate_up[0, e], w_down[0, e], hidden)
    x_rows = [xrows]
    s_rows = [srows]
    h_rows = [hrows]
    dab_rows = [dab]
    back = [slot_grad.reshape(owners, capacity, width)]
    send_back = jnp.stack(back, axis=1).reshape(experts, capacity, width)
    returned = lax.all_to_all(send_back, "expert", split_axis=0, concat_axis=0, tiled=True)
    ret_flat = returned.reshape(experts * capacity, width)
    gathered = ret_flat[target].reshape(tok, topk, width).astype(jnp.float32)
    layer_grad = (out_grad[0].astype(jnp.float32) + jnp.sum(gathered, axis=1)).astype(jnp.bfloat16)
    upstream = passed_along(layer_grad, "section", -1)
    e = 0
    xs = x_rows[e]
    ss = s_rows[e]
    gate_part = lax.dot_general(
        xs, dab_rows[e], (((0,), (0,)), ((), ())), preferred_element_type=jnp.float32
    )
    down_part = lax.dot_general(
        ss, h_rows[e], (((0,), (0,)), ((), ())), preferred_element_type=jnp.float32
    )
    parts = [jnp.concatenate([gate_part, down_part], axis=1)]
    summed = lax.psum_scatter(jnp.stack(parts, axis=1), "edata", scatter_dimension=0, tiled=True)
    gate_up_grad = jnp.transpose(summed[:, :, : 2 * hidden], (1, 0, 2)).astype(jnp.bfloat16)[None]
    down_grad = jnp.transpose(summed[:, :, 2 * hidden :], (1, 2, 0)).astype(jnp.bfloat16)[None]
    return (upstream[None], gate_up_grad, down_grad)


def solution(mesh):
    return jax.shard_map(
        body,
        mesh=mesh,
        in_specs=(
            P("section", ("edata", "expert"), None),
            P("section", ("edata", "expert"), None),
            P("section", ("edata", "expert"), None),
            P("section", ("edata", "expert"), None),
            P("section", "expert", None, None),
            P("section", "expert", None, None),
        ),
        out_specs=(
            P("section", ("edata", "expert"), None),
            P("section", "expert", "edata", None),
            P("section", "expert", None, "edata"),
        ),
        check_vma=False,
    )
```

profile of v0, /device:TPU:0, one launch (start us, length us, event | category | flops | bytes accessed | tf_op | source)
XLA Modules:
  0.0 398.4 jit_solution(9934869048361974155)
XLA Ops:
  7.2 0.8 broadcast_multiply_fusion
  8.0 0.9 copy.16
  9.3 4.5 %reduce-window.6 = s32[16,8,128]{2,1,0:T(8,128)S(1)} reduce-window(s32[16,8,128]{2,1,0:T(8,128)S(1)} %fusion.12, s32[]{:T(128)} %constant.12.clone.1), window={size=1x1x128 pad=0_0x0_0x127_0}, to_apply=%region_0.0 | reduce-window | flops 2080768 | bytes 131076 | tf_op jit(solution)/shard_map/reduce-window
  14.3 4.3 %scatter_custom_fusion = s32[1152]{0:T(1024)S(1)} fusion(s32[1024]{0:T(1024)S(1)} %bitcast.71, s32[1024]{0:T(1024)S(1)} %iota.11, s32[]{:T(128)} %constant.14.clone.1), kind=kCustom, calls=%fused_computation.46 | custom fusion | bytes 4612 | tf_op jit(solution)/shard_map/scatter | solution.py:48
  18.7 1.9 concatenate.14
  20.6 11.8 %gather_fusion.1 = bf16[1152,2048]{1,0:T(8,128)(2,1)} fusion(bf16[129,2048]{1,0:T(8,128)(2,1)} %concatenate.14, s32[2048]{0:T(1024)S(1)} %get-tuple-element.13), kind=kCustom, calls=%fused_computation.1 | custom fusion | bytes 9441792 | tf_op jit(solution)/shard_map/gather | solution.py:51
  32.4 8.1 %all-to-all-start.1 = ((bf16[16,72,2048]{2,1,0:T(8,128)(2,1)}), bf16[16,72,2048]{2,1,0:T(8,128)(2,1)}, u32[]{:S(2)}, u32[]{:S(2)}) async-start(bf16[16,72,2048]{2,1,0:T(8,128)(2,1)} %bitcast.63), calls=%async_computation.1 | async-start | bytes 9437184 | tf_op jit(solution)/shard_map/all_to_all | solution.py:60
  40.7 1.1 bitcast_convert_fusion
  41.9 0.9 fusion
  42.8 2.3 concatenate.13
  45.1 13.4 %gather_fusion = bf16[1152,2048]{1,0:T(8,128)(2,1)} fusion(bf16[1025,2048]{1,0:T(8,128)(2,1)} %concatenate.13, s32[2048]{0:T(1024)S(1)} %get-tuple-element.14), kind=kCustom, calls=%fused_computation | custom fusion | bytes 9441792 | tf_op jit(solution)/shard_map/gather | solution.py:58
  58.5 55.3 %all-to-all-done.1 = bf16[16,72,2048]{2,1,0:T(8,128)(2,1)} async-done(((bf16[16,72,2048]{2,1,0:T(8,128)(2,1)}), bf16[16,72,2048]{2,1,0:T(8,128)(2,1)}, u32[]{:S(2)}, u32[]{:S(2)}) %all-to-all-start.1) | async-done | bytes 4718624 | tf_op jit(solution)/shard_map/all_to_all | solution.py:60
  113.8 9.6 %all-to-all-start = ((bf16[16,72,2048]{2,1,0:T(8,128)(2,1)}), bf16[16,72,2048]{2,1,0:T(8,128)(2,1)}, u32[]{:S(2)}, u32[]{:S(2)}) async-start(bf16[16,72,2048]{2,1,0:T(8,128)(2,1)} %bitcast.64), calls=%async_computation | async-start | bytes 9437184 | tf_op jit(solution)/shard_map/all_to_all | solution.py:61
  123.7 13.7 %fusion.2 = f32[1152,1536]{0,1:T(8,128)} fusion(bf16[1152,2048]{1,0:T(8,128)(2,1)} %bitcast.12, bf16[1,1,2048,1536]{3,2,1,0:T(8,128)(2,1)} %param.10), kind=kOutput, calls=%fused_computation.10 | convolution fusion | flops 7247757312 | bytes 18087936 | tf_op jit(solution)/shard_map/dot_general | solution.py:14
  137.4 45.7 %all-to-all-done = bf16[16,72,2048]{2,1,0:T(8,128)(2,1)} async-done(((bf16[16,72,2048]{2,1,0:T(8,128)(2,1)}), bf16[16,72,2048]{2,1,0:T(8,128)(2,1)}, u32[]{:S(2)}, u32[]{:S(2)}) %all-to-all-start) | async-done | bytes 4718624 | tf_op jit(solution)/shard_map/all_to_all | solution.py:61
  183.1 8.0 %fusion.7 = f32[2048,768]{0,1:T(8,128)S(1)} fusion(bf16[1152,2048]{1,0:T(8,128)(2,1)} %bitcast.8, f32[1152,1536]{0,1:T(8,128)} %fusion.2), kind=kOutput, calls=%fused_computation.20 | convolution fusion | flops 3629187072 | bytes 18087936 | tf_op jit(solution)/shard_map/dot_general | solution.py:87
  191.2 8.9 %multiply_convert_fusion.2 = (bf16[1152,768]{0,1:T(8,128)(2,1)}, bf16[1152,768]{0,1:T(8,128)(2,1)}) fusion(f32[1152,1536]{0,1:T(8,128)S(1)} %copy-done.5, bf16[1152,2048]{1,0:T(8,128)(2,1)} %bitcast.8, bf16[1,1,768,2048]{3,2,1,0:T(8,128)(2,1)S(1)} %copy-done), kind=kOutput, calls=%fused_computation.15 | convolution fusion | flops 3635380224 | bytes 18481152 | tf_op jit(solution)/shard_map/dot_general | solution.py:22
  200.1 11.4 %fusion.6 = f32[2048,1536]{0,1:T(8,128)S(1)} fusion(bf16[1152,2048]{1,0:T(8,128)(2,1)} %bitcast.12, bf16[1152,768]{0,1:T(8,128)(2,1)} %get-tuple-element.10, bf16[1152,768]{0,1:T(8,128)(2,1)} %get-tuple-element.9), kind=kOutput, calls=%fused_computation.19 | convolution fusion | flops 7254835200 | bytes 20840448 | tf_op jit(solution)/shard_map/dot_general | solution.py:84
  211.5 7.2 %maximum_bitcast_fusion = f32[2048,1,2304]{0,2,1:T(8,128)} fusion(f32[2048,768]{0,1:T(8,128)S(1)} %fusion.7, f32[2048,1536]{0,1:T(8,128)S(1)} %fusion.6), kind=kLoop, calls=%fused_computation.4 | loop fusion | flops 4718592 | bytes 37748736 | tf_op jit(solution)/shard_map/stack | solution.py:91
  218.7 1.4 copy-done.6
  220.1 11.7 %convolution_convert_fusion = bf16[1152,2048]{1,0:T(8,128)(2,1)} fusion(bf16[1,1,2048,1536]{3,2,1,0:T(8,128)(2,1)} %param.10, bf16[1152,768]{0,1:T(8,128)(2,1)} %get-tuple-element.10, bf16[1152,768]{0,1:T(8,128)(2,1)S(1)} %copy-done.6), kind=kOutput, calls=%fused_computation.8 | convolution fusion | flops 7257194496 | bytes 14548992 | tf_op jit(solution)/shard_map/dot_general | solution.py:26
  231.8 4.6 %all-to-all-start.2 = ((bf16[16,72,2048]{2,1,0:T(8,128)(2,1)}), bf16[16,72,2048]{2,1,0:T(8,128)(2,1)}, u32[]{:S(2)}, u32[]{:S(2)}) async-start(bf16[16,72,2048]{2,1,0:T(8,128)(2,1)} %bitcast.65), calls=%async_computation.2 | async-start | bytes 9437184 | tf_op jit(solution)/shard_map/all_to_all | solution.py:76
  236.4 56.0 %all-to-all-done.2 = bf16[16,72,2048]{2,1,0:T(8,128)(2,1)} async-done(((bf16[16,72,2048]{2,1,0:T(8,128)(2,1)}), bf16[16,72,2048]{2,1,0:T(8,128)(2,1)}, u32[]{:S(2)}, u32[]{:S(2)}) %all-to-all-start.2) | async-done | bytes 4718624 | tf_op jit(solution)/shard_map/all_to_all | solution.py:76
  292.4 11.8 %gather_fusion.2 = bf16[1024,2048]{1,0:T(8,128)(2,1)} fusion(bf16[1152,2048]{1,0:T(8,128)(2,1)} %bitcast.15, s32[1024]{0:T(1024)S(1)} %broadcast_clamp_fusion), kind=kCustom, calls=%fused_computation.2 | custom fusion | bytes 8392704 | tf_op jit(solution)/shard_map/gather | solution.py:78
  304.2 5.1 %convert_reduce_fusion = f32[128,2048]{1,0:T(8,128)S(1)} fusion(bf16[1024,2048]{1,0:T(8,128)(2,1)} %gather_fusion.2), kind=kLoop, calls=%fused_computation.5 | loop fusion | flops 3932160 | bytes 5242880 | tf_op jit(solution)/shard_map/reduce_sum | solution.py:79
  309.5 1.9 collective-permute-done
  312.2 69.9 %reduce-scatter.2.cloned.1.call-done = f32[512,1,2304]{0,2,1:T(8,128)} async-done(((f32[2048,1,2304]{0,2,1:T(8,128)}), f32[512,1,2304]{0,2,1:T(8,128)}) %reduce-scatter.2.cloned.1.call-update) | async-done | bytes 4718608 | tf_op jit(solution)/shard_map/reduce_scatter | solution.py:91
  382.1 2.8 convert.14
  384.9 0.9 slice_bitcast_fusion.1
  385.8 1.3 slice_bitcast_fusion
  387.1 2.6 copy.22
  389.7 1.9 copy.27
  (36 shorter events, 2.3 us)
Async XLA Ops:
  7.2 184.0 %copy-start = (bf16[1,1,768,2048]{3,2,1,0:T(8,128)(2,1)S(1)}, bf16[1,1,768,2048]{3,2,1,0:T(8,128)(2,1)}, u32[]{:S(2)}) copy-start(bf16[1,1,768,2048]{3,2,1,0:T(8,128)(2,1)} %param.11) | copy-start | bytes 9437188
  32.4 8.1 %copy-start.4 = (f32[1,128,8]{1,2,0:T(8,128)S(1)}, f32[1,128,8]{1,2,0:T(8,128)}, u32[]{:S(2)}) copy-start(f32[1,128,8]{1,2,0:T(8,128)} %param.9) | copy-start | bytes 12292
  32.4 81.5 %all-to-all-start.1 = ((bf16[16,72,2048]{2,1,0:T(8,128)(2,1)}), bf16[16,72,2048]{2,1,0:T(8,128)(2,1)}, u32[]{:S(2)}, u32[]{:S(2)}) async-start(bf16[16,72,2048]{2,1,0:T(8,128)(2,1)} %bitcast.63), calls=%async_computation.1 | async-start | bytes 9437184 | tf_op jit(solution)/shard_map/all_to_all | solution.py:60
  113.8 69.3 %all-to-all-start = ((bf16[16,72,2048]{2,1,0:T(8,128)(2,1)}), bf16[16,72,2048]{2,1,0:T(8,128)(2,1)}, u32[]{:S(2)}, u32[]{:S(2)}) async-start(bf16[16,72,2048]{2,1,0:T(8,128)(2,1)} %bitcast.64), calls=%async_computation | async-start | bytes 9437184 | tf_op jit(solution)/shard_map/all_to_all | solution.py:61
  123.4 258.7 %reduce-scatter.2.cloned.1.call-start = ((), (), s32[]{:S(2)}) async-start(), calls=%async_computation.4 | async-start | bytes 23592960 | tf_op jit(solution)/shard_map/reduce_scatter | solution.py:91
  183.1 8.1 %copy-start.5 = (f32[1152,1536]{0,1:T(8,128)S(1)}, f32[1152,1536]{0,1:T(8,128)}, u32[]{:S(2)}) copy-start(f32[1152,1536]{0,1:T(8,128)} %fusion.2) | copy-start | bytes 21233668
  218.7 1.5 copy-start.6
  231.8 60.6 %all-to-all-start.2 = ((bf16[16,72,2048]{2,1,0:T(8,128)(2,1)}), bf16[16,72,2048]{2,1,0:T(8,128)(2,1)}, u32[]{:S(2)}, u32[]{:S(2)}) async-start(bf16[16,72,2048]{2,1,0:T(8,128)(2,1)} %bitcast.65), calls=%async_computation.2 | async-start | bytes 9437184 | tf_op jit(solution)/shard_map/all_to_all | solution.py:76
  304.2 5.1 %copy-start.2 = (bf16[1,128,2048]{2,1,0:T(8,128)(2,1)S(1)}, bf16[1,128,2048]{2,1,0:T(8,128)(2,1)}, u32[]{:S(2)}) copy-start(bf16[1,128,2048]{2,1,0:T(8,128)(2,1)} %param.7) | copy-start | bytes 1572868
  309.4 2.0 collective-permute-start
  311.4 0.8 copy-start.3
  382.1 9.5 %copy-start.1 = (bf16[1,1,768,2048]{3,2,1,0:T(8,128)(2,1)S(1)}, bf16[1,1,768,2048]{3,2,1,0:T(8,128)(2,1)}, u32[]{:S(2)}) copy-start(bf16[1,1,768,2048]{3,2,1,0:T(8,128)(2,1)} %param.11) | copy-start | bytes 9437188
Sparse Core Ops, SparseCore 0:
  218.8 163.2 reduce-scatter.1
where the time goes:
time: 400 us; the launch traced here: 398 us
  waiting for transfers between devices  229 us (57%)
  local copies, waits for them, and re-layouts  56.2 us (14%)
  matrix products  53.7 us (13%)
  other arithmetic  22.8 us (6%)
  starting transfers between devices  22.6 us (6%)
  between operations  14.2 us (4%)
    reduce_scatter x1, waiting for transfers between devices, body(): lax.psum_scatter(jnp.stack(parts, axis=1), 'edata', scatter_dimension=0,...  69.9 us
    all_to_all x1, waiting for transfers between devices, body(): lax.all_to_all(send_back, 'expert', split_axis=0, concat_axis=0, tiled=True)  56 us
    all_to_all x1, waiting for transfers between devices, body(): lax.all_to_all(x_buf, 'expert', split_axis=0, concat_axis=0, tiled=True)  55.3 us
    all_to_all x1, waiting for transfers between devices, body(): lax.all_to_all(s_buf, 'expert', split_axis=0, concat_axis=0, tiled=True)  45.7 us
    dot_general x1, matrix products, project_rows(): return jnp.dot(xrows, wgu, preferred_element_type=jnp.float32)  13.7 us
    gather x1, local copies, waits for them, and re-layouts, body(): s_buf = s_pad[table].reshape(experts, capacity, width)  13.4 us
    gather x1, local copies, waits for them, and re-layouts, body(): x_buf = x_pad[table // topk].reshape(experts, capacity, width)  11.8 us
    gather x1, local copies, waits for them, and re-layouts, body(): gathered = ret_flat[target].reshape(tok, topk, width).astype(jnp.float32)  11.8 us
  transfers between devices with their start and end apart: 5, of which 5 were waited for; matrix products, arithmetic and copies ran while one was open for 15% of the time, Pallas kernels for 0%

commit v1 on v0

v1 whole, which is shorter than its diff:
```python
import functools

import jax
import jax.numpy as jnp
from jax import lax
from jax.experimental import pallas as pl
from jax.experimental.pallas import tpu as pltpu
from jax.sharding import PartitionSpec as P

BF16 = jnp.bfloat16
F32 = jnp.float32
OFF = (0, 1, 3, 2)
SIDE = 4
LANES = 128
VMEM_LIMIT = 56 * 1024 * 1024


def params(steps):
    return pltpu.CompilerParams(
        vmem_limit_bytes=VMEM_LIMIT, dimension_semantics=("arbitrary",) * steps
    )


def cost(flops, moved):
    return pl.CostEstimate(flops=int(flops), bytes_accessed=int(moved), transcendentals=0)


def moved_along(block, axis, distance):
    if axis == "edata" or axis == "section":
        size = lax.axis_size(axis)
        return lax.ppermute(block, axis, [(i, (i + distance) % size) for i in range(size)])
    pairs = []
    for a in range(SIDE):
        for b in range(SIDE):
            if axis == "x":
                pairs.append((a * SIDE + b, (a + distance) % SIDE * SIDE + b))
            else:
                pairs.append((a * SIDE + b, a * SIDE + (b + distance) % SIDE))
    return lax.ppermute(block, "expert", pairs)


def iota(shape, dim):
    return lax.broadcasted_iota(jnp.int32, shape, dim)


def dot(a, b, da=1, db=0):
    return lax.dot_general(a, b, (((da,), (db,)), ((), ())), preferred_element_type=F32)


def prep_kernel(experts, routes_ref, gates_ref, x_ref, g_ref, xe_ref, ge_ref):
    tok, width = x_ref.shape
    topk = routes_ref.shape[1]
    lane = iota((tok, LANES), 1)
    expert = lax.rem(lane, experts)
    full = jnp.zeros((tok, LANES), F32)
    for k in range(topk):
        full += jnp.where(routes_ref[:, k : k + 1] == expert, gates_ref[:, k : k + 1], 0.0)
    high = full.astype(BF16).astype(F32)
    rest = full - high
    middle = rest.astype(BF16).astype(F32)
    low = rest - middle
    piece = jnp.where(lane < 2 * experts, middle, jnp.where(lane < 3 * experts, low, 0.0))
    piece = jnp.where(lane < experts, high, piece).astype(BF16)
    for src, dst in ((x_ref, xe_ref), (g_ref, ge_ref)):
        dst[:, :width] = src[...]
        dst[:, width:] = piece


def prep(routes, gates, x, g, experts):
    tok, width = x.shape
    shape = jax.ShapeDtypeStruct((tok, width + LANES), BF16)
    return pl.pallas_call(
        functools.partial(prep_kernel, experts),
        out_shape=(shape, shape),
        compiler_params=params(0),
        name="prep",
    )(routes, gates, x, g)


def pair_table(eids_ref, piece, experts, cap, lanes):
    rows = piece.shape[0]
    tok = rows // 2
    r, c = iota((rows, rows), 0), iota((rows, rows), 1)
    lower = jnp.where((c < r) & ((c >= tok) == (r >= tok)), 1.0, 0.0).astype(BF16)
    lane = iota((rows, LANES), 1)
    mask = jnp.where((lane < experts) & (piece.astype(F32) > 0.0), 1.0, 0.0)
    before = dot(lower, mask.astype(BF16))
    slot = iota((rows, lanes), 1)
    second = jnp.where(iota((rows, 1), 0) >= tok, cap, 0)
    table = jnp.zeros((rows, lanes), F32)
    for j in range(SIDE):
        here = lane == eids_ref[j]
        named = jnp.sum(jnp.where(here, mask, 0.0), axis=1, keepdims=True)
        place = jnp.sum(jnp.where(here, before, 0.0), axis=1, keepdims=True)
        target = jnp.where(named > 0.0, place.astype(jnp.int32) + second + 2 * cap * j, -1)
        table += jnp.where(slot == target, 1.0, 0.0)
    return table


def pack_kernel(scale, experts, cap, eids_ref, *refs):
    blocks, tails, outs = refs[:4], refs[4:8], refs[8:12]
    table_ref, gate_ref = refs[12:]
    pair = 2 * cap
    total = SIDE * pair
    lanes = -(-total // LANES) * LANES

    @pl.when(pl.program_id(0) == 0)
    def _():
        for p in range(2):
            piece = jnp.concatenate([tails[2 * p][...], tails[2 * p + 1][...]], axis=0)
            table = pair_table(eids_ref, piece, experts, cap, lanes).T[:total].astype(BF16)
            table_ref[p] = table
            if scale:
                packed = dot(table, piece)
                row = iota((total, LANES), 0)
                lane = iota((total, LANES), 1)
                want = jnp.full((total, LANES), eids_ref[0], jnp.int32)
                for j in range(1, SIDE):
                    want = jnp.where(row >= j * pair, eids_ref[j], want)
                mine = (lax.rem(lane, experts) == want) & (lane < 3 * experts)
                gate_ref[p] = jnp.sum(jnp.where(mine, packed, 0.0), axis=1, keepdims=True)

    for p in range(2):
        rows = jnp.concatenate([blocks[2 * p][...], blocks[2 * p + 1][...]], axis=0)
        packed = dot(table_ref[p], rows)
        if scale:
            packed = packed * gate_ref[p]
        packed = packed.astype(BF16)
        for j in range(SIDE):
            outs[j][p * pair : (p + 1) * pair, :] = packed[j * pair : (j + 1) * pair]


def pack(eids, blocks, width, experts, cap, scale):
    tok = blocks[0].shape[0]
    step = 512
    pair = 2 * cap
    last = width // LANES
    out = jax.ShapeDtypeStruct((2 * pair, width), BF16)
    return pl.pallas_call(
        functools.partial(pack_kernel, scale, experts, cap),
        grid=(width // step,),
        in_specs=[pl.BlockSpec(memory_space=pltpu.SMEM)]
        + [pl.BlockSpec((tok, step), lambda i: (0, i))] * 4
        + [pl.BlockSpec((tok, LANES), lambda i: (0, last))] * 4,
        out_specs=[pl.BlockSpec((2 * pair, step), lambda i: (0, i))] * 4,
        out_shape=[out] * 4,
        scratch_shapes=[
            pltpu.VMEM((2, SIDE * pair, 2 * tok), BF16),
            pltpu.VMEM((2, SIDE * pair, 1), F32),
        ],
        compiler_params=params(1),
        cost_estimate=cost(4 * SIDE * pair * 2 * tok * width, 8 * pair * width * 4),
        name="pack_scaled" if scale else "pack_rows",
    )(eids, *blocks, *blocks)


def unpack_kernel(experts, cap, eids_ref, *refs):
    tails, rets, outs = refs[:4], refs[4:8], refs[8:12]
    table_ref = refs[12]
    tok = tails[0].shape[0]
    pair = 2 * cap
    lanes = table_ref.shape[2]
    fill = lanes - SIDE * pair

    @pl.when(pl.program_id(0) == 0)
    def _():
        for p in range(2):
            piece = jnp.concatenate([tails[2 * p][...], tails[2 * p + 1][...]], axis=0)
            table_ref[p] = pair_table(eids_ref, piece, experts, cap, lanes).astype(BF16)

    for p in range(2):
        parts = [rets[j][p * pair : (p + 1) * pair, :] for j in range(SIDE)]
        parts.append(jnp.zeros((fill, rets[0].shape[1]), BF16))
        dense = dot(table_ref[p], jnp.concatenate(parts, axis=0))
        for s in range(2):
            outs[2 * p + s][...] = dense[s * tok : (s + 1) * tok].astype(outs[2 * p + s].dtype)


def unpack(eids, blocks, rets, width, experts, cap):
    tok = blocks[0].shape[0]
    pair = 2 * cap
    lanes = -(-SIDE * pair // LANES) * LANES
    cols = rets[0].shape[1]
    step = 512
    last = width // LANES
    return pl.pallas_call(
        functools.partial(unpack_kernel, experts, cap),
        grid=(cols // step,),
        in_specs=[pl.BlockSpec(memory_space=pltpu.SMEM)]
        + [pl.BlockSpec((tok, LANES), lambda i: (0, last))] * 4
        + [pl.BlockSpec((2 * pair, step), lambda i: (0, i))] * 4,
        out_specs=[pl.BlockSpec((tok, step), lambda i: (0, i))] * 4,
        out_shape=[jax.ShapeDtypeStruct((tok, cols), F32)]
        + [jax.ShapeDtypeStruct((tok, cols), BF16)] * 3,
        scratch_shapes=[pltpu.VMEM((2, 2 * tok, lanes), BF16)],
        compiler_params=params(1),
        cost_estimate=cost(4 * SIDE * pair * 2 * tok * cols, 8 * pair * cols * 2),
        name="unpack",
    )(eids, *blocks, *rets)


def up_kernel(count, *refs):
    xs, (wa, wb), outs = refs[:count], refs[count : count + 2], refs[count + 2 :]
    for i in range(count):
        rows = xs[i][...]
        a = dot(rows, wa[...])
        b = dot(rows, wb[...])
        sig = jax.nn.sigmoid(a)
        outs[3 * i][...] = a * sig * b
        outs[3 * i + 1][...] = b * sig * (1.0 + a * (1.0 - sig))
        outs[3 * i + 2][...] = a * sig


def up(xs, wgu):
    count = len(xs)
    rows, width = xs[0].shape
    hidden = wgu.shape[1] // 2
    step = 256
    steps = hidden // step
    out = jax.ShapeDtypeStruct((rows, hidden), F32)
    flat = pl.pallas_call(
        functools.partial(up_kernel, count),
        grid=(steps,),
        in_specs=[pl.BlockSpec((rows, width), lambda i: (0, 0))] * count
        + [
            pl.BlockSpec((width, step), lambda i: (0, i)),
            pl.BlockSpec((width, step), lambda i: (0, i + steps)),
        ],
        out_specs=[pl.BlockSpec((rows, step), lambda i: (0, i))] * (3 * count),
        out_shape=[out] * (3 * count),
        compiler_params=params(1),
        cost_estimate=cost(
            4 * count * rows * width * hidden,
            2 * count * rows * width + 4 * width * hidden + 12 * count * rows * hidden,
        ),
        name="up",
    )(*xs, wgu, wgu)
    return [flat[3 * i : 3 * i + 3] for i in range(count)]


def dh_kernel(count, *refs):
    ss, wd, outs = refs[:count], refs[count], refs[count + 1 :]
    for i in range(count):
        outs[i][...] = dot(ss[i][...], wd[...], 1, 1)


def dh_of(ss, wdown):
    count = len(ss)
    rows, width = ss[0].shape
    hidden = wdown.shape[0]
    step = 256
    return pl.pallas_call(
        functools.partial(dh_kernel, count),
        grid=(hidden // step,),
        in_specs=[pl.BlockSpec((rows, width), lambda i: (0, 0))] * count
        + [pl.BlockSpec((step, width), lambda i: (i, 0))],
        out_specs=[pl.BlockSpec((rows, step), lambda i: (0, i))] * count,
        out_shape=[jax.ShapeDtypeStruct((rows, hidden), F32)] * count,
        compiler_params=params(1),
        cost_estimate=cost(
            2 * count * rows * width * hidden,
            2 * count * rows * width + 2 * width * hidden + 4 * count * rows * hidden,
        ),
        name="dh",
    )(*ss, wdown)


def crossed(refs, j, cap):
    return jnp.concatenate([ref[j * cap : (j + 1) * cap, :] for ref in refs], axis=0)


def keep_quarter(step, part, own, first_up, first_down, wait_up, wait_down):
    half = part.shape[0] // 2

    @pl.when(step == 0)
    def _():
        first_up[:half, :] = part[:half].astype(BF16)
        first_down[half:, :] = part[half:].astype(BF16)

    @pl.when(step == 1)
    def _():
        wait_up[...] = part[:half]
        first_up[half:, :] = part[half:].astype(BF16)

    @pl.when(step == 2)
    def _():
        first_down[:half, :] = part[:half].astype(BF16)
        wait_down[...] = part[half:]

    @pl.when(step == 3)
    def _():
        own[...] = part


STEPS = (2, 1, 3, 0)


def quarter_of(step, place_ref):
    ahead = jnp.where(step == 0, 2, jnp.where(step == 1, 1, jnp.where(step == 2, 3, 0)))
    return lax.rem(place_ref[0] + ahead, SIDE)


def quarter_outs(shape):
    rows, cols = shape
    shapes = [
        ((rows, cols), F32),
        ((rows, cols), BF16),
        ((rows, cols), BF16),
        ((rows // 2, cols), F32),
        ((rows // 2, cols), F32),
    ]
    return (
        [jax.ShapeDtypeStruct(s, t) for s, t in shapes],
        [pl.BlockSpec(s, lambda i, place: (0, 0)) for s, t in shapes],
    )


def down_kernel(cap, place_ref, *refs):
    hs, ss, outs, turned = refs[:4], refs[4:8], refs[8:13], refs[13]
    step = pl.program_id(0)

    @pl.when(step == 0)
    def _():
        rows = jnp.concatenate([crossed(hs, j, cap) for j in range(SIDE)], axis=0)
        turned[...] = rows.T.astype(BF16)

    rows = jnp.concatenate([s[...] for s in ss], axis=0)
    keep_quarter(step, dot(turned[...], rows), *outs)


def down_parts(place, hs, ss, cap):
    rows, hidden = hs[0].shape
    width = ss[0].shape[1]
    quarter = width // SIDE
    shapes, specs = quarter_outs((hidden, quarter))
    return pl.pallas_call(
        functools.partial(down_kernel, cap),
        grid_spec=pltpu.PrefetchScalarGridSpec(
            num_scalar_prefetch=1,
            grid=(SIDE,),
            in_specs=[pl.BlockSpec((rows, hidden), lambda i, place: (0, 0))] * 4
            + [pl.BlockSpec((rows, quarter), lambda i, place: (0, quarter_of(i, place)))] * 4,
            out_specs=specs,
            scratch_shapes=[pltpu.VMEM((hidden, SIDE * rows), BF16)],
        ),
        out_shape=shapes,
        compiler_params=params(1),
        cost_estimate=cost(8 * rows * width * hidden, 16 * rows * hidden + 8 * rows * width),
        name="down_parts",
    )(place, *hs, *ss)


def dab_kernel(cap, *refs):
    cas, cbs, dhs, outs = refs[:4], refs[4:8], refs[8:12], refs[12:]
    for i in range(SIDE):
        hidden = dhs[0].shape[1]
        dh = crossed(dhs, i, cap)
        outs[i][:, :hidden] = (dh * cas[i][...]).astype(BF16)
        outs[i][:, hidden:] = (dh * cbs[i][...]).astype(BF16)


def dab_of(cas, cbs, dhs, cap):
    rows, hidden = dhs[0].shape
    return pl.pallas_call(
        functools.partial(dab_kernel, cap),
        out_shape=[jax.ShapeDtypeStruct((rows, 2 * hidden), BF16)] * 4,
        compiler_params=params(0),
        cost_estimate=cost(8 * rows * hidden, 16 * rows * hidden * 4),
        name="dab",
    )(*cas, *cbs, *dhs)


def gate_up_kernel(place_ref, *refs):
    xs, ds, outs = refs[:4], refs[4:8], refs[8:13]
    total = dot(xs[0][...], ds[0][...], 0, 0)
    for i in range(1, SIDE):
        total += dot(xs[i][...], ds[i][...], 0, 0)
    keep_quarter(pl.program_id(0), total, *outs)


def gate_up_parts(place, xs, ds):
    rows, width = xs[0].shape
    both = ds[0].shape[1]
    quarter = width // SIDE
    shapes, specs = quarter_outs((quarter, both))
    return pl.pallas_call(
        gate_up_kernel,
        grid_spec=pltpu.PrefetchScalarGridSpec(
            num_scalar_prefetch=1,
            grid=(SIDE,),
            in_specs=[pl.BlockSpec((rows, quarter), lambda i, place: (0, quarter_of(i, place)))] * 4
            + [pl.BlockSpec((rows, both), lambda i, place: (0, 0))] * 4,
            out_specs=specs,
        ),
        out_shape=shapes,
        compiler_params=params(1),
        cost_estimate=cost(8 * rows * width * both, 8 * rows * (width + both)),
        name="gate_up_parts",
    )(place, *xs, *ds)


def slot_body(cap, cross, *refs):
    ds, w, outs = refs[:4], refs[4], refs[5:9]
    if not cross:
        for i in range(SIDE):
            outs[i][...] = dot(ds[i][...], w[...], 1, 1).astype(BF16)
        return
    parts = [dot(ds[i][...], w[...], 1, 1) for i in range(SIDE)]
    for j in range(SIDE):
        rows = [part[j * cap : (j + 1) * cap] for part in parts]
        outs[j][...] = jnp.concatenate(rows, axis=0).astype(BF16)


def slot_rows(ds, wgu, first, cols, cap, cross):
    rows, both = ds[0].shape
    step = 512
    base = first // step
    return pl.pallas_call(
        functools.partial(slot_body, cap, cross),
        grid=(cols // step,),
        in_specs=[pl.BlockSpec((rows, both), lambda i: (0, 0))] * 4
        + [pl.BlockSpec((step, both), lambda i: (base + i, 0))],
        out_specs=[pl.BlockSpec((rows, step), lambda i: (0, i))] * 4,
        out_shape=[jax.ShapeDtypeStruct((rows, cols), BF16)] * 4,
        compiler_params=params(1),
        cost_estimate=cost(8 * rows * both * cols, 8 * rows * (both + cols) + 2 * both * cols),
        name="slot_rows",
    )(*ds, wgu)


def around(first, axis):
    return [first] + [moved_along(first, axis, OFF[b]) for b in range(1, SIDE)]


def spread(outs, axis):
    near = [moved_along(outs[j], axis, OFF[j]) for j in (1, 2)]
    far, n0, n1 = lax.optimization_barrier((outs[3], near[0], near[1]))
    return [outs[0], n0, n1, moved_along(far, axis, OFF[3])]


def ring_sum(own, first_up, first_down, wait_up, wait_down):
    half = wait_up.shape[0]
    up1 = moved_along(first_up, "edata", 1)
    down1 = moved_along(first_down, "edata", -1)
    second_up = (wait_up + up1[:half].astype(F32)).astype(BF16)
    second_down = (wait_down + down1[half:].astype(F32)).astype(BF16)
    up2 = moved_along(second_up, "edata", 1)
    down2 = moved_along(second_down, "edata", -1)
    upper = own[:half] + down1[:half].astype(F32) + up2.astype(F32)
    lower = own[half:] + up1[half:].astype(F32) + down2.astype(F32)
    return jnp.concatenate([upper, lower], axis=0).astype(BF16)


def body(hidden_in, out_grad, routes, gates, w_gate_up, w_down):
    tok = hidden_in.shape[1]
    width = hidden_in.shape[2]
    topk = routes.shape[2]
    experts = lax.axis_size("expert")
    cap = min(tok, tok * topk * 9 // (8 * experts))
    half = width // 2
    wgu, wdown = w_gate_up[0, 0], w_down[0, 0]
    me = lax.axis_index("expert")
    mx, mz = me // SIDE, me % SIDE
    off = jnp.array(OFF, jnp.int32)
    eids_x = (mx * SIDE + (mz + off) % SIDE).astype(jnp.int32)
    eids_g = ((mx + off) % SIDE * SIDE + mz).astype(jnp.int32)
    place = lax.axis_index("edata").astype(jnp.int32).reshape(1)

    xe, ge = prep(routes[0], gates[0], hidden_in[0], out_grad[0], experts)
    xblocks = around(xe, "x")
    gblocks = around(ge, "z")
    xs = spread(pack(eids_x, xblocks, width, experts, cap, False), "z")
    ss = spread(pack(eids_g, gblocks, width, experts, cap, True), "x")

    ups = up(xs[:3], wgu) + up(xs[3:], wgu)
    dhs = dh_of(ss[:3], wdown) + dh_of(ss[3:], wdown)
    hs, cas, cbs = ([u[k] for u in ups] for k in range(3))
    down = down_parts(place, hs, ss, cap)
    ds = dab_of(cas, cbs, dhs, cap)
    gate_up = gate_up_parts(place, xs, ds)

    left = slot_rows(ds, wgu, 0, half, cap, False)
    right = slot_rows(ds, wgu, half, half, cap, True)
    back_l = [left[0]] + [moved_along(left[j], "z", -OFF[j]) for j in range(1, SIDE)]
    back_r = [right[0]] + [moved_along(right[j], "x", -OFF[j]) for j in range(1, SIDE)]
    home_l = unpack(eids_x, xblocks, back_l, width, experts, cap)
    home_r = unpack(eids_g, gblocks, back_r, width, experts, cap)
    sums = []
    for parts, axis in ((home_l, "x"), (home_r, "z")):
        total = parts[0]
        for b in range(1, SIDE):
            total = total + moved_along(parts[b], axis, -OFF[b]).astype(F32)
        sums.append(total)
    layer = (out_grad[0].astype(F32) + jnp.concatenate(sums, axis=1)).astype(BF16)
    upstream = moved_along(layer, "section", -1)

    down_grad = ring_sum(*down)
    gate_up_grad = ring_sum(*gate_up)
    return (upstream[None], gate_up_grad[None, None], down_grad[None, None])


def solution(mesh):
    return jax.shard_map(
        body,
        mesh=mesh,
        in_specs=(
            P("section", ("edata", "expert"), None),
            P("section", ("edata", "expert"), None),
            P("section", ("edata", "expert"), None),
            P("section", ("edata", "expert"), None),
            P("section", "expert", None, None),
            P("section", "expert", None, None),
        ),
        out_specs=(
            P("section", ("edata", "expert"), None),
            P("section", "expert", "edata", None),
            P("section", "expert", None, "edata"),
        ),
        check_vma=False,
    )
```

time: 400 us -> 247 us (0.62)
  waiting for transfers between devices: 229 us -> 72.4 us
  Pallas kernels: 0 us -> 106 us
  matrix products: 53.7 us -> 0 us
  local copies, waits for them, and re-layouts: 56.2 us -> 8.96 us
  starting transfers between devices: 22.6 us -> 52.6 us
  other arithmetic: 22.8 us -> 5.47 us
  between operations: 14.2 us -> 0.97 us
    all_to_all x3 -> x0, waiting for transfers between devices: 157 us -> none  [the longest x1 56 us: body(): lax.all_to_all(send_back, 'expert', split_axis=0, concat_axis=0, tiled=True)]
    pallas_call x0 -> x14, Pallas kernels: none -> 106 us  [the longest x1 20.9 us: gate_up_parts(): pl.pallas_call(gate_up_kernel, grid_spec=pltpu.PrefetchScalarGridSpec(num...]
    ppermute x1 -> x33, waiting for transfers between devices: 1.9 us -> 72.4 us  [the longest x24 50.8 us: moved_along(): return lax.ppermute(block, 'expert', pairs)]
    reduce_scatter x1 -> x0, waiting for transfers between devices: 69.9 us -> none  [body(): lax.psum_scatter(jnp.stack(parts, axis=1), 'edata', scatter_dimension=0,...]
    dot_general x5 -> x0, matrix products: 53.7 us -> none  [the longest x1 13.7 us: project_rows(): return jnp.dot(xrows, wgu, preferred_element_type=jnp.float32)]
    ppermute x1 -> x33, starting transfers between devices: 0.09 us -> 52.6 us  [the longest x24 38.9 us: moved_along(): return lax.ppermute(block, 'expert', pairs)]
    gather x3 -> x0, local copies, waits for them, and re-layouts: 37 us -> none  [the longest x1 13.4 us: body(): s_buf = s_pad[table].reshape(experts, capacity, width)]
    all_to_all x3 -> x0, starting transfers between devices: 22.3 us -> none  [the longest x1 9.6 us: body(): lax.all_to_all(s_buf, 'expert', split_axis=0, concat_axis=0, tiled=True)]
  transfers between devices with their start and end apart: 5 -> 33, of which waited for: 5 -> 13; matrix products, arithmetic and copies ran while one was open for 15% -> 1% of each run, Pallas kernels for 0% -> 35%
where the time goes in v1:
time: 247 us; the launch traced here: 246 us
  Pallas kernels  106 us (43%)
  waiting for transfers between devices  72.4 us (29%)
  starting transfers between devices  52.6 us (21%)
  local copies, waits for them, and re-layouts  8.96 us (4%)
  other arithmetic  5.47 us (2%)
    ppermute x24, waiting for transfers between devices, moved_along(): return lax.ppermute(block, 'expert', pairs)  50.8 us
    ppermute x24, starting transfers between devices, moved_along(): return lax.ppermute(block, 'expert', pairs)  38.9 us
    ppermute x9, waiting for transfers between devices, moved_along(): lax.ppermute(block, axis, [(i, (i + distance) % size) for i in range(size)])  21.6 us
    pallas_call x1, Pallas kernels, gate_up_parts(): pl.pallas_call(gate_up_kernel, grid_spec=pltpu.PrefetchScalarGridSpec(num...  20.9 us
    pallas_call x2, Pallas kernels, up(): pl.pallas_call(functools.partial(up_kernel, count), grid=(steps,), in_spe...  17.1 us
    pallas_call x2, Pallas kernels, slot_rows(): pl.pallas_call(functools.partial(slot_body, cap, cross), grid=(cols // st...  14.9 us
    ppermute x9, starting transfers between devices, moved_along(): lax.ppermute(block, axis, [(i, (i + distance) % size) for i in range(size)])  13.7 us
    pallas_call x2, Pallas kernels, pack(): pl.pallas_call(functools.partial(pack_kernel, scale, experts, cap), grid=...  13.6 us
  transfers between devices with their start and end apart: 33, of which 13 were waited for; matrix products, arithmetic and copies ran while one was open for 1% of the time, Pallas kernels for 35%

profile of v1, /device:TPU:0, one launch (start us, length us, event | category | flops | bytes accessed | tf_op | source)
XLA Modules:
  0.0 246.4 jit_solution(14915640327415445789)
XLA Ops:
  3.5 2.7 %prep.1 = (bf16[128,2176]{1,0:T(8,128)(2,1)}, bf16[128,2176]{1,0:T(8,128)(2,1)}) custom-call(s32[128,8]{1,0:T(8,128)} %bitcast.28, f32[128,8]{1,0:T(8,128)} %bitcast.29, bf16[128,2048]{1,0:T(8,128)(2,1)} %bitcast.26, bf16[128,2048]{1,0:T(8,128)(2,1)} %bitcast.25), custom_call_target="tpu_custom_call" | custom-call | tf_op jit(solution)/shard_map/prep/pallas_call | solution.py:72
  15.3 6.5 %collective-permute-done.refs_1_.refs_5_ = bf16[128,2176]{1,0:T(8,128)(2,1)S(1)} collective-permute-done((bf16[128,2176]{1,0:T(8,128)(2,1)}, bf16[128,2176]{1,0:T(8,128)(2,1)S(1)}, u32[]{:S(2)}, u32[]{:S(2)}) %collective-permute-start) | collective-permute-done | bytes 557088 | tf_op jit(solution)/shard_map/ppermute | solution.py:39
  21.8 4.2 %collective-permute-start.8 = (bf16[128,2176]{1,0:T(8,128)(2,1)}, bf16[128,2176]{1,0:T(8,128)(2,1)S(1)}, u32[]{:S(2)}, u32[]{:S(2)}) collective-permute-start(bf16[128,2176]{1,0:T(8,128)(2,1)} %get-tuple-element.80.refs_0_.refs_4_), channel_id=1, source_target_pairs={{0,2},{1,3},{2,0},{3,1},{4,6},{5,7},{6,4},{7,5},{8,10},{9,11},{10,... | collective-permute-start | bytes 1671176 | tf_op jit(solution)/shard_map/ppermute | solution.py:39
  27.2 7.8 %collective-permute-done.2.refs_3_.refs_7_ = bf16[128,2176]{1,0:T(8,128)(2,1)} collective-permute-done((bf16[128,2176]{1,0:T(8,128)(2,1)}, bf16[128,2176]{1,0:T(8,128)(2,1)}, u32[]{:S(2)}, u32[]{:S(2)}) %collective-permute-start.2) | collective-permute-done | bytes 557088 | tf_op jit(solution)/shard_map/ppermute | solution.py:39
  35.0 6.6 %pack_rows.1 = (bf16[288,2048]{1,0:T(8,128)(2,1)}, bf16[288,2048]{1,0:T(8,128)(2,1)}, bf16[288,2048]{1,0:T(8,128)(2,1)}, bf16[288,2048]{1,0:T(8,128)(2,1)}) custom-call(s32[4]{0:T(128)} %get-tuple-element.129.eids_ref, bf16[128,2176]{1,0:T(8,128)(2,1)} %get-tuple-element.64.refs_0_.refs_4_, bf16[128,2176]{1,0:T(8,128)(2,1)} %copy-done.18, ...), custom_call_target="tpu_custom_call" | custom-call | flops 1207959552 | bytes 9437184 | tf_op jit(solution)/shard_map/pack_rows/pallas_call | solution.py:139
  47.1 7.0 %pack_scaled.1 = (bf16[288,2048]{1,0:T(8,128)(2,1)}, bf16[288,2048]{1,0:T(8,128)(2,1)}, bf16[288,2048]{1,0:T(8,128)(2,1)}, bf16[288,2048]{1,0:T(8,128)(2,1)}) custom-call(s32[4]{0:T(128)} %get-tuple-element.130.eids_ref, bf16[128,2176]{1,0:T(8,128)(2,1)} %get-tuple-element.80.refs_0_.refs_4_, bf16[128,2176]{1,0:T(8,128)(2,1)} %copy-done.15, ...), custom_call_target="tpu_custom_call" | custom-call | flops 1207959552 | bytes 9437184 | tf_op jit(solution)/shard_map/pack_scaled/pallas_call | solution.py:139
  54.1 2.7 %collective-permute-start.10 = (bf16[288,2048]{1,0:T(8,128)(2,1)}, bf16[288,2048]{1,0:T(8,128)(2,1)S(1)}, u32[]{:S(2)}, u32[]{:S(2)}) collective-permute-start(bf16[288,2048]{1,0:T(8,128)(2,1)} %get-tuple-element.84), channel_id=1, source_target_pairs={{0,12},{1,13},{2,14},{3,15},{4,0},{5,1},{6,2},{7,3},{8,4},{9,5},{1... | collective-permute-start | bytes 3538952 | tf_op jit(solution)/shard_map/ppermute | solution.py:39
  56.8 14.2 %collective-permute-done.3.refs_1_ = bf16[288,2048]{1,0:T(8,128)(2,1)S(1)} collective-permute-done((bf16[288,2048]{1,0:T(8,128)(2,1)}, bf16[288,2048]{1,0:T(8,128)(2,1)S(1)}, u32[]{:S(2)}, u32[]{:S(2)}) %collective-permute-start.3) | collective-permute-done | bytes 1179680 | tf_op jit(solution)/shard_map/ppermute | solution.py:39
  71.0 2.9 %collective-permute-start.5 = (bf16[288,2048]{1,0:T(8,128)(2,1)}, bf16[288,2048]{1,0:T(8,128)(2,1)S(1)}, u32[]{:S(2)}, u32[]{:S(2)}) collective-permute-start(bf16[288,2048]{1,0:T(8,128)(2,1)} %get-tuple-element.74), channel_id=1, source_target_pairs={{0,2},{1,3},{2,0},{3,1},{4,6},{5,7},{6,4},{7,5},{8,10},{9,11},{10,... | collective-permute-start | bytes 3538952 | tf_op jit(solution)/shard_map/ppermute | solution.py:39
  74.0 7.0 %collective-permute-done.10.refs_2_.refs_6_ = bf16[288,2048]{1,0:T(8,128)(2,1)S(1)} collective-permute-done((bf16[288,2048]{1,0:T(8,128)(2,1)}, bf16[288,2048]{1,0:T(8,128)(2,1)S(1)}, u32[]{:S(2)}, u32[]{:S(2)}) %collective-permute-start.10) | collective-permute-done | bytes 1179680 | tf_op jit(solution)/shard_map/ppermute | solution.py:39
  84.6 6.8 %dh.2 = (f32[288,768]{1,0:T(8,128)}, f32[288,768]{1,0:T(8,128)}, f32[288,768]{1,0:T(8,128)}) custom-call(bf16[288,2048]{1,0:T(8,128)(2,1)} %get-tuple-element.81.refs_0_.refs_4_, bf16[288,2048]{1,0:T(8,128)(2,1)} %copy-done.25, bf16[288,2048]{1,0:T(8,128)(2,1)} %copy-done.24, bf16[768,2048]{1,0:T(8,128)(2,1)} %bitcast.23), custom_call_target="tpu_custom_call" | custom-call | flops 2717908992 | bytes 9338880 | tf_op jit(solution)/shard_map/dh/pallas_call | solution.py:252
  91.4 10.1 %up.2 = (f32[288,768]{1,0:T(8,128)}, f32[288,768]{1,0:T(8,128)}, f32[288,768]{1,0:T(8,128)}, f32[288,768]{1,0:T(8,128)}, f32[288,768]{1,0:T(8,128)}, /*index=5*/...) custom-call(bf16[288,2048]{1,0:T(8,128)(2,1)} %get-tuple-element.65.refs_0_, ...), custom_call_target="tpu_custom_call" | custom-call | flops 5435817984 | bytes 17793024 | tf_op jit(solution)/shard_map/up/pallas_call | solution.py:221
  102.5 7.1 %up.3 = (f32[288,768]{1,0:T(8,128)}, f32[288,768]{1,0:T(8,128)}, f32[288,768]{1,0:T(8,128)}) custom-call(bf16[288,2048]{1,0:T(8,128)(2,1)} %copy-done.6, bf16[2048,1536]{1,0:T(8,128)(2,1)} %bitcast.19, bf16[2048,1536]{1,0:T(8,128)(2,1)} %bitcast.20), custom_call_target="tpu_custom_call" | custom-call | flops 1811939328 | bytes 10125312 | tf_op jit(solution)/shard_map/up/pallas_call | solution.py:221
  111.4 4.7 %dh.3.refs_11_ = f32[288,768]{1,0:T(8,128)} custom-call(bf16[288,2048]{1,0:T(8,128)(2,1)} %copy-done.5, bf16[768,2048]{1,0:T(8,128)(2,1)} %bitcast.24), custom_call_target="tpu_custom_call" | custom-call | flops 905969664 | bytes 5210112 | tf_op jit(solution)/shard_map/dh/pallas_call | solution.py:252
  116.0 6.1 %dab.1 = (bf16[288,1536]{1,0:T(8,128)(2,1)}, bf16[288,1536]{1,0:T(8,128)(2,1)}, bf16[288,1536]{1,0:T(8,128)(2,1)}, bf16[288,1536]{1,0:T(8,128)(2,1)}) custom-call(f32[288,768]{1,0:T(8,128)} %get-tuple-element.71.refs_0_, f32[288,768]{1,0:T(8,128)} %get-tuple-element.72.refs_1_, f32[288,768]{1,0:T(8,128)} %get-tuple-element.73.refs_2_, ...), custom_call_target="tpu_custom_call" | custom-call | flops 1769472 | bytes 14155776 | tf_op jit(solution)/shard_map/dab/pallas_call | solution.py:364
  122.1 7.3 %slot_rows.2 = (bf16[288,1024]{1,0:T(8,128)(2,1)}, bf16[288,1024]{1,0:T(8,128)(2,1)}, bf16[288,1024]{1,0:T(8,128)(2,1)}, bf16[288,1024]{1,0:T(8,128)(2,1)}) custom-call(bf16[288,1536]{1,0:T(8,128)(2,1)} %get-tuple-element.91.refs_0_.refs_4_, bf16[288,1536]{1,0:T(8,128)(2,1)} %get-tuple-element.92.refs_1_.refs_5_, ...), custom_call_target="tpu_custom_call" | custom-call | flops 3623878656 | bytes 9043968 | tf_op jit(solution)/shard_map/slot_rows/pallas_call | solution.py:418
  132.7 10.5 %down_parts.1 = (f32[768,512]{1,0:T(8,128)}, bf16[768,512]{1,0:T(8,128)(2,1)}, bf16[768,512]{1,0:T(8,128)(2,1)}, f32[384,512]{1,0:T(8,128)}, f32[384,512]{1,0:T(8,128)}) custom-call(s32[1]{0:T(128)} %bitcast.7.place_ref, f32[288,768]{1,0:T(8,128)} %get-tuple-element.116.refs_0_, f32[288,768]{1,0:T(8,128)} %get-tuple-element.117.refs_1_, ...), custom_call_target="tpu_custom_call" | custom-call | flops 3623878656 | bytes 8257536 | tf_op jit(solution)/shard_map/down_parts/pallas_call | solution.py:336
  143.2 3.0 %collective-permute-start.29 = (bf16[768,512]{1,0:T(8,128)(2,1)}, bf16[768,512]{1,0:T(8,128)(2,1)S(1)}, u32[]{:S(2)}, u32[]{:S(2)}) collective-permute-start(bf16[768,512]{1,0:T(8,128)(2,1)} %get-tuple-element.121), channel_id=1, source_target_pairs={{0,48},{16,0},{32,16},{48,32},{1,49},{17,1},{33,17},{49,33},{2,50}... | collective-permute-start | bytes 2359304 | tf_op jit(solution)/shard_map/ppermute | solution.py:31
  146.2 7.6 %slot_rows.3 = (bf16[288,1024]{1,0:T(8,128)(2,1)}, bf16[288,1024]{1,0:T(8,128)(2,1)}, bf16[288,1024]{1,0:T(8,128)(2,1)}, bf16[288,1024]{1,0:T(8,128)(2,1)}) custom-call(bf16[288,1536]{1,0:T(8,128)(2,1)} %get-tuple-element.91.refs_0_.refs_4_, bf16[288,1536]{1,0:T(8,128)(2,1)} %get-tuple-element.92.refs_1_.refs_5_, ...), custom_call_target="tpu_custom_call" | custom-call | flops 3623878656 | bytes 9043968 | tf_op jit(solution)/shard_map/slot_rows/pallas_call | solution.py:418
  157.2 2.4 collective-permute-start.20
  159.6 20.9 %gate_up_parts.1 = (f32[512,1536]{1,0:T(8,128)}, bf16[512,1536]{1,0:T(8,128)(2,1)}, bf16[512,1536]{1,0:T(8,128)(2,1)}, f32[256,1536]{1,0:T(8,128)}, f32[256,1536]{1,0:T(8,128)}) custom-call(s32[1]{0:T(128)} %bitcast.7.place_ref, bf16[288,2048]{1,0:T(8,128)(2,1)} %get-tuple-element.65.refs_0_, bf16[288,2048]{1,0:T(8,128)(2,1)} %copy-done.22, ...), custom_call_target="tpu_custom_call" | custom-call | flops 7247757312 | bytes 8257536 | tf_op jit(solution)/shard_map/gate_up_parts/pallas_call | solution.py:386
  180.6 3.1 %collective-permute-start.25 = (bf16[512,1536]{1,0:T(8,128)(2,1)}, bf16[512,1536]{1,0:T(8,128)(2,1)S(1)}, u32[]{:S(2)}, u32[]{:S(2)}) collective-permute-start(bf16[512,1536]{1,0:T(8,128)(2,1)} %get-tuple-element.112), channel_id=1, source_target_pairs={{0,48},{16,0},{32,16},{48,32},{1,49},{17,1},{33,17},{49,33},{2,50}... | collective-permute-start | bytes 4718600 | tf_op jit(solution)/shard_map/ppermute | solution.py:31
  183.6 4.3 %unpack.2 = (f32[128,1024]{1,0:T(8,128)}, bf16[128,1024]{1,0:T(8,128)(2,1)}, bf16[128,1024]{1,0:T(8,128)(2,1)}, bf16[128,1024]{1,0:T(8,128)(2,1)}) custom-call(s32[4]{0:T(128)} %get-tuple-element.129.eids_ref, bf16[128,2176]{1,0:T(8,128)(2,1)} %get-tuple-element.64.refs_0_.refs_4_, bf16[128,2176]{1,0:T(8,128)(2,1)} %copy-done.18, ...), custom_call_target="tpu_custom_call" | custom-call | flops 603979776 | bytes 2359296 | tf_op jit(solution)/shard_map/unpack/pallas_call | solution.py:186
  189.8 4.4 %unpack.3 = (f32[128,1024]{1,0:T(8,128)}, bf16[128,1024]{1,0:T(8,128)(2,1)}, bf16[128,1024]{1,0:T(8,128)(2,1)}, bf16[128,1024]{1,0:T(8,128)(2,1)}) custom-call(s32[4]{0:T(128)} %get-tuple-element.130.eids_ref, bf16[128,2176]{1,0:T(8,128)(2,1)} %get-tuple-element.80.refs_0_.refs_4_, bf16[128,2176]{1,0:T(8,128)(2,1)} %copy-done.15, ...), custom_call_target="tpu_custom_call" | custom-call | flops 603979776 | bytes 2359296 | tf_op jit(solution)/shard_map/unpack/pallas_call | solution.py:186
  198.2 6.4 %collective-permute-done.16 = bf16[128,1024]{1,0:T(8,128)(2,1)S(1)} collective-permute-done((bf16[128,1024]{1,0:T(8,128)(2,1)S(1)}, bf16[128,1024]{1,0:T(8,128)(2,1)S(1)}, u32[]{:S(2)}, u32[]{:S(2)}) %collective-permute-start.16) | collective-permute-done | bytes 262176 | tf_op jit(solution)/shard_map/ppermute | solution.py:39
  206.7 3.2 %collective-permute-start.32 = (bf16[384,512]{1,0:T(8,128)(2,1)S(1)}, bf16[384,512]{1,0:T(8,128)(2,1)S(1)}, u32[]{:S(2)}, u32[]{:S(2)}) collective-permute-start(bf16[384,512]{1,0:T(8,128)(2,1)S(1)} %add_convert_fusion.5), channel_id=1, source_target_pairs={{0,48},{16,0},{32,16},{48,32},{1,49},{17,1},{33,17},{49,33},{2,50}... | collective-permute-start | bytes 1179656 | tf_op jit(solution)/shard_map/ppermute | solution.py:31
  209.9 5.1 %collective-permute-done.22 = bf16[128,1024]{1,0:T(8,128)(2,1)S(1)} collective-permute-done((bf16[128,1024]{1,0:T(8,128)(2,1)S(1)}, bf16[128,1024]{1,0:T(8,128)(2,1)S(1)}, u32[]{:S(2)}, u32[]{:S(2)}) %collective-permute-start.22) | collective-permute-done | bytes 262176 | tf_op jit(solution)/shard_map/ppermute | solution.py:39
  215.6 3.2 %collective-permute-done.25 = bf16[512,1536]{1,0:T(8,128)(2,1)S(1)} collective-permute-done((bf16[512,1536]{1,0:T(8,128)(2,1)}, bf16[512,1536]{1,0:T(8,128)(2,1)S(1)}, u32[]{:S(2)}, u32[]{:S(2)}) %collective-permute-start.25) | collective-permute-done | bytes 1572896 | tf_op jit(solution)/shard_map/ppermute | solution.py:31
  219.0 3.7 %collective-permute-start.28 = (bf16[256,1536]{1,0:T(8,128)(2,1)S(1)}, bf16[256,1536]{1,0:T(8,128)(2,1)S(1)}, u32[]{:S(2)}, u32[]{:S(2)}) collective-permute-start(bf16[256,1536]{1,0:T(8,128)(2,1)S(1)} %add_convert_fusion.1), channel_id=1, source_target_pairs={{0,48},{16,0},{32,16},{48,32},{1,49},{17,1},{33,17},{49,33},{2,50}... | collective-permute-start | bytes 2359304 | tf_op jit(solution)/shard_map/ppermute | solution.py:31
  222.7 4.1 %collective-permute-done.26 = bf16[512,1536]{1,0:T(8,128)(2,1)S(1)} collective-permute-done((bf16[512,1536]{1,0:T(8,128)(2,1)}, bf16[512,1536]{1,0:T(8,128)(2,1)S(1)}, u32[]{:S(2)}, u32[]{:S(2)}) %collective-permute-start.26) | collective-permute-done | bytes 1572896 | tf_op jit(solution)/shard_map/ppermute | solution.py:31
  228.1 7.2 %collective-permute-done.31 = bf16[384,512]{1,0:T(8,128)(2,1)S(1)} collective-permute-done((bf16[384,512]{1,0:T(8,128)(2,1)S(1)}, bf16[384,512]{1,0:T(8,128)(2,1)S(1)}, u32[]{:S(2)}, u32[]{:S(2)}) %collective-permute-start.31) | collective-permute-done | bytes 393248 | tf_op jit(solution)/shard_map/ppermute | solution.py:31
  236.6 7.2 %collective-permute-done.27 = bf16[256,1536]{1,0:T(8,128)(2,1)S(1)} collective-permute-done((bf16[256,1536]{1,0:T(8,128)(2,1)S(1)}, bf16[256,1536]{1,0:T(8,128)(2,1)S(1)}, u32[]{:S(2)}, u32[]{:S(2)}) %collective-permute-start.27) | collective-permute-done | bytes 786464 | tf_op jit(solution)/shard_map/ppermute | solution.py:31
  (125 shorter events, 45.6 us)
Async XLA Ops:
  6.1 15.7 %collective-permute-start = (bf16[128,2176]{1,0:T(8,128)(2,1)}, bf16[128,2176]{1,0:T(8,128)(2,1)S(1)}, u32[]{:S(2)}, u32[]{:S(2)}) collective-permute-start(bf16[128,2176]{1,0:T(8,128)(2,1)} %get-tuple-element.64.refs_0_.refs_4_), channel_id=1, source_target_pairs={{0,4},{1,5},{2,6},{3,7},{4,8},{5,9},{6,10},{7,11},{8,12},{9,13},{1... | collective-permute-start | bytes 1671176 | tf_op jit(solution)/shard_map/ppermute | solution.py:39
  7.7 19.5 %collective-permute-start.1 = (bf16[128,2176]{1,0:T(8,128)(2,1)}, bf16[128,2176]{1,0:T(8,128)(2,1)S(1)}, u32[]{:S(2)}, u32[]{:S(2)}) collective-permute-start(bf16[128,2176]{1,0:T(8,128)(2,1)} %get-tuple-element.64.refs_0_.refs_4_), channel_id=1, source_target_pairs={{0,12},{1,13},{2,14},{3,15},{4,0},{5,1},{6,2},{7,3},{8,4},{9,5},{1... | collective-permute-start | bytes 1671176 | tf_op jit(solution)/shard_map/ppermute | solution.py:39
  9.4 25.7 %collective-permute-start.2 = (bf16[128,2176]{1,0:T(8,128)(2,1)}, bf16[128,2176]{1,0:T(8,128)(2,1)}, u32[]{:S(2)}, u32[]{:S(2)}) collective-permute-start(bf16[128,2176]{1,0:T(8,128)(2,1)} %get-tuple-element.64.refs_0_.refs_4_), channel_id=1, source_target_pairs={{0,8},{1,9},{2,10},{3,11},{4,12},{5,13},{6,14},{7,15},{8,0},{9,1},... | collective-permute-start | bytes 1671176 | tf_op jit(solution)/shard_map/ppermute | solution.py:39
  11.2 34.6 %collective-permute-start.6 = (bf16[128,2176]{1,0:T(8,128)(2,1)}, bf16[128,2176]{1,0:T(8,128)(2,1)S(1)}, u32[]{:S(2)}, u32[]{:S(2)}) collective-permute-start(bf16[128,2176]{1,0:T(8,128)(2,1)} %get-tuple-element.80.refs_0_.refs_4_), channel_id=1, source_target_pairs={{0,1},{1,2},{2,3},{3,0},{4,5},{5,6},{6,7},{7,4},{8,9},{9,10},{10,1... | collective-permute-start | bytes 1671176 | tf_op jit(solution)/shard_map/ppermute | solution.py:39
  13.2 32.6 %collective-permute-start.7 = (bf16[128,2176]{1,0:T(8,128)(2,1)}, bf16[128,2176]{1,0:T(8,128)(2,1)S(1)}, u32[]{:S(2)}, u32[]{:S(2)}) collective-permute-start(bf16[128,2176]{1,0:T(8,128)(2,1)} %get-tuple-element.80.refs_0_.refs_4_), channel_id=1, source_target_pairs={{0,3},{1,0},{2,1},{3,2},{4,7},{5,4},{6,5},{7,6},{8,11},{9,8},{10,9... | collective-permute-start | bytes 1671176 | tf_op jit(solution)/shard_map/ppermute | solution.py:39
  21.8 24.0 %collective-permute-start.8 = (bf16[128,2176]{1,0:T(8,128)(2,1)}, bf16[128,2176]{1,0:T(8,128)(2,1)S(1)}, u32[]{:S(2)}, u32[]{:S(2)}) collective-permute-start(bf16[128,2176]{1,0:T(8,128)(2,1)} %get-tuple-element.80.refs_0_.refs_4_), channel_id=1, source_target_pairs={{0,2},{1,3},{2,0},{3,1},{4,6},{5,7},{6,4},{7,5},{8,10},{9,11},{10,... | collective-permute-start | bytes 1671176 | tf_op jit(solution)/shard_map/ppermute | solution.py:39
  41.6 29.4 %collective-permute-start.3 = (bf16[288,2048]{1,0:T(8,128)(2,1)}, bf16[288,2048]{1,0:T(8,128)(2,1)S(1)}, u32[]{:S(2)}, u32[]{:S(2)}) collective-permute-start(bf16[288,2048]{1,0:T(8,128)(2,1)} %get-tuple-element.67), channel_id=1, source_target_pairs={{0,1},{1,2},{2,3},{3,0},{4,5},{5,6},{6,7},{7,4},{8,9},{9,10},{10,1... | collective-permute-start | bytes 3538952 | tf_op jit(solution)/shard_map/ppermute | solution.py:39
  43.6 27.4 %collective-permute-start.4 = (bf16[288,2048]{1,0:T(8,128)(2,1)}, bf16[288,2048]{1,0:T(8,128)(2,1)S(1)}, u32[]{:S(2)}, u32[]{:S(2)}) collective-permute-start(bf16[288,2048]{1,0:T(8,128)(2,1)} %get-tuple-element.68), channel_id=1, source_target_pairs={{0,3},{1,0},{2,1},{3,2},{4,7},{5,4},{6,5},{7,6},{8,11},{9,8},{10,9... | collective-permute-start | bytes 3538952 | tf_op jit(solution)/shard_map/ppermute | solution.py:39
  54.1 26.8 %collective-permute-start.10 = (bf16[288,2048]{1,0:T(8,128)(2,1)}, bf16[288,2048]{1,0:T(8,128)(2,1)S(1)}, u32[]{:S(2)}, u32[]{:S(2)}) collective-permute-start(bf16[288,2048]{1,0:T(8,128)(2,1)} %get-tuple-element.84), channel_id=1, source_target_pairs={{0,12},{1,13},{2,14},{3,15},{4,0},{5,1},{6,2},{7,3},{8,4},{9,5},{1... | collective-permute-start | bytes 3538952 | tf_op jit(solution)/shard_map/ppermute | solution.py:39
  56.8 26.5 %collective-permute-start.9 = (bf16[288,2048]{1,0:T(8,128)(2,1)}, bf16[288,2048]{1,0:T(8,128)(2,1)S(1)}, u32[]{:S(2)}, u32[]{:S(2)}) collective-permute-start(bf16[288,2048]{1,0:T(8,128)(2,1)} %get-tuple-element.83), channel_id=1, source_target_pairs={{0,4},{1,5},{2,6},{3,7},{4,8},{5,9},{6,10},{7,11},{8,12},{9,13},{1... | collective-permute-start | bytes 3538952 | tf_op jit(solution)/shard_map/ppermute | solution.py:39
  71.0 30.4 %collective-permute-start.5 = (bf16[288,2048]{1,0:T(8,128)(2,1)}, bf16[288,2048]{1,0:T(8,128)(2,1)S(1)}, u32[]{:S(2)}, u32[]{:S(2)}) collective-permute-start(bf16[288,2048]{1,0:T(8,128)(2,1)} %get-tuple-element.74), channel_id=1, source_target_pairs={{0,2},{1,3},{2,0},{3,1},{4,6},{5,7},{6,4},{7,5},{8,10},{9,11},{10,... | collective-permute-start | bytes 3538952 | tf_op jit(solution)/shard_map/ppermute | solution.py:39
  84.3 26.0 %collective-permute-start.11 = (bf16[288,2048]{1,0:T(8,128)(2,1)}, bf16[288,2048]{1,0:T(8,128)(2,1)S(1)}, u32[]{:S(2)}, u32[]{:S(2)}) collective-permute-start(bf16[288,2048]{1,0:T(8,128)(2,1)} %get-tuple-element.90), channel_id=1, source_target_pairs={{0,8},{1,9},{2,10},{3,11},{4,12},{5,13},{6,14},{7,15},{8,0},{9,1},... | collective-permute-start | bytes 3538952 | tf_op jit(solution)/shard_map/ppermute | solution.py:39
  129.4 24.4 %collective-permute-start.12 = (bf16[288,1024]{1,0:T(8,128)(2,1)}, bf16[288,1024]{1,0:T(8,128)(2,1)S(1)}, u32[]{:S(2)}, u32[]{:S(2)}) collective-permute-start(bf16[288,1024]{1,0:T(8,128)(2,1)} %get-tuple-element.96), channel_id=1, source_target_pairs={{0,3},{1,0},{2,1},{3,2},{4,7},{5,4},{6,5},{7,6},{8,11},{9,8},{10,9... | collective-permute-start | bytes 1769480 | tf_op jit(solution)/shard_map/ppermute | solution.py:39
  130.8 25.1 %collective-permute-start.13 = (bf16[288,1024]{1,0:T(8,128)(2,1)}, bf16[288,1024]{1,0:T(8,128)(2,1)S(1)}, u32[]{:S(2)}, u32[]{:S(2)}) collective-permute-start(bf16[288,1024]{1,0:T(8,128)(2,1)} %get-tuple-element.97), channel_id=1, source_target_pairs={{0,1},{1,2},{2,3},{3,0},{4,5},{5,6},{6,7},{7,4},{8,9},{9,10},{10,1... | collective-permute-start | bytes 1769480 | tf_op jit(solution)/shard_map/ppermute | solution.py:39
  131.4 25.7 %collective-permute-start.14 = (bf16[288,1024]{1,0:T(8,128)(2,1)}, bf16[288,1024]{1,0:T(8,128)(2,1)S(1)}, u32[]{:S(2)}, u32[]{:S(2)}) collective-permute-start(bf16[288,1024]{1,0:T(8,128)(2,1)} %get-tuple-element.98), channel_id=1, source_target_pairs={{0,2},{1,3},{2,0},{3,1},{4,6},{5,7},{6,4},{7,5},{8,10},{9,11},{10,... | collective-permute-start | bytes 1769480 | tf_op jit(solution)/shard_map/ppermute | solution.py:39
  143.2 51.0 %collective-permute-start.29 = (bf16[768,512]{1,0:T(8,128)(2,1)}, bf16[768,512]{1,0:T(8,128)(2,1)S(1)}, u32[]{:S(2)}, u32[]{:S(2)}) collective-permute-start(bf16[768,512]{1,0:T(8,128)(2,1)} %get-tuple-element.121), channel_id=1, source_target_pairs={{0,48},{16,0},{32,16},{48,32},{1,49},{17,1},{33,17},{49,33},{2,50}... | collective-permute-start | bytes 2359304 | tf_op jit(solution)/shard_map/ppermute | solution.py:31
  146.2 48.7 %collective-permute-start.30 = (bf16[768,512]{1,0:T(8,128)(2,1)}, bf16[768,512]{1,0:T(8,128)(2,1)S(1)}, u32[]{:S(2)}, u32[]{:S(2)}) collective-permute-start(bf16[768,512]{1,0:T(8,128)(2,1)} %get-tuple-element.123), channel_id=1, source_target_pairs={{0,16},{16,32},{32,48},{48,0},{1,17},{17,33},{33,49},{49,1},{2,18}... | collective-permute-start | bytes 2359304 | tf_op jit(solution)/shard_map/ppermute | solution.py:31
  153.8 26.8 %collective-permute-start.18 = (bf16[288,1024]{1,0:T(8,128)(2,1)}, bf16[288,1024]{1,0:T(8,128)(2,1)S(1)}, u32[]{:S(2)}, u32[]{:S(2)}) collective-permute-start(bf16[288,1024]{1,0:T(8,128)(2,1)} %get-tuple-element.104), channel_id=1, source_target_pairs={{0,12},{1,13},{2,14},{3,15},{4,0},{5,1},{6,2},{7,3},{8,4},{9,5},{1... | collective-permute-start | bytes 1769480 | tf_op jit(solution)/shard_map/ppermute | solution.py:39
  155.9 32.1 %collective-permute-start.19 = (bf16[288,1024]{1,0:T(8,128)(2,1)}, bf16[288,1024]{1,0:T(8,128)(2,1)S(1)}, u32[]{:S(2)}, u32[]{:S(2)}) collective-permute-start(bf16[288,1024]{1,0:T(8,128)(2,1)} %get-tuple-element.105), channel_id=1, source_target_pairs={{0,4},{1,5},{2,6},{3,7},{4,8},{5,9},{6,10},{7,11},{8,12},{9,13},{1... | collective-permute-start | bytes 1769480 | tf_op jit(solution)/shard_map/ppermute | solution.py:39
  157.2 30.9 %collective-permute-start.20 = (bf16[288,1024]{1,0:T(8,128)(2,1)}, bf16[288,1024]{1,0:T(8,128)(2,1)S(1)}, u32[]{:S(2)}, u32[]{:S(2)}) collective-permute-start(bf16[288,1024]{1,0:T(8,128)(2,1)} %get-tuple-element.106), channel_id=1, source_target_pairs={{0,8},{1,9},{2,10},{3,11},{4,12},{5,13},{6,14},{7,15},{8,0},{9,1},... | collective-permute-start | bytes 1769480 | tf_op jit(solution)/shard_map/ppermute | solution.py:39
  180.6 38.2 %collective-permute-start.25 = (bf16[512,1536]{1,0:T(8,128)(2,1)}, bf16[512,1536]{1,0:T(8,128)(2,1)S(1)}, u32[]{:S(2)}, u32[]{:S(2)}) collective-permute-start(bf16[512,1536]{1,0:T(8,128)(2,1)} %get-tuple-element.112), channel_id=1, source_target_pairs={{0,48},{16,0},{32,16},{48,32},{1,49},{17,1},{33,17},{49,33},{2,50}... | collective-permute-start | bytes 4718600 | tf_op jit(solution)/shard_map/ppermute | solution.py:31
  188.0 38.8 %collective-permute-start.26 = (bf16[512,1536]{1,0:T(8,128)(2,1)}, bf16[512,1536]{1,0:T(8,128)(2,1)S(1)}, u32[]{:S(2)}, u32[]{:S(2)}) collective-permute-start(bf16[512,1536]{1,0:T(8,128)(2,1)} %get-tuple-element.114), channel_id=1, source_target_pairs={{0,16},{16,32},{32,48},{48,0},{1,17},{17,33},{33,49},{49,1},{2,18}... | collective-permute-start | bytes 4718600 | tf_op jit(solution)/shard_map/ppermute | solution.py:31
  188.1 8.8 %collective-permute-start.15 = (bf16[128,1024]{1,0:T(8,128)(2,1)}, bf16[128,1024]{1,0:T(8,128)(2,1)S(1)}, u32[]{:S(2)}, u32[]{:S(2)}) collective-permute-start(bf16[128,1024]{1,0:T(8,128)(2,1)} %get-tuple-element.100), channel_id=1, source_target_pairs={{0,12},{1,13},{2,14},{3,15},{4,0},{5,1},{6,2},{7,3},{8,4},{9,5},{1... | collective-permute-start | bytes 786440 | tf_op jit(solution)/shard_map/ppermute | solution.py:39
  194.2 10.5 %collective-permute-start.16 = (bf16[128,1024]{1,0:T(8,128)(2,1)S(1)}, bf16[128,1024]{1,0:T(8,128)(2,1)S(1)}, u32[]{:S(2)}, u32[]{:S(2)}) collective-permute-start(bf16[128,1024]{1,0:T(8,128)(2,1)S(1)} %copy-done.28), channel_id=1, source_target_pairs={{0,4},{1,5},{2,6},{3,7},{4,8},{5,9},{6,10},{7,11},{8,12},{9,13},{1... | collective-permute-start | bytes 786440 | tf_op jit(solution)/shard_map/ppermute | solution.py:39
  195.1 10.8 %collective-permute-start.17 = (bf16[128,1024]{1,0:T(8,128)(2,1)S(1)}, bf16[128,1024]{1,0:T(8,128)(2,1)S(1)}, u32[]{:S(2)}, u32[]{:S(2)}) collective-permute-start(bf16[128,1024]{1,0:T(8,128)(2,1)S(1)} %copy-done.26), channel_id=1, source_target_pairs={{0,8},{1,9},{2,10},{3,11},{4,12},{5,13},{6,14},{7,15},{8,0},{9,1},... | collective-permute-start | bytes 786440 | tf_op jit(solution)/shard_map/ppermute | solution.py:39
  196.9 9.8 %collective-permute-start.21 = (bf16[128,1024]{1,0:T(8,128)(2,1)S(1)}, bf16[128,1024]{1,0:T(8,128)(2,1)S(1)}, u32[]{:S(2)}, u32[]{:S(2)}) collective-permute-start(bf16[128,1024]{1,0:T(8,128)(2,1)S(1)} %copy-done.30), channel_id=1, source_target_pairs={{0,3},{1,0},{2,1},{3,2},{4,7},{5,4},{6,5},{7,6},{8,11},{9,8},{10,9... | collective-permute-start | bytes 786440 | tf_op jit(solution)/shard_map/ppermute | solution.py:39
  204.6 10.4 %collective-permute-start.22 = (bf16[128,1024]{1,0:T(8,128)(2,1)S(1)}, bf16[128,1024]{1,0:T(8,128)(2,1)S(1)}, u32[]{:S(2)}, u32[]{:S(2)}) collective-permute-start(bf16[128,1024]{1,0:T(8,128)(2,1)S(1)} %copy-done.29), channel_id=1, source_target_pairs={{0,1},{1,2},{2,3},{3,0},{4,5},{5,6},{6,7},{7,4},{8,9},{9,10},{10,1... | collective-permute-start | bytes 786440 | tf_op jit(solution)/shard_map/ppermute | solution.py:39
  205.9 9.6 %collective-permute-start.23 = (bf16[128,1024]{1,0:T(8,128)(2,1)S(1)}, bf16[128,1024]{1,0:T(8,128)(2,1)S(1)}, u32[]{:S(2)}, u32[]{:S(2)}) collective-permute-start(bf16[128,1024]{1,0:T(8,128)(2,1)S(1)} %copy-done.27), channel_id=1, source_target_pairs={{0,2},{1,3},{2,0},{3,1},{4,6},{5,7},{6,4},{7,5},{8,10},{9,11},{10,... | collective-permute-start | bytes 786440 | tf_op jit(solution)/shard_map/ppermute | solution.py:39
  206.7 21.4 %collective-permute-start.32 = (bf16[384,512]{1,0:T(8,128)(2,1)S(1)}, bf16[384,512]{1,0:T(8,128)(2,1)S(1)}, u32[]{:S(2)}, u32[]{:S(2)}) collective-permute-start(bf16[384,512]{1,0:T(8,128)(2,1)S(1)} %add_convert_fusion.5), channel_id=1, source_target_pairs={{0,48},{16,0},{32,16},{48,32},{1,49},{17,1},{33,17},{49,33},{2,50}... | collective-permute-start | bytes 1179656 | tf_op jit(solution)/shard_map/ppermute | solution.py:31
  215.0 20.2 %collective-permute-start.31 = (bf16[384,512]{1,0:T(8,128)(2,1)S(1)}, bf16[384,512]{1,0:T(8,128)(2,1)S(1)}, u32[]{:S(2)}, u32[]{:S(2)}) collective-permute-start(bf16[384,512]{1,0:T(8,128)(2,1)S(1)} %add_convert_fusion.7), channel_id=1, source_target_pairs={{0,16},{16,32},{32,48},{48,0},{1,17},{17,33},{33,49},{49,1},{2,18}... | collective-permute-start | bytes 1179656 | tf_op jit(solution)/shard_map/ppermute | solution.py:31
  219.0 17.5 %collective-permute-start.28 = (bf16[256,1536]{1,0:T(8,128)(2,1)S(1)}, bf16[256,1536]{1,0:T(8,128)(2,1)S(1)}, u32[]{:S(2)}, u32[]{:S(2)}) collective-permute-start(bf16[256,1536]{1,0:T(8,128)(2,1)S(1)} %add_convert_fusion.1), channel_id=1, source_target_pairs={{0,48},{16,0},{32,16},{48,32},{1,49},{17,1},{33,17},{49,33},{2,50}... | collective-permute-start | bytes 2359304 | tf_op jit(solution)/shard_map/ppermute | solution.py:31
  227.1 16.7 %collective-permute-start.27 = (bf16[256,1536]{1,0:T(8,128)(2,1)S(1)}, bf16[256,1536]{1,0:T(8,128)(2,1)S(1)}, u32[]{:S(2)}, u32[]{:S(2)}) collective-permute-start(bf16[256,1536]{1,0:T(8,128)(2,1)S(1)} %add_convert_fusion.3), channel_id=1, source_target_pairs={{0,16},{16,32},{32,48},{48,0},{1,17},{17,33},{33,49},{49,1},{2,18}... | collective-permute-start | bytes 2359304 | tf_op jit(solution)/shard_map/ppermute | solution.py:31
  (32 other events, 261.2 us)

commit v2 on v1

v2 whole, which is shorter than its diff:
```python
import functools

import jax
import jax.numpy as jnp
from jax import lax
from jax.experimental import pallas as pl
from jax.experimental.pallas import tpu as pltpu
from jax.sharding import PartitionSpec as P

BF16 = jnp.bfloat16
F32 = jnp.float32
OFF = (0, 1, 3, 2)
SIDE = 4
LANES = 128
MIB = 1024 * 1024


def params(steps, limit):
    return pltpu.CompilerParams(
        vmem_limit_bytes=limit * MIB, dimension_semantics=("arbitrary",) * steps
    )


def held(shape, index):
    return pl.BlockSpec(shape, index, pipeline_mode=pl.Buffered(1))


def cost(flops, moved):
    return pl.CostEstimate(flops=int(flops), bytes_accessed=int(moved), transcendentals=0)


def moved_along(block, axis, distance):
    if axis == "edata" or axis == "section":
        size = lax.axis_size(axis)
        return lax.ppermute(block, axis, [(i, (i + distance) % size) for i in range(size)])
    pairs = []
    for a in range(SIDE):
        for b in range(SIDE):
            if axis == "x":
                pairs.append((a * SIDE + b, (a + distance) % SIDE * SIDE + b))
            else:
                pairs.append((a * SIDE + b, a * SIDE + (b + distance) % SIDE))
    return lax.ppermute(block, "expert", pairs)


def iota(shape, dim):
    return lax.broadcasted_iota(jnp.int32, shape, dim)


def dot(a, b, da=1, db=0):
    return lax.dot_general(a, b, (((da,), (db,)), ((), ())), preferred_element_type=F32)


def prep_kernel(experts, routes_ref, gates_ref, x_ref, g_ref, xe_ref, ge_ref):
    tok, width = x_ref.shape
    topk = routes_ref.shape[0]
    expert = lax.rem(iota((LANES, tok), 0), experts)
    full = jnp.zeros((LANES, tok), F32)
    for k in range(topk):
        full += jnp.where(routes_ref[k : k + 1, :] == expert, gates_ref[k : k + 1, :], 0.0)
    full = full.T
    lane = iota((tok, LANES), 1)
    high = full.astype(BF16).astype(F32)
    rest = full - high
    middle = rest.astype(BF16).astype(F32)
    low = rest - middle
    piece = jnp.where(lane < 2 * experts, middle, jnp.where(lane < 3 * experts, low, 0.0))
    piece = jnp.where(lane < experts, high, piece).astype(BF16)
    for src, dst in ((x_ref, xe_ref), (g_ref, ge_ref)):
        dst[:, :width] = src[...]
        dst[:, width:] = piece


def prep(routes, gates, x, g, experts):
    tok, width = x.shape
    shape = jax.ShapeDtypeStruct((tok, width + LANES), BF16)
    return pl.pallas_call(
        functools.partial(prep_kernel, experts),
        out_shape=(shape, shape),
        compiler_params=params(0, 8),
        name="prep",
    )(routes, gates, x, g)


def places(piece, experts, blocks):
    rows = piece.shape[0]
    tok = rows // blocks
    r, c = iota((rows, rows), 0), iota((rows, rows), 1)
    upto = jnp.where((c <= r) & (lax.div(c, tok) == lax.div(r, tok)), 1.0, 0.0).astype(BF16)
    lane = iota((rows, LANES), 1)
    mask = jnp.where((lane < experts) & (piece.astype(F32) > 0.0), 1.0, 0.0)
    return (dot(upto, mask.astype(BF16)) * mask).astype(BF16)


def pack_kernel(scale, experts, cap, eids_ref, *refs):
    blocks, tails, outs = refs[:4], refs[4:8], refs[8:12]
    table_ref, gate_ref = refs[12:]
    pair = 2 * cap
    total = SIDE * pair
    tok = tails[0].shape[0]

    @pl.when(pl.program_id(0) == 0)
    def _():
        row = iota((total, LANES), 0)
        lane = iota((total, LANES), 1)
        want = jnp.full((total, LANES), eids_ref[0], jnp.int32)
        for j in range(1, SIDE):
            want = jnp.where(row >= j * pair, eids_ref[j], want)
        choose = jnp.where(lane == want, 1.0, 0.0).astype(BF16)
        mine = (lax.rem(lane, experts) == want) & (lane < 3 * experts)
        slot = lax.rem(iota((total, 2 * tok), 0), pair)
        place = slot + 1 - jnp.where(iota((total, 2 * tok), 1) >= tok, cap, 0)
        place = jnp.where(place > 0, place, -1).astype(F32)
        for p in range(2):
            piece = jnp.concatenate([tails[2 * p][...], tails[2 * p + 1][...]], axis=0)
            found = dot(choose, places(piece, experts, 2), 1, 1)
            table = jnp.where(found == place, 1.0, 0.0).astype(BF16)
            table_ref[p] = table
            if scale:
                packed = dot(table, piece)
                gate_ref[p] = jnp.sum(jnp.where(mine, packed, 0.0), axis=1, keepdims=True)

    for p in range(2):
        rows = jnp.concatenate([blocks[2 * p][...], blocks[2 * p + 1][...]], axis=0)
        packed = dot(table_ref[p], rows)
        if scale:
            packed = packed * gate_ref[p]
        packed = packed.astype(BF16)
        for j in range(SIDE):
            outs[j][p * pair : (p + 1) * pair, :] = packed[j * pair : (j + 1) * pair]


def pack(eids, blocks, width, experts, cap, scale):
    tok = blocks[0].shape[0]
    step = 512
    pair = 2 * cap
    last = width // LANES
    out = jax.ShapeDtypeStruct((2 * pair, width), BF16)
    return pl.pallas_call(
        functools.partial(pack_kernel, scale, experts, cap),
        grid=(width // step,),
        in_specs=[pl.BlockSpec(memory_space=pltpu.SMEM)]
        + [pl.BlockSpec((tok, step), lambda i: (0, i))] * 4
        + [held((tok, LANES), lambda i: (0, last))] * 4,
        out_specs=[pl.BlockSpec((2 * pair, step), lambda i: (0, i))] * 4,
        out_shape=[out] * 4,
        scratch_shapes=[
            pltpu.VMEM((2, SIDE * pair, 2 * tok), BF16),
            pltpu.VMEM((2, SIDE * pair, 1), F32),
        ],
        compiler_params=params(1, 20),
        cost_estimate=cost(4 * SIDE * pair * 2 * tok * width, 8 * pair * width * 4),
        name="pack_scaled" if scale else "pack_rows",
    )(eids, *blocks, *blocks)


def home_kernel(experts, cap, tail_ref, rows_ref, grad_ref, out_ref, table_ref):
    tok = tail_ref.shape[0]
    total = experts * cap

    @pl.when(pl.program_id(0) == 0)
    def _():
        choose = jnp.where(iota((LANES, total), 0) == lax.div(iota((LANES, total), 1), cap), 1.0, 0.0)
        found = dot(places(tail_ref[...], experts, 1), choose.astype(BF16))
        place = lax.rem(iota((tok, total), 1), cap) + 1
        table_ref[...] = jnp.where(found == place.astype(F32), 1.0, 0.0).astype(BF16)

    total_grad = dot(table_ref[...], rows_ref[...]) + grad_ref[...].astype(F32)
    out_ref[...] = total_grad.astype(BF16)


def home(ge, rows, grad, experts, cap):
    tok, width = grad.shape
    step = 512
    last = width // LANES
    total = experts * cap
    return pl.pallas_call(
        functools.partial(home_kernel, experts, cap),
        grid=(width // step,),
        in_specs=[
            held((tok, LANES), lambda i: (0, last)),
            pl.BlockSpec((total, step), lambda i: (0, i)),
            pl.BlockSpec((tok, step), lambda i: (0, i)),
        ],
        out_specs=pl.BlockSpec((tok, step), lambda i: (0, i)),
        out_shape=jax.ShapeDtypeStruct((tok, width), BF16),
        scratch_shapes=[pltpu.VMEM((tok, total), BF16)],
        compiler_params=params(1, 16),
        cost_estimate=cost(2 * tok * total * width, 2 * total * width + 4 * tok * width),
        name="home",
    )(ge, rows, grad)


def up_kernel(count, *refs):
    xs, (wa, wb), outs = refs[:count], refs[count : count + 2], refs[count + 2 :]
    for i in range(count):
        rows = xs[i][...]
        a = dot(rows, wa[...])
        b = dot(rows, wb[...])
        sig = jax.nn.sigmoid(a)
        outs[3 * i][...] = a * sig * b
        outs[3 * i + 1][...] = b * sig * (1.0 + a * (1.0 - sig))
        outs[3 * i + 2][...] = a * sig


def up(xs, wgu):
    count = len(xs)
    rows, width = xs[0].shape
    hidden = wgu.shape[1] // 2
    step = 256
    steps = hidden // step
    out = jax.ShapeDtypeStruct((rows, hidden), F32)
    flat = pl.pallas_call(
        functools.partial(up_kernel, count),
        grid=(steps,),
        in_specs=[held((rows, width), lambda i: (0, 0))] * count
        + [
            pl.BlockSpec((width, step), lambda i: (0, i)),
            pl.BlockSpec((width, step), lambda i: (0, i + steps)),
        ],
        out_specs=[pl.BlockSpec((rows, step), lambda i: (0, i))] * (3 * count),
        out_shape=[out] * (3 * count),
        compiler_params=params(1, 22),
        cost_estimate=cost(
            4 * count * rows * width * hidden,
            2 * count * rows * width + 4 * width * hidden + 12 * count * rows * hidden,
        ),
        name="up",
    )(*xs, wgu, wgu)
    return [flat[3 * i : 3 * i + 3] for i in range(count)]


def dh_kernel(count, *refs):
    ss, wd, outs = refs[:count], refs[count], refs[count + 1 :]
    for i in range(count):
        outs[i][...] = dot(ss[i][...], wd[...], 1, 1)


def dh_of(ss, wdown):
    count = len(ss)
    rows, width = ss[0].shape
    hidden = wdown.shape[0]
    step = 256
    return pl.pallas_call(
        functools.partial(dh_kernel, count),
        grid=(hidden // step,),
        in_specs=[held((rows, width), lambda i: (0, 0))] * count
        + [pl.BlockSpec((step, width), lambda i: (i, 0))],
        out_specs=[pl.BlockSpec((rows, step), lambda i: (0, i))] * count,
        out_shape=[jax.ShapeDtypeStruct((rows, hidden), F32)] * count,
        compiler_params=params(1, 16),
        cost_estimate=cost(
            2 * count * rows * width * hidden,
            2 * count * rows * width + 2 * width * hidden + 4 * count * rows * hidden,
        ),
        name="dh",
    )(*ss, wdown)


def crossed(parts, j, cap):
    return jnp.concatenate([part[j * cap : (j + 1) * cap, :] for part in parts], axis=0)


def turn_kernel(cap, *refs):
    hs, out = refs[:4], refs[4]
    rows = jnp.concatenate([crossed(hs, j, cap) for j in range(SIDE)], axis=0)
    out[...] = rows.T.astype(BF16)


def turned(hs, cap):
    rows, hidden = hs[0].shape
    step = 256
    return pl.pallas_call(
        functools.partial(turn_kernel, cap),
        grid=(hidden // step,),
        in_specs=[pl.BlockSpec((rows, step), lambda i: (0, i))] * 4,
        out_specs=pl.BlockSpec((step, SIDE * rows), lambda i: (i, 0)),
        out_shape=jax.ShapeDtypeStruct((hidden, SIDE * rows), BF16),
        compiler_params=params(1, 16),
        cost_estimate=cost(8 * rows * hidden, 24 * rows * hidden),
        name="turned",
    )(*hs)


def dab_kernel(cap, *refs):
    s, wd, dhs, cas, cbs = refs[0], refs[1], refs[2:5], refs[5:9], refs[9:13]
    da, db = refs[13:]
    rows = s.shape[0]
    parts = [d[...] for d in dhs] + [dot(s[...], wd[...], 1, 1)]
    for i in range(SIDE):
        dh = crossed(parts, i, cap)
        da[i * rows : (i + 1) * rows, :] = (dh * cas[i][...]).astype(BF16)
        db[i * rows : (i + 1) * rows, :] = (dh * cbs[i][...]).astype(BF16)


def dab_of(s, wdown, dhs, cas, cbs, cap):
    rows, width = s.shape
    hidden = wdown.shape[0]
    step = 256
    out = jax.ShapeDtypeStruct((SIDE * rows, hidden), BF16)
    return pl.pallas_call(
        functools.partial(dab_kernel, cap),
        grid=(hidden // step,),
        in_specs=[
            held((rows, width), lambda i: (0, 0)),
            pl.BlockSpec((step, width), lambda i: (i, 0)),
        ]
        + [pl.BlockSpec((rows, step), lambda i: (0, i))] * 11,
        out_specs=[pl.BlockSpec((SIDE * rows, step), lambda i: (0, i))] * 2,
        out_shape=[out] * 2,
        compiler_params=params(1, 24),
        cost_estimate=cost(2 * rows * width * hidden, 64 * rows * hidden),
        name="dab",
    )(s, wdown, *dhs, *cas, *cbs)


def keep_quarter(step, part, first_up, first_down, wait_up, wait_down):
    half = part.shape[0] // 2

    @pl.when(step == 0)
    def _():
        first_up[:half, :] = part[:half].astype(BF16)
        first_down[half:, :] = part[half:].astype(BF16)

    @pl.when(step == 1)
    def _():
        wait_up[...] = part[:half]
        first_up[half:, :] = part[half:].astype(BF16)

    @pl.when(step == 2)
    def _():
        first_down[:half, :] = part[:half].astype(BF16)
        wait_down[...] = part[half:]


def quarter_of(own, step, place_ref):
    if own:
        return place_ref[0]
    ahead = jnp.where(step == 0, 2, jnp.where(step == 1, 1, 3))
    return lax.rem(place_ref[0] + ahead, SIDE)


def quarter_outs(own, shape):
    rows, cols = shape
    shapes = [
        ((rows, cols), BF16),
        ((rows, cols), BF16),
        ((rows // 2, cols), F32),
        ((rows // 2, cols), F32),
    ]
    if own:
        shapes = [((rows, cols), F32)]
    return (
        [jax.ShapeDtypeStruct(s, t) for s, t in shapes],
        [pl.BlockSpec(s, lambda i, place: (0, 0)) for s, t in shapes],
    )


def down_kernel(own, place_ref, *refs):
    turned_ref, ss, outs = refs[0], refs[1:5], refs[5:]
    rows = jnp.concatenate([s[...] for s in ss], axis=0)
    part = dot(turned_ref[...], rows)
    if own:
        outs[0][...] = part
    else:
        keep_quarter(pl.program_id(0), part, *outs)


def down_parts(place, turned_h, ss, own):
    hidden, total = turned_h.shape
    rows, width = ss[0].shape
    quarter = width // SIDE
    steps = 1 if own else SIDE - 1
    shapes, specs = quarter_outs(own, (hidden, quarter))
    column = functools.partial(quarter_of, own)
    return pl.pallas_call(
        functools.partial(down_kernel, own),
        grid_spec=pltpu.PrefetchScalarGridSpec(
            num_scalar_prefetch=1,
            grid=(steps,),
            in_specs=[held((hidden, total), lambda i, place: (0, 0))]
            + [pl.BlockSpec((rows, quarter), lambda i, place: (0, column(i, place)))] * 4,
            out_specs=specs,
        ),
        out_shape=shapes,
        compiler_params=params(1, 20),
        cost_estimate=cost(2 * total * steps * quarter * hidden, 4 * total * width),
        name="down_own" if own else "down_parts",
    )(place, turned_h, *ss)


def gate_up_kernel(own, place_ref, *refs):
    xs, ds, outs = refs[:4], refs[4:6], refs[6:]
    rows = jnp.concatenate([x[...] for x in xs], axis=0).T
    part = jnp.concatenate([dot(rows, d[...]) for d in ds], axis=1)
    if own:
        outs[0][...] = part
    else:
        keep_quarter(pl.program_id(0), part, *outs)


def gate_up_parts(place, xs, ds, own):
    rows, width = xs[0].shape
    total, hidden = ds[0].shape
    quarter = width // SIDE
    steps = 1 if own else SIDE - 1
    shapes, specs = quarter_outs(own, (quarter, 2 * hidden))
    column = functools.partial(quarter_of, own)
    return pl.pallas_call(
        functools.partial(gate_up_kernel, own),
        grid_spec=pltpu.PrefetchScalarGridSpec(
            num_scalar_prefetch=1,
            grid=(steps,),
            in_specs=[pl.BlockSpec((rows, quarter), lambda i, place: (0, column(i, place)))] * 4
            + [held((total, hidden), lambda i, place: (0, 0))] * 2,
            out_specs=specs,
        ),
        out_shape=shapes,
        compiler_params=params(1, 32),
        cost_estimate=cost(4 * total * steps * quarter * hidden, 4 * total * width),
        name="gate_up_own" if own else "gate_up_parts",
    )(place, *xs, *ds)


def slot_kernel(cap, to_ref, *refs):
    da, db, w, out = refs
    hidden = da.shape[1]
    part = dot(da[...], w[:, :hidden], 1, 1) + dot(db[...], w[:, hidden:], 1, 1)
    for b in range(SIDE * SIDE):
        out[to_ref[b]] = part[b * cap : (b + 1) * cap].astype(BF16)


def slot_rows(to, ds, wgu, cap):
    total, hidden = ds[0].shape
    width = wgu.shape[0]
    step = 512
    blocks = total // cap
    return pl.pallas_call(
        functools.partial(slot_kernel, cap),
        grid=(width // step,),
        in_specs=[pl.BlockSpec(memory_space=pltpu.SMEM)]
        + [held((total, hidden), lambda i: (0, 0))] * 2
        + [pl.BlockSpec((step, 2 * hidden), lambda i: (i, 0))],
        out_specs=pl.BlockSpec((blocks, cap, step), lambda i: (0, 0, i)),
        out_shape=jax.ShapeDtypeStruct((blocks, cap, width), BF16),
        compiler_params=params(1, 24),
        cost_estimate=cost(4 * total * hidden * width, 4 * total * hidden + 4 * hidden * width),
        name="slot_rows",
    )(to, *ds, wgu)


def around(first, axis):
    return [first] + [moved_along(first, axis, OFF[b]) for b in range(1, SIDE)]


def spread(outs, axis):
    near = [moved_along(outs[j], axis, OFF[j]) for j in (1, 2)]
    far, n0, n1 = lax.optimization_barrier((outs[3], near[0], near[1]))
    return [outs[0], n0, n1, moved_along(far, axis, OFF[3])]


def ring_sum(own, first_up, first_down, wait_up, wait_down):
    half = wait_up.shape[0]
    up1 = moved_along(first_up, "edata", 1)
    down1 = moved_along(first_down, "edata", -1)
    second_up = (wait_up + up1[:half].astype(F32)).astype(BF16)
    second_down = (wait_down + down1[half:].astype(F32)).astype(BF16)
    up2 = moved_along(second_up, "edata", 1)
    down2 = moved_along(second_down, "edata", -1)
    upper = own[:half] + down1[:half].astype(F32) + up2.astype(F32)
    lower = own[half:] + up1[half:].astype(F32) + down2.astype(F32)
    return jnp.concatenate([upper, lower], axis=0).astype(BF16)


def body(hidden_in, out_grad, routes, gates, w_gate_up, w_down):
    tok = hidden_in.shape[1]
    width = hidden_in.shape[2]
    topk = routes.shape[2]
    experts = lax.axis_size("expert")
    cap = min(tok, tok * topk * 9 // (8 * experts))
    wgu, wdown = w_gate_up[0, 0], w_down[0, 0]
    me = lax.axis_index("expert")
    mx, mz = me // SIDE, me % SIDE
    off = jnp.array(OFF, jnp.int32)
    eids_x = (mx * SIDE + (mz + off) % SIDE).astype(jnp.int32)
    eids_g = ((mx + off) % SIDE * SIDE + mz).astype(jnp.int32)
    to = ((mx - off)[None, :] % SIDE * SIDE + (mz - off)[:, None] % SIDE).reshape(-1)
    place = lax.axis_index("edata").astype(jnp.int32).reshape(1)

    xe, ge = prep(routes[0].T, gates[0].T, hidden_in[0], out_grad[0], experts)
    xblocks = around(xe, "x")
    gblocks = around(ge, "z")
    xs = spread(pack(eids_x, xblocks, width, experts, cap, False), "z")
    ss = spread(pack(eids_g, gblocks, width, experts, cap, True), "x")

    ups = up(xs[:3], wgu) + up(xs[3:], wgu)
    hs, cas, cbs = ([u[k] for u in ups] for k in range(3))
    dhs = dh_of(ss[:3], wdown)
    turned_h = turned(hs, cap)
    down = down_parts(place, turned_h, ss, False)
    last, *down = lax.optimization_barrier((ss[3], *down))
    ds = dab_of(last, wdown, dhs, cas, cbs, cap)
    rows = slot_rows(to.astype(jnp.int32), ds, wgu, cap)
    rows, *ds = lax.optimization_barrier((rows, *ds))
    returned = lax.all_to_all(rows, "expert", split_axis=0, concat_axis=0, tiled=True)
    gate_up = gate_up_parts(place, xs, ds, False)
    own_down = down_parts(place, turned_h, ss, True)
    own_gate_up = gate_up_parts(place, xs, ds, True)
    down_grad = ring_sum(*own_down, *down)
    gate_up_grad = ring_sum(*own_gate_up, *gate_up)

    layer = home(ge, returned.reshape(experts * cap, width), out_grad[0], experts, cap)
    upstream = moved_along(layer, "section", -1)
    return (upstream[None], gate_up_grad[None, None], down_grad[None, None])


def solution(mesh):
    return jax.shard_map(
        body,
        mesh=mesh,
        in_specs=(
            P("section", ("edata", "expert"), None),
            P("section", ("edata", "expert"), None),
            P("section", ("edata", "expert"), None),
            P("section", ("edata", "expert"), None),
            P("section", "expert", None, None),
            P("section", "expert", None, None),
        ),
        out_specs=(
            P("section", ("edata", "expert"), None),
            P("section", "expert", "edata", None),
            P("section", "expert", None, "edata"),
        ),
        check_vma=False,
    )
```

time: 247 us -> 240 us (0.972)
  Pallas kernels: 106 us -> 61 us
  local copies, waits for them, and re-layouts: 8.96 us -> 36.7 us
  waiting for transfers between devices: 72.4 us -> 93.1 us
  starting transfers between devices: 52.6 us -> 38.9 us
    ppermute x9, waiting for transfers between devices: 21.6 us -> 50.5 us  [moved_along(): lax.ppermute(block, axis, [(i, (i + distance) % size) for i in range(size)])]
    unnamed x65 -> x129, local copies, waits for them, and re-layouts: 8.96 us -> 36.7 us
    pallas_call x7 -> x8, Pallas kernels: 61.1 us -> 36.8 us  [the longest x2 9.87 us: gate_up_parts(): pl.pallas_call(functools.partial(gate_up_kernel, own), grid_spec=pltpu.Pr...]
    ppermute x24 -> x12, starting transfers between devices: 38.9 us -> 21.2 us  [moved_along(): return lax.ppermute(block, 'expert', pairs)]
    ppermute x24 -> x12, waiting for transfers between devices: 50.8 us -> 42.5 us  [moved_along(): return lax.ppermute(block, 'expert', pairs)]
    pallas_call x2 -> x1, Pallas kernels: 11.5 us -> 3.52 us  [dh_of(): pl.pallas_call(functools.partial(dh_kernel, count), grid=(hidden // step,...]
    pallas_call x2, Pallas kernels: 17.1 us -> 10.2 us  [up(): pl.pallas_call(functools.partial(up_kernel, count), grid=(steps,), in_spe...]
    all_to_all x0 -> x1, starting transfers between devices: none -> 5.33 us  [body(): lax.all_to_all(rows, 'expert', split_axis=0, concat_axis=0, tiled=True)]
  transfers between devices with their start and end apart: 33 -> 22, of which waited for: 13 -> 9; matrix products, arithmetic and copies ran while one was open for 1% -> 3% of each run, Pallas kernels for 35% -> 18%
where the time goes in v2:
time: 240 us; the launch traced here: 238 us
  waiting for transfers between devices  93.1 us (39%)
  Pallas kernels  61 us (25%)
  starting transfers between devices  38.9 us (16%)
  local copies, waits for them, and re-layouts  36.7 us (15%)
  other arithmetic  7.69 us (3%)
    ppermute x9, waiting for transfers between devices, moved_along(): lax.ppermute(block, axis, [(i, (i + distance) % size) for i in range(size)])  50.5 us
    ppermute x12, waiting for transfers between devices, moved_along(): return lax.ppermute(block, 'expert', pairs)  42.5 us
    unnamed x129, local copies, waits for them, and re-layouts  36.7 us
    ppermute x12, starting transfers between devices, moved_along(): return lax.ppermute(block, 'expert', pairs)  21.2 us
    ppermute x9, starting transfers between devices, moved_along(): lax.ppermute(block, axis, [(i, (i + distance) % size) for i in range(size)])  12.4 us
    pallas_call x2, Pallas kernels, pack(): pl.pallas_call(functools.partial(pack_kernel, scale, experts, cap), grid=...  10.3 us
    pallas_call x2, Pallas kernels, up(): pl.pallas_call(functools.partial(up_kernel, count), grid=(steps,), in_spe...  10.2 us
    pallas_call x2, Pallas kernels, gate_up_parts(): pl.pallas_call(functools.partial(gate_up_kernel, own), grid_spec=pltpu.Pr...  9.87 us
  transfers between devices with their start and end apart: 22, of which 9 were waited for; matrix products, arithmetic and copies ran while one was open for 3% of the time, Pallas kernels for 18%

profile of v2, /device:TPU:0, one launch (start us, length us, event | category | flops | bytes accessed | tf_op | source)
XLA Modules:
  0.0 238.5 jit_solution(12779489131224737613)
XLA Ops:
  7.6 1.9 collective-permute-start.8
  9.5 1.9 collective-permute-start
  11.4 2.1 collective-permute-start.1
  13.5 6.3 %collective-permute-done.6.refs_1_.refs_5_ = bf16[128,2176]{1,0:T(8,128)(2,1)S(1)} collective-permute-done((bf16[128,2176]{1,0:T(8,128)(2,1)S(1)}, bf16[128,2176]{1,0:T(8,128)(2,1)S(1)}, u32[]{:S(2)}, u32[]{:S(2)}) %collective-permute-start.6) | collective-permute-done | bytes 557088 | tf_op jit(solution)/shard_map/ppermute | solution.py:43
  20.6 4.2 %collective-permute-start.2 = (bf16[128,2176]{1,0:T(8,128)(2,1)S(1)}, bf16[128,2176]{1,0:T(8,128)(2,1)S(1)}, u32[]{:S(2)}, u32[]{:S(2)}) collective-permute-start(bf16[128,2176]{1,0:T(8,128)(2,1)S(1)} %get-tuple-element.52.refs_0_.refs_4_.tail_ref), channel_id=1, source_target_pairs={{0,2},{1,3},{2,0},{3,1},{4,6},{5,7},{6,4},{7,5},{8,10},{9,11},{10,... | collective-permute-start | bytes 1671176 | tf_op jit(solution)/shard_map/ppermute | solution.py:43
  25.5 7.5 %collective-permute-done.8.refs_3_.refs_7_ = bf16[128,2176]{1,0:T(8,128)(2,1)} collective-permute-done((bf16[128,2176]{1,0:T(8,128)(2,1)S(1)}, bf16[128,2176]{1,0:T(8,128)(2,1)}, u32[]{:S(2)}, u32[]{:S(2)}) %collective-permute-start.8) | collective-permute-done | bytes 557088 | tf_op jit(solution)/shard_map/ppermute | solution.py:43
  34.1 5.2 %pack_rows.1 = (bf16[288,2048]{1,0:T(8,128)(2,1)S(1)}, bf16[288,2048]{1,0:T(8,128)(2,1)S(1)}, bf16[288,2048]{1,0:T(8,128)(2,1)S(1)}, bf16[288,2048]{1,0:T(8,128)(2,1)}) custom-call(s32[4]{0:T(128)S(1)} %get-tuple-element.105.eids_ref, bf16[128,2176]{1,0:T(8,128)(2,1)S(1)} %get-tuple-element.57.refs_0_.refs_4_, bf16[128,2176]{1,0:T(8,128)(2,1)S(1)} %copy-done.56, ...), custom_call_target="tpu_custom_call" | custom-call | flops 1207959552 | bytes 9437184 | tf_op jit(solution)/shard_map/pack_rows/pallas_call | solution.py:139
  40.3 4.0 %collective-permute-start.10 = (bf16[288,2048]{1,0:T(8,128)(2,1)S(1)}, bf16[288,2048]{1,0:T(8,128)(2,1)S(1)}, u32[]{:S(2)}, u32[]{:S(2)}) collective-permute-start(bf16[288,2048]{1,0:T(8,128)(2,1)S(1)} %get-tuple-element.61), channel_id=1, source_target_pairs={{0,3},{1,0},{2,1},{3,2},{4,7},{5,4},{6,5},{7,6},{8,11},{9,8},{10,9... | collective-permute-start | bytes 3538952 | tf_op jit(solution)/shard_map/ppermute | solution.py:43
  48.1 5.1 %pack_scaled.1 = (bf16[288,2048]{1,0:T(8,128)(2,1)S(1)}, bf16[288,2048]{1,0:T(8,128)(2,1)S(1)}, bf16[288,2048]{1,0:T(8,128)(2,1)S(1)}, bf16[288,2048]{1,0:T(8,128)(2,1)}) custom-call(s32[4]{0:T(128)S(1)} %get-tuple-element.106.eids_ref, bf16[128,2176]{1,0:T(8,128)(2,1)S(1)} %get-tuple-element.52.refs_0_.refs_4_.tail_ref, ...), custom_call_target="tpu_custom_call" | custom-call | flops 1207959552 | bytes 9437184 | tf_op jit(solution)/shard_map/pack_scaled/pallas_call | solution.py:139
  55.3 2.1 collective-permute-start.4
  57.4 11.3 %collective-permute-done.10.refs_2_ = bf16[288,2048]{1,0:T(8,128)(2,1)S(1)} collective-permute-done((bf16[288,2048]{1,0:T(8,128)(2,1)S(1)}, bf16[288,2048]{1,0:T(8,128)(2,1)S(1)}, u32[]{:S(2)}, u32[]{:S(2)}) %collective-permute-start.10) | collective-permute-done | bytes 1179680 | tf_op jit(solution)/shard_map/ppermute | solution.py:43
  69.7 2.4 collective-permute-done.9.refs_1_
  73.1 8.8 %collective-permute-done.3.refs_2_.refs_1_ = bf16[288,2048]{1,0:T(8,128)(2,1)S(1)} collective-permute-done((bf16[288,2048]{1,0:T(8,128)(2,1)S(1)}, bf16[288,2048]{1,0:T(8,128)(2,1)S(1)}, u32[]{:S(2)}, u32[]{:S(2)}) %collective-permute-start.3) | collective-permute-done | bytes 1179680 | tf_op jit(solution)/shard_map/ppermute | solution.py:43
  90.4 3.5 %dh.1 = (f32[288,768]{1,0:T(8,128)S(1)}, f32[288,768]{1,0:T(8,128)S(1)}, f32[288,768]{1,0:T(8,128)S(1)}) custom-call(bf16[288,2048]{1,0:T(8,128)(2,1)S(1)} %copy-done.27, bf16[288,2048]{1,0:T(8,128)(2,1)S(1)} %copy-done.31, bf16[288,2048]{1,0:T(8,128)(2,1)S(1)} %copy-done.35, bf16[768,2048]{1,0:T(8,128)(2,1)S(1)} %bitcast.28), custom_call_target="tpu_custom_call" | custom-call | flops 2717908992 | bytes 9338880 | tf_op jit(solution)/shard_map/dh/pallas_call | solution.py:244
  94.0 7.1 %up.2 = (f32[288,768]{1,0:T(8,128)S(1)}, f32[288,768]{1,0:T(8,128)S(1)}, f32[288,768]{1,0:T(8,128)S(1)}, f32[288,768]{1,0:T(8,128)S(1)}, f32[288,768]{1,0:T(8,12...) custom-call(bf16[288,2048]{1,0:T(8,128)(2,1)S(1)} %copy-done.16, ...), custom_call_target="tpu_custom_call" | custom-call | flops 5435817984 | bytes 17793024 | tf_op jit(solution)/shard_map/up/pallas_call | solution.py:213
  101.2 3.1 %up.3 = (f32[288,768]{1,0:T(8,128)S(1)}, f32[288,768]{1,0:T(8,128)S(1)}, f32[288,768]{1,0:T(8,128)S(1)}) custom-call(bf16[288,2048]{1,0:T(8,128)(2,1)S(1)} %collective-permute-done.11.refs_0_.refs_3_, bf16[2048,1536]{1,0:T(8,128)(2,1)S(1)} %bitcast.25, bf16[2048,1536]{1,0:T(8,128)(2,1)S(1)} %bitcast.26), custom_call_target="tpu_custom_call" | custom-call | flops 1811939328 | bytes 10125312 | tf_op jit(solution)/shard_map/up/pallas_call | solution.py:213
  105.3 6.2 %collective-permute-done.5.refs_4_.refs_0_ = bf16[288,2048]{1,0:T(8,128)(2,1)} collective-permute-done((bf16[288,2048]{1,0:T(8,128)(2,1)}, bf16[288,2048]{1,0:T(8,128)(2,1)}, u32[]{:S(2)}, u32[]{:S(2)}) %collective-permute-start.5) | collective-permute-done | bytes 1179680 | tf_op jit(solution)/shard_map/ppermute | solution.py:43
  111.5 5.2 %down_parts.1 = (bf16[768,512]{1,0:T(8,128)(2,1)S(1)}, bf16[768,512]{1,0:T(8,128)(2,1)S(1)}, f32[384,512]{1,0:T(8,128)S(1)}, f32[384,512]{1,0:T(8,128)S(1)}) custom-call(s32[1]{0:T(128)} %bitcast.6.place_ref, bf16[768,1152]{1,0:T(8,128)(2,1)S(1)} %turned.1.refs_0_, bf16[288,2048]{1,0:T(8,128)(2,1)S(1)} %copy-done.28, bf16[288,2048]{1,0:T(8,128)(2,1)S(1)} %copy-done.32, ...), custom_call_target="tpu_custom_call" | custom-call | flops 2717908992 | bytes 9437184 | tf_op jit(solution)/shard_map/down_parts/pallas_call | solution.py:376
  117.7 4.4 %dab.1 = (bf16[1152,768]{1,0:T(8,128)(2,1)S(1)}, bf16[1152,768]{1,0:T(8,128)(2,1)S(1)}) custom-call(bf16[288,2048]{1,0:T(8,128)(2,1)} %collective-permute-done.5.refs_4_.refs_0_, bf16[768,2048]{1,0:T(8,128)(2,1)S(1)} %bitcast.29, f32[288,768]{1,0:T(8,128)S(1)} %get-tuple-element.77.refs_2_, f32[288,768]{1,0:T(8,128)S(1)} %get-tuple-element.78.refs_3_, ...), custom_call_target="tpu_custom_call" | custom-call | flops 905969664 | bytes 14155776 | tf_op jit(solution)/shard_map/dab/pallas_call | solution.py:301
  122.1 9.1 %slot_rows.1 = bf16[16,72,2048]{2,1,0:T(8,128)(2,1)S(1)} custom-call(s32[16]{0:T(128)S(1)} %add.106.to_ref, bf16[1152,768]{1,0:T(8,128)(2,1)S(1)} %get-tuple-element.91.refs_0_.refs_4_, bf16[1152,768]{1,0:T(8,128)(2,1)S(1)} %get-tuple-element.92.refs_1_.refs_5_, bf16[2048,1536]{1,0:T(8,128)(2,1)S(1)} %bitcast.27), custom_call_target="tpu_custom_call" | custom-call | flops 7247757312 | bytes 9830400 | tf_op jit(solution)/shard_map/slot_rows/pallas_call | solution.py:438
  131.3 2.2 copy-done.2
  135.9 5.3 %all-to-all-start = ((bf16[16,72,2048]{2,1,0:T(8,128)(2,1)}), bf16[16,72,2048]{2,1,0:T(8,128)(2,1)}, u32[]{:S(2)}, u32[]{:S(2)}) async-start(bf16[16,72,2048]{2,1,0:T(8,128)(2,1)} %copy-done.2), calls=%async_computation | async-start | bytes 9437184 | tf_op jit(solution)/shard_map/all_to_all | solution.py:505
  146.8 7.6 %gate_up_parts.1 = (bf16[512,1536]{1,0:T(8,128)(2,1)S(1)}, bf16[512,1536]{1,0:T(8,128)(2,1)S(1)}, f32[256,1536]{1,0:T(8,128)S(1)}, f32[256,1536]{1,0:T(8,128)S(1)}) custom-call(s32[1]{0:T(128)} %bitcast.6.place_ref, bf16[288,2048]{1,0:T(8,128)(2,1)S(1)} %copy-done.17, bf16[288,2048]{1,0:T(8,128)(2,1)S(1)} %copy-done.25, bf16[288,2048]{1,0:T(8,128)(2,1)S(1)} %copy-done.21, ...), custom_call_target="tpu_custom_call" | custom-call | flops 5435817984 | bytes 9437184 | tf_op jit(solution)/shard_map/gate_up_parts/pallas_call | solution.py:409
  154.4 3.1 %collective-permute-start.13 = (bf16[512,1536]{1,0:T(8,128)(2,1)S(1)}, bf16[512,1536]{1,0:T(8,128)(2,1)S(1)}, u32[]{:S(2)}, u32[]{:S(2)}) collective-permute-start(bf16[512,1536]{1,0:T(8,128)(2,1)S(1)} %get-tuple-element.93), channel_id=1, source_target_pairs={{0,48},{16,0},{32,16},{48,32},{1,49},{17,1},{33,17},{49,33},{2,50}... | collective-permute-start | bytes 4718600 | tf_op jit(solution)/shard_map/ppermute | solution.py:35
  159.5 45.6 %collective-permute-done.17 = bf16[768,512]{1,0:T(8,128)(2,1)S(1)} collective-permute-done((bf16[768,512]{1,0:T(8,128)(2,1)S(1)}, bf16[768,512]{1,0:T(8,128)(2,1)S(1)}, u32[]{:S(2)}, u32[]{:S(2)}) %collective-permute-start.17) | collective-permute-done | bytes 786464 | tf_op jit(solution)/shard_map/ppermute | solution.py:35
  205.3 3.6 %collective-permute-start.20 = (bf16[384,512]{1,0:T(8,128)(2,1)S(1)}, bf16[384,512]{1,0:T(8,128)(2,1)S(1)}, u32[]{:S(2)}, u32[]{:S(2)}) collective-permute-start(bf16[384,512]{1,0:T(8,128)(2,1)S(1)} %add_convert_fusion.2), channel_id=1, source_target_pairs={{0,48},{16,0},{32,16},{48,32},{1,49},{17,1},{33,17},{49,33},{2,50}... | collective-permute-start | bytes 1179656 | tf_op jit(solution)/shard_map/ppermute | solution.py:35
  210.7 3.2 %collective-permute-start.16 = (bf16[256,1536]{1,0:T(8,128)(2,1)}, bf16[256,1536]{1,0:T(8,128)(2,1)}, u32[]{:S(2)}, u32[]{:S(2)}) collective-permute-start(bf16[256,1536]{1,0:T(8,128)(2,1)} %add_convert_fusion), channel_id=1, source_target_pairs={{0,48},{16,0},{32,16},{48,32},{1,49},{17,1},{33,17},{49,33},{2,50}... | collective-permute-start | bytes 2359304 | tf_op jit(solution)/shard_map/ppermute | solution.py:35
  216.6 3.0 %down_own.1 = f32[768,512]{1,0:T(8,128)S(1)} custom-call(s32[1]{0:T(128)} %bitcast.6.place_ref, bf16[768,1152]{1,0:T(8,128)(2,1)S(1)} %copy-done.1, bf16[288,2048]{1,0:T(8,128)(2,1)S(1)} %copy-done.29, bf16[288,2048]{1,0:T(8,128)(2,1)S(1)} %copy-done.33, bf16[288,2048]{1,0:T(8,128)(2,1)S(1)} %copy-done.37, ...), custom_call_target="tpu_custom_call" | custom-call | flops 905969664 | bytes 9437184 | tf_op jit(solution)/shard_map/down_own/pallas_call | solution.py:376
  219.6 2.2 gate_up_own.1
  225.8 4.2 %home.1 = bf16[128,2048]{1,0:T(8,128)(2,1)S(1)} custom-call(bf16[128,2176]{1,0:T(8,128)(2,1)S(1)} %copy-done.43, bf16[1152,2048]{1,0:T(8,128)(2,1)} %bitcast.9.rows_ref, bf16[128,2048]{1,0:T(8,128)(2,1)S(1)} %bitcast.31), custom_call_target="tpu_custom_call" | custom-call | flops 603979776 | bytes 5767168 | tf_op jit(solution)/shard_map/home/pallas_call | solution.py:177
  230.2 4.3 %collective-permute-done.15 = bf16[256,1536]{1,0:T(8,128)(2,1)} collective-permute-done((bf16[256,1536]{1,0:T(8,128)(2,1)}, bf16[256,1536]{1,0:T(8,128)(2,1)}, u32[]{:S(2)}, u32[]{:S(2)}) %collective-permute-start.15) | collective-permute-done | bytes 786464 | tf_op jit(solution)/shard_map/ppermute | solution.py:35
  234.5 2.0 fusion.4
  (168 shorter events, 49.5 us)
Async XLA Ops:
  4.2 41.7 %copy-start.42 = (bf16[128,2176]{1,0:T(8,128)(2,1)}, bf16[128,2176]{1,0:T(8,128)(2,1)S(1)}, u32[]{:S(2)}) copy-start(bf16[128,2176]{1,0:T(8,128)(2,1)S(1)} %get-tuple-element.52.refs_0_.refs_4_.tail_ref) | copy-start | bytes 1671172
  4.2 15.5 %collective-permute-start.6 = (bf16[128,2176]{1,0:T(8,128)(2,1)S(1)}, bf16[128,2176]{1,0:T(8,128)(2,1)S(1)}, u32[]{:S(2)}, u32[]{:S(2)}) collective-permute-start(bf16[128,2176]{1,0:T(8,128)(2,1)S(1)} %get-tuple-element.57.refs_0_.refs_4_), channel_id=1, source_target_pairs={{0,4},{1,5},{2,6},{3,7},{4,8},{5,9},{6,10},{7,11},{8,12},{9,13},{1... | collective-permute-start | bytes 1671176 | tf_op jit(solution)/shard_map/ppermute | solution.py:43
  5.9 19.6 %collective-permute-start.7 = (bf16[128,2176]{1,0:T(8,128)(2,1)S(1)}, bf16[128,2176]{1,0:T(8,128)(2,1)}, u32[]{:S(2)}, u32[]{:S(2)}) collective-permute-start(bf16[128,2176]{1,0:T(8,128)(2,1)S(1)} %get-tuple-element.57.refs_0_.refs_4_), channel_id=1, source_target_pairs={{0,12},{1,13},{2,14},{3,15},{4,0},{5,1},{6,2},{7,3},{8,4},{9,5},{1... | collective-permute-start | bytes 1671176 | tf_op jit(solution)/shard_map/ppermute | solution.py:43
  7.6 25.4 %collective-permute-start.8 = (bf16[128,2176]{1,0:T(8,128)(2,1)S(1)}, bf16[128,2176]{1,0:T(8,128)(2,1)}, u32[]{:S(2)}, u32[]{:S(2)}) collective-permute-start(bf16[128,2176]{1,0:T(8,128)(2,1)S(1)} %get-tuple-element.57.refs_0_.refs_4_), channel_id=1, source_target_pairs={{0,8},{1,9},{2,10},{3,11},{4,12},{5,13},{6,14},{7,15},{8,0},{9,1},... | collective-permute-start | bytes 1671176 | tf_op jit(solution)/shard_map/ppermute | solution.py:43
  9.5 34.9 %collective-permute-start = (bf16[128,2176]{1,0:T(8,128)(2,1)S(1)}, bf16[128,2176]{1,0:T(8,128)(2,1)S(1)}, u32[]{:S(2)}, u32[]{:S(2)}) collective-permute-start(bf16[128,2176]{1,0:T(8,128)(2,1)S(1)} %get-tuple-element.52.refs_0_.refs_4_.tail_ref), channel_id=1, source_target_pairs={{0,1},{1,2},{2,3},{3,0},{4,5},{5,6},{6,7},{7,4},{8,9},{9,10},{10,1... | collective-permute-start | bytes 1671176 | tf_op jit(solution)/shard_map/ppermute | solution.py:43
  11.4 33.0 %collective-permute-start.1 = (bf16[128,2176]{1,0:T(8,128)(2,1)S(1)}, bf16[128,2176]{1,0:T(8,128)(2,1)S(1)}, u32[]{:S(2)}, u32[]{:S(2)}) collective-permute-start(bf16[128,2176]{1,0:T(8,128)(2,1)S(1)} %get-tuple-element.52.refs_0_.refs_4_.tail_ref), channel_id=1, source_target_pairs={{0,3},{1,0},{2,1},{3,2},{4,7},{5,4},{6,5},{7,6},{8,11},{9,8},{10,9... | collective-permute-start | bytes 1671176 | tf_op jit(solution)/shard_map/ppermute | solution.py:43
  20.6 24.6 %collective-permute-start.2 = (bf16[128,2176]{1,0:T(8,128)(2,1)S(1)}, bf16[128,2176]{1,0:T(8,128)(2,1)S(1)}, u32[]{:S(2)}, u32[]{:S(2)}) collective-permute-start(bf16[128,2176]{1,0:T(8,128)(2,1)S(1)} %get-tuple-element.52.refs_0_.refs_4_.tail_ref), channel_id=1, source_target_pairs={{0,2},{1,3},{2,0},{3,1},{4,6},{5,7},{6,4},{7,5},{8,10},{9,11},{10,... | collective-permute-start | bytes 1671176 | tf_op jit(solution)/shard_map/ppermute | solution.py:43
  40.3 28.4 %collective-permute-start.10 = (bf16[288,2048]{1,0:T(8,128)(2,1)S(1)}, bf16[288,2048]{1,0:T(8,128)(2,1)S(1)}, u32[]{:S(2)}, u32[]{:S(2)}) collective-permute-start(bf16[288,2048]{1,0:T(8,128)(2,1)S(1)} %get-tuple-element.61), channel_id=1, source_target_pairs={{0,3},{1,0},{2,1},{3,2},{4,7},{5,4},{6,5},{7,6},{8,11},{9,8},{10,9... | collective-permute-start | bytes 3538952 | tf_op jit(solution)/shard_map/ppermute | solution.py:43
  44.3 27.8 %collective-permute-start.9 = (bf16[288,2048]{1,0:T(8,128)(2,1)S(1)}, bf16[288,2048]{1,0:T(8,128)(2,1)S(1)}, u32[]{:S(2)}, u32[]{:S(2)}) collective-permute-start(bf16[288,2048]{1,0:T(8,128)(2,1)S(1)} %get-tuple-element.60), channel_id=1, source_target_pairs={{0,1},{1,2},{2,3},{3,0},{4,5},{5,6},{6,7},{7,4},{8,9},{9,10},{10,1... | collective-permute-start | bytes 3538952 | tf_op jit(solution)/shard_map/ppermute | solution.py:43
  48.1 36.4 %copy-start.61 = (s32[4]{0:T(128)S(1)}, s32[4]{0:T(128)}, u32[]{:S(2)}) copy-start(s32[4]{0:T(128)} %constant.75) | copy-start | bytes 52
  48.1 45.9 %slice-start = ((s8[6291456]{0:T(1024)(128)(4,1)}), s8[2097152]{0:T(1024)(128)(4,1)S(1)}, s32[]{:S(2)}) async-start(s8[6291456]{0:T(1024)(128)(4,1)} %bitcast.21), calls=%async_computation.1 | async-start | bytes 4194304
  54.2 27.8 %collective-permute-start.3 = (bf16[288,2048]{1,0:T(8,128)(2,1)S(1)}, bf16[288,2048]{1,0:T(8,128)(2,1)S(1)}, u32[]{:S(2)}, u32[]{:S(2)}) collective-permute-start(bf16[288,2048]{1,0:T(8,128)(2,1)S(1)} %get-tuple-element.54), channel_id=1, source_target_pairs={{0,4},{1,5},{2,6},{3,7},{4,8},{5,9},{6,10},{7,11},{8,12},{9,13},{1... | collective-permute-start | bytes 3538952 | tf_op jit(solution)/shard_map/ppermute | solution.py:43
  55.3 27.7 %collective-permute-start.4 = (bf16[288,2048]{1,0:T(8,128)(2,1)S(1)}, bf16[288,2048]{1,0:T(8,128)(2,1)S(1)}, u32[]{:S(2)}, u32[]{:S(2)}) collective-permute-start(bf16[288,2048]{1,0:T(8,128)(2,1)S(1)} %get-tuple-element.55), channel_id=1, source_target_pairs={{0,12},{1,13},{2,14},{3,15},{4,0},{5,1},{6,2},{7,3},{8,4},{9,5},{1... | collective-permute-start | bytes 3538952 | tf_op jit(solution)/shard_map/ppermute | solution.py:43
  73.1 28.0 %collective-permute-start.11 = (bf16[288,2048]{1,0:T(8,128)(2,1)}, bf16[288,2048]{1,0:T(8,128)(2,1)S(1)}, u32[]{:S(2)}, u32[]{:S(2)}) collective-permute-start(bf16[288,2048]{1,0:T(8,128)(2,1)} %get-tuple-element.67), channel_id=1, source_target_pairs={{0,2},{1,3},{2,0},{3,1},{4,6},{5,7},{6,4},{7,5},{8,10},{9,11},{10,... | collective-permute-start | bytes 3538952 | tf_op jit(solution)/shard_map/ppermute | solution.py:43
  84.1 27.5 %collective-permute-start.5 = (bf16[288,2048]{1,0:T(8,128)(2,1)}, bf16[288,2048]{1,0:T(8,128)(2,1)}, u32[]{:S(2)}, u32[]{:S(2)}) collective-permute-start(bf16[288,2048]{1,0:T(8,128)(2,1)} %get-tuple-element.56), channel_id=1, source_target_pairs={{0,8},{1,9},{2,10},{3,11},{4,12},{5,13},{6,14},{7,15},{8,0},{9,1},... | collective-permute-start | bytes 3538952 | tf_op jit(solution)/shard_map/ppermute | solution.py:43
  101.1 40.1 %copy-start.3 = (bf16[288,2048]{1,0:T(8,128)(2,1)}, bf16[288,2048]{1,0:T(8,128)(2,1)S(1)}, u32[]{:S(2)}) copy-start(bf16[288,2048]{1,0:T(8,128)(2,1)S(1)} %collective-permute-done.11.refs_0_.refs_3_) | copy-start | bytes 3538948
  105.3 11.5 %copy-start = (bf16[768,1152]{1,0:T(8,128)(2,1)}, bf16[768,1152]{1,0:T(8,128)(2,1)S(1)}, u32[]{:S(2)}) copy-start(bf16[768,1152]{1,0:T(8,128)(2,1)S(1)} %turned.1.refs_0_) | copy-start | bytes 5308420
  135.9 87.8 %all-to-all-start = ((bf16[16,72,2048]{2,1,0:T(8,128)(2,1)}), bf16[16,72,2048]{2,1,0:T(8,128)(2,1)}, u32[]{:S(2)}, u32[]{:S(2)}) async-start(bf16[16,72,2048]{2,1,0:T(8,128)(2,1)} %copy-done.2), calls=%async_computation | async-start | bytes 9437184 | tf_op jit(solution)/shard_map/all_to_all | solution.py:505
  146.7 10.7 %copy-start.50 = (bf16[768,512]{1,0:T(8,128)(2,1)S(1)}, bf16[768,512]{1,0:T(8,128)(2,1)}, u32[]{:S(2)}) copy-start(bf16[768,512]{1,0:T(8,128)(2,1)} %copy-done.49) | copy-start | bytes 2359300
  146.8 11.5 %copy-start.48 = (bf16[768,512]{1,0:T(8,128)(2,1)S(1)}, bf16[768,512]{1,0:T(8,128)(2,1)}, u32[]{:S(2)}) copy-start(bf16[768,512]{1,0:T(8,128)(2,1)} %copy-done.47) | copy-start | bytes 2359300
  146.8 58.4 %copy-start.41 = (f32[384,512]{1,0:T(8,128)S(1)}, f32[384,512]{1,0:T(8,128)}, u32[]{:S(2)}) copy-start(f32[384,512]{1,0:T(8,128)} %copy-done.40) | copy-start | bytes 2359300
  154.4 54.5 %copy-start.39 = (f32[384,512]{1,0:T(8,128)S(1)}, f32[384,512]{1,0:T(8,128)}, u32[]{:S(2)}) copy-start(f32[384,512]{1,0:T(8,128)} %copy-done.38) | copy-start | bytes 2359300
  154.4 54.9 %collective-permute-start.13 = (bf16[512,1536]{1,0:T(8,128)(2,1)S(1)}, bf16[512,1536]{1,0:T(8,128)(2,1)S(1)}, u32[]{:S(2)}, u32[]{:S(2)}) collective-permute-start(bf16[512,1536]{1,0:T(8,128)(2,1)S(1)} %get-tuple-element.93), channel_id=1, source_target_pairs={{0,48},{16,0},{32,16},{48,32},{1,49},{17,1},{33,17},{49,33},{2,50}... | collective-permute-start | bytes 4718600 | tf_op jit(solution)/shard_map/ppermute | solution.py:35
  157.5 47.7 %collective-permute-start.17 = (bf16[768,512]{1,0:T(8,128)(2,1)S(1)}, bf16[768,512]{1,0:T(8,128)(2,1)S(1)}, u32[]{:S(2)}, u32[]{:S(2)}) collective-permute-start(bf16[768,512]{1,0:T(8,128)(2,1)S(1)} %copy-done.50), channel_id=1, source_target_pairs={{0,48},{16,0},{32,16},{48,32},{1,49},{17,1},{33,17},{49,33},{2,50}... | collective-permute-start | bytes 2359304 | tf_op jit(solution)/shard_map/ppermute | solution.py:35
  158.2 50.7 %collective-permute-start.18 = (bf16[768,512]{1,0:T(8,128)(2,1)S(1)}, bf16[768,512]{1,0:T(8,128)(2,1)S(1)}, u32[]{:S(2)}, u32[]{:S(2)}) collective-permute-start(bf16[768,512]{1,0:T(8,128)(2,1)S(1)} %copy-done.48), channel_id=1, source_target_pairs={{0,16},{16,32},{32,48},{48,0},{1,17},{17,33},{33,49},{49,1},{2,18}... | collective-permute-start | bytes 2359304 | tf_op jit(solution)/shard_map/ppermute | solution.py:35
  159.5 54.4 %collective-permute-start.14 = (bf16[512,1536]{1,0:T(8,128)(2,1)S(1)}, bf16[512,1536]{1,0:T(8,128)(2,1)S(1)}, u32[]{:S(2)}, u32[]{:S(2)}) collective-permute-start(bf16[512,1536]{1,0:T(8,128)(2,1)S(1)} %get-tuple-element.95), channel_id=1, source_target_pairs={{0,16},{16,32},{32,48},{48,0},{1,17},{17,33},{33,49},{49,1},{2,18}... | collective-permute-start | bytes 4718600 | tf_op jit(solution)/shard_map/ppermute | solution.py:35
  205.3 16.6 %collective-permute-start.20 = (bf16[384,512]{1,0:T(8,128)(2,1)S(1)}, bf16[384,512]{1,0:T(8,128)(2,1)S(1)}, u32[]{:S(2)}, u32[]{:S(2)}) collective-permute-start(bf16[384,512]{1,0:T(8,128)(2,1)S(1)} %add_convert_fusion.2), channel_id=1, source_target_pairs={{0,48},{16,0},{32,16},{48,32},{1,49},{17,1},{33,17},{49,33},{2,50}... | collective-permute-start | bytes 1179656 | tf_op jit(solution)/shard_map/ppermute | solution.py:35
  209.0 13.5 %collective-permute-start.19 = (bf16[384,512]{1,0:T(8,128)(2,1)S(1)}, bf16[384,512]{1,0:T(8,128)(2,1)S(1)}, u32[]{:S(2)}, u32[]{:S(2)}) collective-permute-start(bf16[384,512]{1,0:T(8,128)(2,1)S(1)} %add_convert_fusion.3), channel_id=1, source_target_pairs={{0,16},{16,32},{32,48},{48,0},{1,17},{17,33},{33,49},{49,1},{2,18}... | collective-permute-start | bytes 1179656 | tf_op jit(solution)/shard_map/ppermute | solution.py:35
  210.7 19.4 %collective-permute-start.16 = (bf16[256,1536]{1,0:T(8,128)(2,1)}, bf16[256,1536]{1,0:T(8,128)(2,1)}, u32[]{:S(2)}, u32[]{:S(2)}) collective-permute-start(bf16[256,1536]{1,0:T(8,128)(2,1)} %add_convert_fusion), channel_id=1, source_target_pairs={{0,48},{16,0},{32,16},{48,32},{1,49},{17,1},{33,17},{49,33},{2,50}... | collective-permute-start | bytes 2359304 | tf_op jit(solution)/shard_map/ppermute | solution.py:35
  215.4 19.1 %collective-permute-start.15 = (bf16[256,1536]{1,0:T(8,128)(2,1)}, bf16[256,1536]{1,0:T(8,128)(2,1)}, u32[]{:S(2)}, u32[]{:S(2)}) collective-permute-start(bf16[256,1536]{1,0:T(8,128)(2,1)} %add_convert_fusion.1), channel_id=1, source_target_pairs={{0,16},{16,32},{32,48},{48,0},{1,17},{17,33},{33,49},{49,1},{2,18}... | collective-permute-start | bytes 2359304 | tf_op jit(solution)/shard_map/ppermute | solution.py:35
  225.8 8.6 %copy-start.60 = (bf16[512,1536]{1,0:T(8,128)(2,1)S(1)}, bf16[512,1536]{1,0:T(8,128)(2,1)}, u32[]{:S(2)}) copy-start(bf16[512,1536]{1,0:T(8,128)(2,1)} %copy-done.59) | copy-start | bytes 4718596
  230.1 7.6 %collective-permute-start.12 = (bf16[128,2048]{1,0:T(8,128)(2,1)S(1)}, bf16[128,2048]{1,0:T(8,128)(2,1)S(1)}, u32[]{:S(2)}, u32[]{:S(2)}) collective-permute-start(bf16[128,2048]{1,0:T(8,128)(2,1)S(1)} %home.1), channel_id=1, source_target_pairs={{0,64},{64,0},{1,65},{65,1},{2,66},{66,2},{3,67},{67,3},{4,68},{68... | collective-permute-start | bytes 1572872 | tf_op jit(solution)/shard_map/ppermute | solution.py:35
  (54 other events, 144.9 us)

commit v3 on v2

v3 whole, which is shorter than its diff:
```python
import functools

import jax
import jax.numpy as jnp
from jax import lax
from jax.experimental import pallas as pl
from jax.experimental.pallas import tpu as pltpu
from jax.sharding import PartitionSpec as P

BF16 = jnp.bfloat16
F32 = jnp.float32
OFF = (0, 1, 3, 2)
SIDE = 4
LANES = 128
MIB = 1024 * 1024


def params(steps):
    return pltpu.CompilerParams(
        vmem_limit_bytes=58 * MIB, dimension_semantics=("arbitrary",) * steps
    )


SCALARS = pl.BlockSpec(memory_space=pltpu.SMEM)
FAR = pl.BlockSpec(memory_space=pl.ANY)


def begun(src, dst, sem):
    copy = pltpu.make_async_copy(src, dst, sem)
    copy.start()
    return copy


def held(shape, index):
    return pl.BlockSpec(shape, index, pipeline_mode=pl.Buffered(1))


def cost(flops, moved):
    return pl.CostEstimate(flops=int(flops), bytes_accessed=int(moved), transcendentals=0)


def moved_along(block, axis, distance):
    if axis == "edata" or axis == "section":
        size = lax.axis_size(axis)
        return lax.ppermute(block, axis, [(i, (i + distance) % size) for i in range(size)])
    pairs = []
    for a in range(SIDE):
        for b in range(SIDE):
            if axis == "x":
                pairs.append((a * SIDE + b, (a + distance) % SIDE * SIDE + b))
            else:
                pairs.append((a * SIDE + b, a * SIDE + (b + distance) % SIDE))
    return lax.ppermute(block, "expert", pairs)


def iota(shape, dim):
    return lax.broadcasted_iota(jnp.int32, shape, dim)


def dot(a, b, da=1, db=0):
    return lax.dot_general(a, b, (((da,), (db,)), ((), ())), preferred_element_type=F32)


def prep_kernel(experts, routes_ref, gates_ref, x_ref, g_ref, xe_ref, ge_ref, tail_ref):
    tok, width = x_ref.shape
    topk = routes_ref.shape[0]
    expert = lax.rem(iota((LANES, tok), 0), experts)
    full = jnp.zeros((LANES, tok), F32)
    for k in range(topk):
        full += jnp.where(routes_ref[k : k + 1, :] == expert, gates_ref[k : k + 1, :], 0.0)
    full = full.T
    lane = iota((tok, LANES), 1)
    high = full.astype(BF16).astype(F32)
    rest = full - high
    middle = rest.astype(BF16).astype(F32)
    low = rest - middle
    piece = jnp.where(lane < 2 * experts, middle, jnp.where(lane < 3 * experts, low, 0.0))
    piece = jnp.where(lane < experts, high, piece).astype(BF16)
    for src, dst in ((x_ref, xe_ref), (g_ref, ge_ref)):
        dst[:, :width] = src[...]
        dst[:, width:] = piece
    tail_ref[...] = piece


def prep(routes, gates, x, g, experts):
    tok, width = x.shape
    shape = jax.ShapeDtypeStruct((tok, width + LANES), BF16)
    return pl.pallas_call(
        functools.partial(prep_kernel, experts),
        out_shape=(shape, shape, jax.ShapeDtypeStruct((tok, LANES), BF16)),
        compiler_params=params(0),
        name="prep",
    )(routes, gates, x, g)


def places(piece, experts, blocks):
    rows = piece.shape[0]
    tok = rows // blocks
    r, c = iota((rows, rows), 0), iota((rows, rows), 1)
    upto = jnp.where((c <= r) & (lax.div(c, tok) == lax.div(r, tok)), 1.0, 0.0).astype(BF16)
    lane = iota((rows, LANES), 1)
    mask = jnp.where((lane < experts) & (piece.astype(F32) > 0.0), 1.0, 0.0)
    return (dot(upto, mask.astype(BF16)) * mask).astype(BF16)


def pack_kernel(scale, experts, cap, eids_ref, *refs):
    blocks, outs = refs[:4], refs[4:8]
    rows_v, packed_v, table_v, in_sems, out_sems = refs[8:]
    pair = 2 * cap
    tok, width = blocks[0].shape[0], outs[0].shape[1]
    steps, step = packed_v.shape[0], packed_v.shape[3]
    pieces = [slice(width, width + LANES)] + [slice(t * step, (t + 1) * step) for t in range(steps)]
    loads = []
    for n, cols in enumerate(pieces):
        for b in range(4):
            part = rows_v.at[b // 2, pl.ds(b % 2 * tok, tok), cols]
            loads.append(begun(blocks[b].at[:, cols], part, in_sems.at[n, b]))
    for load in loads[:4]:
        load.wait()
    lane = iota((pair, LANES), 1)
    second = jnp.where(iota((pair, 2 * tok), 1) >= tok, cap, 0)
    place = iota((pair, 2 * tok), 0) + 1 - second
    place = jnp.where(place > 0, place, -1).astype(F32)
    factors = []
    for p in range(2):
        piece = rows_v[p, :, width:]
        known = places(piece, experts, 2)
        for j in range(SIDE):
            choose = jnp.where(lane == eids_ref[j], 1.0, 0.0).astype(BF16)
            found = dot(choose, known, 1, 1)
            table = jnp.where(found == place, 1.0, 0.0).astype(BF16)
            table_v[p, j * pair : (j + 1) * pair, :] = table
            if scale:
                mine = (lax.rem(lane, experts) == eids_ref[j]) & (lane < 3 * experts)
                gate = jnp.where(mine, dot(table, piece), 0.0)
                factors.append(jnp.sum(gate, axis=1, keepdims=True))
    stores = []
    for t in range(steps):
        for load in loads[4 * t + 4 : 4 * t + 8]:
            load.wait()
        for p in range(2):
            packed = dot(table_v[p], rows_v[p, :, pieces[t + 1]])
            for j in range(SIDE):
                part = packed[j * pair : (j + 1) * pair]
                if scale:
                    part = part * factors[p * SIDE + j]
                packed_v[t, j, p * pair : (p + 1) * pair, :] = part.astype(BF16)
        for j in range(SIDE):
            target = outs[j].at[:, pieces[t + 1]]
            stores.append(begun(packed_v.at[t, j], target, out_sems.at[t, j]))
    for store in stores:
        store.wait()


def pack(eids, blocks, width, experts, cap, scale):
    tok = blocks[0].shape[0]
    step = 512
    steps = width // step
    pair = 2 * cap
    out = jax.ShapeDtypeStruct((2 * pair, width), BF16)
    return pl.pallas_call(
        functools.partial(pack_kernel, scale, experts, cap),
        in_specs=[SCALARS] + [FAR] * 4,
        out_specs=[FAR] * 4,
        out_shape=[out] * 4,
        scratch_shapes=[
            pltpu.VMEM((2, 2 * tok, width + LANES), BF16),
            pltpu.VMEM((steps, SIDE, 2 * pair, step), BF16),
            pltpu.VMEM((2, SIDE * pair, 2 * tok), BF16),
            pltpu.SemaphoreType.DMA((steps + 1, 4)),
            pltpu.SemaphoreType.DMA((steps, SIDE)),
        ],
        compiler_params=params(0),
        cost_estimate=cost(3e9, 10e6),
        name="pack_scaled" if scale else "pack_rows",
    )(eids, *blocks)


def home_kernel(experts, cap, tail_ref, rows_ref, grad_ref, out_ref, table_ref):
    tok = tail_ref.shape[0]
    total = experts * cap

    @pl.when(pl.program_id(0) == 0)
    def _():
        choose = jnp.where(iota((LANES, total), 0) == lax.div(iota((LANES, total), 1), cap), 1.0, 0.0)
        found = dot(places(tail_ref[...], experts, 1), choose.astype(BF16))
        place = lax.rem(iota((tok, total), 1), cap) + 1
        table_ref[...] = jnp.where(found == place.astype(F32), 1.0, 0.0).astype(BF16)

    total_grad = dot(table_ref[...], rows_ref[...]) + grad_ref[...].astype(F32)
    out_ref[...] = total_grad.astype(BF16)


def home(tail, rows, grad, experts, cap):
    tok, width = grad.shape
    step = 512
    total = experts * cap
    return pl.pallas_call(
        functools.partial(home_kernel, experts, cap),
        grid=(width // step,),
        in_specs=[
            held((tok, LANES), lambda i: (0, 0)),
            pl.BlockSpec((total, step), lambda i: (0, i)),
            pl.BlockSpec((tok, step), lambda i: (0, i)),
        ],
        out_specs=pl.BlockSpec((tok, step), lambda i: (0, i)),
        out_shape=jax.ShapeDtypeStruct((tok, width), BF16),
        scratch_shapes=[pltpu.VMEM((tok, total), BF16)],
        compiler_params=params(1),
        cost_estimate=cost(3e9, 10e6),
        name="home",
    )(tail, rows, grad)


def up_kernel(count, *refs):
    xs, (wa, wb), outs = refs[:count], refs[count : count + 2], refs[count + 2 :]
    for i in range(count):
        rows = xs[i][...]
        a = dot(rows, wa[...])
        b = dot(rows, wb[...])
        sig = jax.nn.sigmoid(a)
        outs[3 * i][...] = a * sig * b
        outs[3 * i + 1][...] = (b * sig * (1.0 + a * (1.0 - sig))).astype(BF16)
        outs[3 * i + 2][...] = (a * sig).astype(BF16)


def up(xs, wgu):
    count = len(xs)
    rows, width = xs[0].shape
    hidden = wgu.shape[1] // 2
    step = 256
    steps = hidden // step
    kinds = (F32, BF16, BF16) * count
    flat = pl.pallas_call(
        functools.partial(up_kernel, count),
        grid=(steps,),
        in_specs=[held((rows, width), lambda i: (0, 0))] * count
        + [
            pl.BlockSpec((width, step), lambda i: (0, i)),
            pl.BlockSpec((width, step), lambda i: (0, i + steps)),
        ],
        out_specs=[pl.BlockSpec((rows, step), lambda i: (0, i))] * (3 * count),
        out_shape=[jax.ShapeDtypeStruct((rows, hidden), kind) for kind in kinds],
        compiler_params=params(1),
        cost_estimate=cost(3e9, 10e6),
        name="up",
    )(*xs, wgu, wgu)
    return [flat[3 * i : 3 * i + 3] for i in range(count)]


def dh_kernel(count, *refs):
    ss, wd, outs = refs[:count], refs[count], refs[count + 1 :]
    for i in range(count):
        outs[i][...] = dot(ss[i][...], wd[...], 1, 1)


def dh_of(ss, wdown):
    count = len(ss)
    rows, width = ss[0].shape
    hidden = wdown.shape[0]
    step = 256
    return pl.pallas_call(
        functools.partial(dh_kernel, count),
        grid=(hidden // step,),
        in_specs=[held((rows, width), lambda i: (0, 0))] * count
        + [pl.BlockSpec((step, width), lambda i: (i, 0))],
        out_specs=[pl.BlockSpec((rows, step), lambda i: (0, i))] * count,
        out_shape=[jax.ShapeDtypeStruct((rows, hidden), F32)] * count,
        compiler_params=params(1),
        cost_estimate=cost(3e9, 10e6),
        name="dh",
    )(*ss, wdown)


def crossed(parts, j, cap):
    return jnp.concatenate([part[j * cap : (j + 1) * cap, :] for part in parts], axis=0)


AHEAD = (2, 1, 3)
SPOTS = (((0, 0), (1, 1)), ((2, 0), (0, 1)), ((1, 0), (2, 1)))


def put_halves(k, part, sent_v, wait_v, outs, sems):
    half = part.shape[0] // 2
    copies = []
    for side in range(2):
        out, row = SPOTS[k][side]
        piece = part[side * half : (side + 1) * half]
        if out == 2:
            staged = wait_v.at[row]
            staged[...] = piece
        else:
            staged = sent_v.at[out, row]
            staged[...] = piece.astype(BF16)
        target = outs[out].at[row * half : (row + 1) * half, :]
        copies.append(begun(staged, target, sems.at[k, side]))
    return copies


def ahead_of(place_ref, ahead, size):
    start = lax.rem(place_ref[0] + ahead, SIDE) * size
    return pl.ds(pl.multiple_of(start, size), size)


def message_outs(rows, cols):
    return [jax.ShapeDtypeStruct((rows, cols), kind) for kind in (BF16, BF16, F32)]


def message_scratch(rows, cols):
    return [
        pltpu.VMEM((2, 2, rows // 2, cols), BF16),
        pltpu.VMEM((2, rows // 2, cols), F32),
        pltpu.SemaphoreType.DMA((3, 2)),
    ]


def down_kernel(cap, place_ref, *refs):
    hs, ss, outs, turned_out = refs[:4], refs[4:8], refs[8:11], refs[11]
    h_v, s_v, turned_v, sent_v, wait_v, out_sems, h_sems, s_sems, turned_sem = refs[12:]
    rows, width = ss[0].shape
    size = width // SIDE
    h_loads = [begun(hs[i], h_v.at[i], h_sems.at[i]) for i in range(SIDE)]
    s_loads = []
    for k, ahead in enumerate(AHEAD):
        cols = ahead_of(place_ref, ahead, size)
        for j in range(SIDE):
            part = s_v.at[k, pl.ds(j * rows, rows), :]
            s_loads.append(begun(ss[j].at[:, cols], part, s_sems.at[k, j]))
    for load in h_loads:
        load.wait()
    step = 256
    for t in range(turned_v.shape[0] // step):
        cols = slice(t * step, (t + 1) * step)
        parts = [h_v[i, :, cols] for i in range(SIDE)]
        whole = jnp.concatenate([crossed(parts, j, cap) for j in range(SIDE)], axis=0)
        turned_v[cols, :] = whole.T.astype(BF16)
    copies = [begun(turned_v, turned_out, turned_sem)]
    for k in range(3):
        for load in s_loads[4 * k : 4 * k + 4]:
            load.wait()
        copies += put_halves(k, dot(turned_v[...], s_v[k]), sent_v, wait_v, outs, out_sems)
    for copy in copies:
        copy.wait()


def down_parts(place, hs, ss, cap):
    rows, hidden = hs[0].shape
    quarter = ss[0].shape[1] // SIDE
    total = SIDE * rows
    *messages, turned_h = pl.pallas_call(
        functools.partial(down_kernel, cap),
        in_specs=[SCALARS] + [FAR] * 8,
        out_specs=[FAR] * 4,
        out_shape=message_outs(hidden, quarter) + [jax.ShapeDtypeStruct((hidden, total), BF16)],
        scratch_shapes=[
            pltpu.VMEM((SIDE, rows, hidden), F32),
            pltpu.VMEM((3, total, quarter), BF16),
            pltpu.VMEM((hidden, total), BF16),
        ]
        + message_scratch(hidden, quarter)
        + [
            pltpu.SemaphoreType.DMA((SIDE,)),
            pltpu.SemaphoreType.DMA((3, SIDE)),
            pltpu.SemaphoreType.DMA,
        ],
        compiler_params=params(0),
        cost_estimate=cost(1, 1),
        name="down_parts",
    )(place, *hs, *ss)
    return messages, turned_h


def down_own_kernel(place_ref, *refs):
    turned_ref, ss, out = refs[0], refs[1:5], refs[5]
    out[...] = dot(turned_ref[...], jnp.concatenate([s[...] for s in ss], axis=0))


def down_own(place, turned_h, ss):
    hidden, total = turned_h.shape
    rows, width = ss[0].shape
    quarter = width // SIDE
    return pl.pallas_call(
        down_own_kernel,
        grid_spec=pltpu.PrefetchScalarGridSpec(
            num_scalar_prefetch=1,
            grid=(2,),
            in_specs=[pl.BlockSpec((hidden // 2, total), lambda i, place: (i, 0))]
            + [held((rows, quarter), lambda i, place: (0, place[0]))] * 4,
            out_specs=pl.BlockSpec((hidden // 2, quarter), lambda i, place: (i, 0)),
        ),
        out_shape=jax.ShapeDtypeStruct((hidden, quarter), F32),
        compiler_params=params(1),
        cost_estimate=cost(1, 1),
        name="down_own",
    )(place, turned_h, *ss)


EARLY = tuple((i, j) for i in range(3) for j in range(3))
LATE = tuple((3, j) for j in range(3)) + tuple((i, 3) for i in range(4))


def early_kernel(cap, to_ref, *refs):
    dhs, cas, cbs, w, out, ds = refs[:3], refs[3:6], refs[6:9], refs[9], refs[10], refs[11:13]
    dh_v, f_v, d_v, e_v, w_v, rows_v, dh_sems, f_sems, w_sems, d_sems, out_sems = refs[13:]
    rows, hidden = dhs[0].shape
    loads = []
    for i in range(3):
        loads.append(begun(dhs[i], dh_v.at[i], dh_sems.at[i]))
        loads.append(begun(cas[i], f_v.at[0, i], f_sems.at[0, i]))
        loads.append(begun(cbs[i], f_v.at[1, i], f_sems.at[1, i]))
    steps, step = w_v.shape[0], w_v.shape[1]
    cols = [pl.ds(t * step, step) for t in range(steps)]
    w_loads = [begun(w.at[cols[t], :], w_v.at[t], w_sems.at[t]) for t in range(steps)]
    for load in loads:
        load.wait()
    copies = []
    for k in range(2):
        for t in range(hidden // 256):
            part = slice(t * 256, (t + 1) * 256)
            chunks = [dh_v[j, :, part] for j in range(3)]
            kept = []
            for i in range(3):
                factor = f_v[k, i, :, part].astype(F32)[: 3 * cap]
                product = crossed(chunks, i, cap) * factor
                kept.append(product)
                whole = jnp.concatenate([product, jnp.zeros((cap, 256), F32)], axis=0)
                d_v[k, i * rows : (i + 1) * rows, part] = whole.astype(BF16)
            e_v[k, :, part] = jnp.concatenate(kept, axis=0).astype(BF16)
        target = ds[k].at[pl.ds(0, 3 * rows), :]
        copies.append(begun(d_v.at[k], target, d_sems.at[k]))
    for t in range(steps):
        w_loads[t].wait()
        part = dot(e_v[0], w_v[t, :, :hidden], 1, 1) + dot(e_v[1], w_v[t, :, hidden:], 1, 1)
        for n, (i, j) in enumerate(EARLY):
            block = part[n * cap : (n + 1) * cap].astype(BF16)
            rows_v[t, n] = block
            target = out.at[to_ref[i * SIDE + j], :, cols[t]]
            copies.append(begun(rows_v.at[t, n], target, out_sems.at[t, n]))
    for copy in copies:
        copy.wait()


def early_rows(to, dhs, cas, cbs, wgu, cap):
    rows, hidden = dhs[0].shape
    width = wgu.shape[0]
    step = 512
    steps = width // step
    early = len(EARLY)
    out = jax.ShapeDtypeStruct((SIDE * rows, hidden), BF16)
    slots, da, db = pl.pallas_call(
        functools.partial(early_kernel, cap),
        in_specs=[SCALARS] + [FAR] * 10,
        out_specs=[FAR] * 3,
        out_shape=[jax.ShapeDtypeStruct((SIDE * SIDE, cap, width), BF16), out, out],
        scratch_shapes=[
            pltpu.VMEM((3, rows, hidden), F32),
            pltpu.VMEM((2, 3, rows, hidden), BF16),
            pltpu.VMEM((2, 3 * rows, hidden), BF16),
            pltpu.VMEM((2, early * cap, hidden), BF16),
            pltpu.VMEM((steps, step, 2 * hidden), BF16),
            pltpu.VMEM((steps, early, cap, step), BF16),
            pltpu.SemaphoreType.DMA((3,)),
            pltpu.SemaphoreType.DMA((2, 3)),
            pltpu.SemaphoreType.DMA((steps,)),
            pltpu.SemaphoreType.DMA((2,)),
            pltpu.SemaphoreType.DMA((steps, early)),
        ],
        compiler_params=params(0),
        cost_estimate=cost(3e9, 10e6),
        name="early_rows",
    )(to, *dhs, *cas, *cbs, wgu)
    return slots, [da, db]


def late_kernel(cap, to_ref, s, wd, *refs):
    dhs, cas, cbs, w, _, out, ds = refs[:3], refs[3:7], refs[7:11], refs[11], refs[12], refs[13], refs[14:16]
    s_v, wd_v, dh_v, f_v, d_v, w_v, rows_v = refs[16:23]
    s_sem, wd_sems, dh_sems, f_sems, w_sems, d_sems, out_sems = refs[23:]
    rows = s.shape[0]
    hidden = wd.shape[0]
    step = 256
    s_load = begun(s, s_v, s_sem)
    wd_loads, f_loads = [], []
    for t in range(hidden // step):
        cols = pl.ds(t * step, step)
        wd_loads.append(begun(wd.at[cols, :], wd_v.at[cols, :], wd_sems.at[t]))
    for j in range(3):
        f_loads.append(begun(dhs[j], dh_v.at[j], dh_sems.at[j]))
    for i in range(SIDE):
        f_loads.append(begun(cas[i], f_v.at[0, i], f_sems.at[0, i]))
        f_loads.append(begun(cbs[i], f_v.at[1, i], f_sems.at[1, i]))
    steps, part_width = w_v.shape[0], w_v.shape[1]
    parts = [pl.ds(t * part_width, part_width) for t in range(steps)]
    w_loads = [begun(w.at[parts[t], :], w_v.at[t], w_sems.at[t]) for t in range(steps)]
    s_load.wait()
    for t in range(hidden // step):
        cols = slice(t * step, (t + 1) * step)
        wd_loads[t].wait()
        last = dot(s_v[...], wd_v[cols, :], 1, 1)
        if t == 0:
            for load in f_loads:
                load.wait()
        chunks = [dh_v[j, 3 * cap :, cols] for j in range(3)] + [last]
        dh = jnp.concatenate(chunks, axis=0)
        for k in range(2):
            factors = [f_v[k, 3, :, cols].astype(F32)[: 3 * cap]]
            factors += [f_v[k, i, :, cols].astype(F32)[3 * cap :] for i in range(SIDE)]
            d_v[k, :, cols] = (dh * jnp.concatenate(factors, axis=0)).astype(BF16)
    copies = [begun(d_v.at[k], ds[k], d_sems.at[k]) for k in range(2)]
    for t in range(steps):
        w_loads[t].wait()
        part = dot(d_v[0], w_v[t, :, :hidden], 1, 1) + dot(d_v[1], w_v[t, :, hidden:], 1, 1)
        for n, (i, j) in enumerate(LATE):
            rows_v[t, n] = part[n * cap : (n + 1) * cap].astype(BF16)
            target = out.at[to_ref[i * SIDE + j], :, parts[t]]
            copies.append(begun(rows_v.at[t, n], target, out_sems.at[t, n]))
    for copy in copies:
        copy.wait()


def late_rows(to, s, wdown, dhs, cas, cbs, wgu, slots, cap):
    rows, width = s.shape
    hidden = wdown.shape[0]
    step = 512
    steps = width // step
    late = len(LATE)
    out = jax.ShapeDtypeStruct((late * cap, hidden), BF16)
    slots, da, db = pl.pallas_call(
        functools.partial(late_kernel, cap),
        in_specs=[SCALARS] + [FAR] * 15,
        out_specs=[FAR] * 3,
        out_shape=[jax.ShapeDtypeStruct(slots.shape, BF16), out, out],
        input_output_aliases={15: 0},
        scratch_shapes=[
            pltpu.VMEM((rows, width), BF16),
            pltpu.VMEM((hidden, width), BF16),
            pltpu.VMEM((3, rows, hidden), F32),
            pltpu.VMEM((2, SIDE, rows, hidden), BF16),
            pltpu.VMEM((2, late * cap, hidden), BF16),
            pltpu.VMEM((steps, step, 2 * hidden), BF16),
            pltpu.VMEM((steps, late, cap, step), BF16),
            pltpu.SemaphoreType.DMA,
            pltpu.SemaphoreType.DMA((hidden // 256,)),
            pltpu.SemaphoreType.DMA((3,)),
            pltpu.SemaphoreType.DMA((2, SIDE)),
            pltpu.SemaphoreType.DMA((steps,)),
            pltpu.SemaphoreType.DMA((2,)),
            pltpu.SemaphoreType.DMA((steps, late)),
        ],
        compiler_params=params(0),
        cost_estimate=cost(1, 1),
        name="late_rows",
    )(to, s, wdown, *dhs, *cas, *cbs, wgu, slots)
    return slots, [da, db]


def gate_up_kernel(cap, place_ref, *refs):
    early, late, xs, outs, ds = refs[:2], refs[2:4], refs[4:8], refs[8:11], refs[11:13]
    d_v, late_v, x_v, sent_v, wait_v, out_sems, d_sems, x_sems = refs[13:]
    rows, width = xs[0].shape
    size = width // SIDE
    loads = []
    for k in range(2):
        part = pl.ds(0, 3 * rows)
        loads.append(begun(early[k].at[part, :], d_v.at[k, part, :], d_sems.at[0, k]))
        loads.append(begun(late[k], late_v.at[k], d_sems.at[1, k]))
    for k, ahead in enumerate(AHEAD):
        cols = ahead_of(place_ref, ahead, size)
        for i in range(SIDE):
            part = x_v.at[k, pl.ds(i * rows, rows), :]
            loads.append(begun(xs[i].at[:, cols], part, x_sems.at[k, i]))
    for load in loads[:4]:
        load.wait()
    edge = 3 * cap - 8
    copies = []
    for k in range(2):
        fresh = late_v[k].astype(F32)
        for i in range(3):
            at = slice(i * rows + edge, (i + 1) * rows)
            old = d_v[k, at, :].astype(F32)[:8]
            new = fresh[(3 + i) * cap : (4 + i) * cap]
            d_v[k, at, :] = jnp.concatenate([old, new], axis=0).astype(BF16)
        new = jnp.concatenate([fresh[: 3 * cap], fresh[6 * cap :]], axis=0)
        d_v[k, 3 * rows :, :] = new.astype(BF16)
        copies.append(begun(d_v.at[k], ds[k], d_sems.at[2, k]))
    for k in range(3):
        for load in loads[4 * k + 4 : 4 * k + 8]:
            load.wait()
        turned_x = x_v[k].T
        part = jnp.concatenate([dot(turned_x, d_v[0]), dot(turned_x, d_v[1])], axis=1)
        copies += put_halves(k, part, sent_v, wait_v, outs, out_sems)
    for copy in copies:
        copy.wait()


def gate_up_parts(place, early, late, xs, cap):
    rows, width = xs[0].shape
    total, hidden = early[0].shape
    quarter = width // SIDE
    out = jax.ShapeDtypeStruct((total, hidden), BF16)
    *messages, da, db = pl.pallas_call(
        functools.partial(gate_up_kernel, cap),
        in_specs=[SCALARS] + [FAR] * 8,
        out_specs=[FAR] * 5,
        out_shape=message_outs(quarter, 2 * hidden) + [out, out],
        scratch_shapes=[
            pltpu.VMEM((2, total, hidden), BF16),
            pltpu.VMEM((2, *late[0].shape), BF16),
            pltpu.VMEM((3, total, quarter), BF16),
        ]
        + message_scratch(quarter, 2 * hidden)
        + [pltpu.SemaphoreType.DMA((3, 2)), pltpu.SemaphoreType.DMA((3, SIDE))],
        compiler_params=params(0),
        cost_estimate=cost(1, 1),
        name="gate_up_parts",
    )(place, *early, *late, *xs)
    return messages, [da, db]


def gate_up_own_kernel(place_ref, *refs):
    xs, ds, out = refs[:4], refs[4:6], refs[6]
    rows = jnp.concatenate([x[...] for x in xs], axis=0).T
    out[...] = jnp.concatenate([dot(rows, d[...]) for d in ds], axis=1)


def gate_up_own(place, xs, ds):
    rows, width = xs[0].shape
    total, hidden = ds[0].shape
    half = width // SIDE // 2
    return pl.pallas_call(
        gate_up_own_kernel,
        grid_spec=pltpu.PrefetchScalarGridSpec(
            num_scalar_prefetch=1,
            grid=(2,),
            in_specs=[pl.BlockSpec((rows, half), lambda i, place: (0, 2 * place[0] + i))] * 4
            + [held((total, hidden), lambda i, place: (0, 0))] * 2,
            out_specs=pl.BlockSpec((half, 2 * hidden), lambda i, place: (i, 0)),
        ),
        out_shape=jax.ShapeDtypeStruct((2 * half, 2 * hidden), F32),
        compiler_params=params(1),
        cost_estimate=cost(200e9, 10e6),
        name="gate_up_own",
    )(place, *xs, *ds)


def around(first, axis):
    return [first] + [moved_along(first, axis, OFF[b]) for b in range(1, SIDE)]


def spread(outs, axis, work):
    near = [moved_along(outs[j], axis, OFF[j]) for j in (1, 2)]
    done = work(outs[0])
    far, near[0], near[1], *done = lax.optimization_barrier((outs[3], *near, *done))
    return [outs[0], *near, moved_along(far, axis, OFF[3])], done


def ring_first(first_up, first_down, wait):
    return moved_along(first_up, "edata", 1), moved_along(first_down, "edata", -1)


def ring_second(up1, down1, first_up, first_down, wait):
    half = wait.shape[0] // 2
    second_up = (wait[:half] + up1[:half].astype(F32)).astype(BF16)
    second_down = (wait[half:] + down1[half:].astype(F32)).astype(BF16)
    return moved_along(second_up, "edata", 1), moved_along(second_down, "edata", -1)


def ring_last(own, up1, down1, up2, down2):
    half = own.shape[0] // 2
    upper = own[:half] + down1[:half].astype(F32) + up2.astype(F32)
    lower = own[half:] + up1[half:].astype(F32) + down2.astype(F32)
    return jnp.concatenate([upper, lower], axis=0).astype(BF16)


def body(hidden_in, out_grad, routes, gates, w_gate_up, w_down):
    tok = hidden_in.shape[1]
    width = hidden_in.shape[2]
    topk = routes.shape[2]
    experts = lax.axis_size("expert")
    cap = min(tok, tok * topk * 9 // (8 * experts))
    wgu, wdown = w_gate_up[0, 0], w_down[0, 0]
    me = lax.axis_index("expert")
    mx, mz = me // SIDE, me % SIDE
    off = jnp.array(OFF, jnp.int32)
    eids_x = (mx * SIDE + (mz + off) % SIDE).astype(jnp.int32)
    eids_g = ((mx + off) % SIDE * SIDE + mz).astype(jnp.int32)
    to = ((mx - off)[None, :] % SIDE * SIDE + (mz - off)[:, None] % SIDE).reshape(-1)
    place = lax.axis_index("edata").astype(jnp.int32).reshape(1)

    xe, ge, tail = prep(routes[0].T, gates[0].T, hidden_in[0], out_grad[0], experts)
    xblocks = around(xe, "x")
    gblocks = around(ge, "z")
    xpacked = list(pack(eids_x, xblocks, width, experts, cap, False))
    xpacked[0], gblocks[0] = lax.optimization_barrier((xpacked[0], gblocks[0]))
    gpacked = pack(eids_g, gblocks, width, experts, cap, True)
    xs, first_up = spread(xpacked, "z", lambda rows: up([rows], wgu)[0])
    ss, first_dh = spread(gpacked, "x", lambda rows: dh_of([rows], wdown))
    to = to.astype(jnp.int32)
    ups = [first_up] + up(xs[1:3], wgu)
    dhs = [*first_dh, *dh_of(ss[1:3], wdown)]
    cas, cbs = ([u[k] for u in ups] for k in (1, 2))
    slots, early = early_rows(to, dhs, cas, cbs, wgu, cap)
    ups += up(xs[3:], wgu)
    hs, cas, cbs = ([u[k] for u in ups] for k in range(3))
    last, slots, hs[3], *dhs = lax.optimization_barrier((ss[3], slots, hs[3], *dhs))
    ss = ss[:3] + [last]
    down, turned_h = down_parts(place, hs, ss, cap)
    last, *down = lax.optimization_barrier((last, *down))
    down_first = ring_first(*down)
    rows, late = late_rows(to, last, wdown, dhs, cas, cbs, wgu, slots, cap)
    returned = lax.all_to_all(rows, "expert", split_axis=0, concat_axis=0, tiled=True)
    rows, *later = lax.optimization_barrier((rows, *late, *down_first))
    late, down_first = later[:2], later[2:]
    gate_up, ds = gate_up_parts(place, early, late, xs, cap)
    gate_up_first = ring_first(*gate_up)
    wait, da, db, turned_h = lax.optimization_barrier((gate_up[2], *ds, turned_h))
    gate_up = [*gate_up[:2], wait]
    own_down = down_own(place, turned_h, ss)
    own_gate_up = gate_up_own(place, xs, [da, db])
    own_down, own_gate_up, *gate_up_first = lax.optimization_barrier(
        (own_down, own_gate_up, *gate_up_first)
    )
    down_second = ring_second(*down_first, *down)
    gate_up_second = ring_second(*gate_up_first, *gate_up)
    down_grad = ring_last(own_down, *down_first, *down_second)
    gate_up_grad = ring_last(own_gate_up, *gate_up_first, *gate_up_second)

    layer = home(tail, returned.reshape(experts * cap, width), out_grad[0], experts, cap)
    upstream = moved_along(layer, "section", -1)
    return (upstream[None], gate_up_grad[None, None], down_grad[None, None])


def solution(mesh):
    return jax.shard_map(
        body,
        mesh=mesh,
        in_specs=(
            P("section", ("edata", "expert"), None),
            P("section", ("edata", "expert"), None),
            P("section", ("edata", "expert"), None),
            P("section", ("edata", "expert"), None),
            P("section", "expert", None, None),
            P("section", "expert", None, None),
        ),
        out_specs=(
            P("section", ("edata", "expert"), None),
            P("section", "expert", "edata", None),
            P("section", "expert", None, "edata"),
        ),
        check_vma=False,
    )
```

time: 240 us -> 224 us (0.933)
  Pallas kernels: 61 us -> 107 us
  waiting for transfers between devices: 93.1 us -> 56.5 us
  local copies, waits for them, and re-layouts: 36.7 us -> 6.23 us
  starting transfers between devices: 38.9 us -> 42 us
  other arithmetic: 7.69 us -> 10.4 us
    unnamed x129 -> x39, local copies, waits for them, and re-layouts: 36.7 us -> 5.61 us
    pallas_call x9 -> x8, Pallas kernels: 42.8 us -> 68.9 us  [the longest x1 16.5 us: late_rows(): pl.pallas_call(functools.partial(late_kernel, cap), in_specs=[SCALARS] +...]
    ppermute x9, waiting for transfers between devices: 50.5 us -> 28.6 us  [moved_along(): lax.ppermute(block, axis, [(i, (i + distance) % size) for i in range(size)])]
    ppermute x12, waiting for transfers between devices: 42.5 us -> 27.2 us  [moved_along(): return lax.ppermute(block, 'expert', pairs)]
    pallas_call x2 -> x3, Pallas kernels: 10.2 us -> 20.4 us  [up(): pl.pallas_call(functools.partial(up_kernel, count), grid=(steps,), in_spe...]
    pallas_call x1 -> x2, Pallas kernels: 3.52 us -> 10.6 us  [dh_of(): pl.pallas_call(functools.partial(dh_kernel, count), grid=(hidden // step,...]
    ppermute x12, starting transfers between devices: 21.2 us -> 24 us  [moved_along(): return lax.ppermute(block, 'expert', pairs)]
  transfers between devices with their start and end apart: 22 -> 22, of which waited for: 9 -> 8; matrix products, arithmetic and copies ran while one was open for 3% -> 5% of each run, Pallas kernels for 18% -> 43%
where the time goes in v3:
time: 224 us; the launch traced here: 223 us
  Pallas kernels  107 us (48%)
  waiting for transfers between devices  56.5 us (25%)
  starting transfers between devices  42 us (19%)
  other arithmetic  10.4 us (5%)
  local copies, waits for them, and re-layouts  6.23 us (3%)
    ppermute x9, waiting for transfers between devices, moved_along(): lax.ppermute(block, axis, [(i, (i + distance) % size) for i in range(size)])  28.6 us
    ppermute x12, waiting for transfers between devices, moved_along(): return lax.ppermute(block, 'expert', pairs)  27.2 us
    ppermute x12, starting transfers between devices, moved_along(): return lax.ppermute(block, 'expert', pairs)  24 us
    pallas_call x3, Pallas kernels, up(): pl.pallas_call(functools.partial(up_kernel, count), grid=(steps,), in_spe...  20.4 us
    pallas_call x1, Pallas kernels, late_rows(): pl.pallas_call(functools.partial(late_kernel, cap), in_specs=[SCALARS] +...  16.5 us
    ppermute x9, starting transfers between devices, moved_along(): lax.ppermute(block, axis, [(i, (i + distance) % size) for i in range(size)])  13.2 us
    pallas_call x1, Pallas kernels, gate_up_parts(): pl.pallas_call(functools.partial(gate_up_kernel, cap), in_specs=[SCALARS]...  11.6 us
    pallas_call x2, Pallas kernels, pack(): pl.pallas_call(functools.partial(pack_kernel, scale, experts, cap), in_sp...  11.5 us
  transfers between devices with their start and end apart: 22, of which 8 were waited for; matrix products, arithmetic and copies ran while one was open for 5% of the time, Pallas kernels for 43%

profile of v3, /device:TPU:0, one launch (start us, length us, event | category | flops | bytes accessed | tf_op | source)
XLA Modules:
  0.0 223.3 jit_solution(16568086244426331108)
XLA Ops:
  0.6 2.4 %prep.1 = (bf16[128,2176]{1,0:T(8,128)(2,1)}, bf16[128,2176]{1,0:T(8,128)(2,1)}, bf16[128,128]{1,0:T(8,128)(2,1)}) custom-call(s32[8,128]{1,0:T(8,128)} %bitcast.36, f32[8,128]{1,0:T(8,128)} %bitcast.37, bf16[128,2048]{1,0:T(8,128)(2,1)} %bitcast.32, bf16[128,2048]{1,0:T(8,128)(2,1)} %bitcast.33), custom_call_target="tpu_custom_call" | custom-call | tf_op jit(solution)/shard_map/prep/pallas_call | solution.py:88
  3.0 3.1 %collective-permute-start.2 = (bf16[128,2176]{1,0:T(8,128)(2,1)}, bf16[128,2176]{1,0:T(8,128)(2,1)S(1)}, u32[]{:S(2)}, u32[]{:S(2)}) collective-permute-start(bf16[128,2176]{1,0:T(8,128)(2,1)} %get-tuple-element.78.refs_0_), channel_id=1, source_target_pairs={{0,8},{1,9},{2,10},{3,11},{4,12},{5,13},{6,14},{7,15},{8,0},{9,1},... | collective-permute-start | bytes 1671176 | tf_op jit(solution)/shard_map/ppermute | solution.py:53
  8.1 3.9 %collective-permute-start.5 = (bf16[128,2176]{1,0:T(8,128)(2,1)}, bf16[128,2176]{1,0:T(8,128)(2,1)S(1)}, u32[]{:S(2)}, u32[]{:S(2)}) collective-permute-start(bf16[128,2176]{1,0:T(8,128)(2,1)} %get-tuple-element.81.refs_0_), channel_id=1, source_target_pairs={{0,2},{1,3},{2,0},{3,1},{4,6},{5,7},{6,4},{7,5},{8,10},{9,11},{10,... | collective-permute-start | bytes 1671176 | tf_op jit(solution)/shard_map/ppermute | solution.py:53
  12.7 7.6 %collective-permute-done.2.refs_3_ = bf16[128,2176]{1,0:T(8,128)(2,1)S(1)} collective-permute-done((bf16[128,2176]{1,0:T(8,128)(2,1)}, bf16[128,2176]{1,0:T(8,128)(2,1)S(1)}, u32[]{:S(2)}, u32[]{:S(2)}) %collective-permute-start.2) | collective-permute-done | bytes 557088 | tf_op jit(solution)/shard_map/ppermute | solution.py:53
  20.3 2.0 collective-permute-start.3
  23.5 7.7 %collective-permute-done.1.refs_2_ = bf16[128,2176]{1,0:T(8,128)(2,1)S(1)} collective-permute-done((bf16[128,2176]{1,0:T(8,128)(2,1)}, bf16[128,2176]{1,0:T(8,128)(2,1)S(1)}, u32[]{:S(2)}, u32[]{:S(2)}) %collective-permute-start.1) | collective-permute-done | bytes 557088 | tf_op jit(solution)/shard_map/ppermute | solution.py:53
  32.2 5.5 %pack_rows.1 = (bf16[288,2048]{1,0:T(8,128)(2,1)}, bf16[288,2048]{1,0:T(8,128)(2,1)}, bf16[288,2048]{1,0:T(8,128)(2,1)}, bf16[288,2048]{1,0:T(8,128)(2,1)}) custom-call(s32[4]{0:T(128)} %get-tuple-element.159.eids_ref, bf16[128,2176]{1,0:T(8,128)(2,1)} %get-tuple-element.78.refs_0_, bf16[128,2176]{1,0:T(8,128)(2,1)} %copy-done.18, ...), custom_call_target="tpu_custom_call" | custom-call | flops 3000000000 | bytes 10000000 | tf_op jit(solution)/shard_map/pack_rows/pallas_call | solution.py:161
  37.7 2.0 collective-permute-start.9
  39.7 2.2 collective-permute-start.10
  42.9 6.0 %pack_scaled.1 = (bf16[288,2048]{1,0:T(8,128)(2,1)}, bf16[288,2048]{1,0:T(8,128)(2,1)}, bf16[288,2048]{1,0:T(8,128)(2,1)}, bf16[288,2048]{1,0:T(8,128)(2,1)}) custom-call(s32[4]{0:T(128)} %get-tuple-element.160.eids_ref, bf16[128,2176]{1,0:T(8,128)(2,1)} %get-tuple-element.81.refs_0_, bf16[128,2176]{1,0:T(8,128)(2,1)} %collective-permute-done.3.refs_1_, ...), custom_call_target="tpu_custom_call" | custom-call | flops 3000000000 | bytes 10000000 | tf_op jit(solution)/shard_map/pack_scaled/pallas_call | solution.py:161
  52.2 6.3 %up.3 = (f32[288,768]{1,0:T(8,128)}, bf16[288,768]{1,0:T(8,128)(2,1)}, bf16[288,768]{1,0:T(8,128)(2,1)}) custom-call(bf16[288,2048]{1,0:T(8,128)(2,1)} %get-tuple-element.95.refs_0_.refs_4_, bf16[2048,1536]{1,0:T(8,128)(2,1)} %bitcast.21, bf16[2048,1536]{1,0:T(8,128)(2,1)} %bitcast.22), custom_call_target="tpu_custom_call" | custom-call | flops 3000000000 | bytes 10000000 | tf_op jit(solution)/shard_map/up/pallas_call | solution.py:234
  58.5 9.4 %collective-permute-done.9.refs_0_.refs_5_.refs_1_ = bf16[288,2048]{1,0:T(8,128)(2,1)S(1)} collective-permute-done((bf16[288,2048]{1,0:T(8,128)(2,1)}, bf16[288,2048]{1,0:T(8,128)(2,1)S(1)}, u32[]{:S(2)}, u32[]{:S(2)}) %collective-permute-start.9) | collective-permute-done | bytes 1179680 | tf_op jit(solution)/shard_map/ppermute | solution.py:53
  67.9 2.9 %collective-permute-start.11 = (bf16[288,2048]{1,0:T(8,128)(2,1)}, bf16[288,2048]{1,0:T(8,128)(2,1)}, u32[]{:S(2)}, u32[]{:S(2)}) collective-permute-start(bf16[288,2048]{1,0:T(8,128)(2,1)} %get-tuple-element.108), channel_id=1, source_target_pairs={{0,2},{1,3},{2,0},{3,1},{4,6},{5,7},{6,4},{7,5},{8,10},{9,11},{10,... | collective-permute-start | bytes 3538952 | tf_op jit(solution)/shard_map/ppermute | solution.py:53
  70.8 4.7 %dh.2.refs_0_ = f32[288,768]{1,0:T(8,128)} custom-call(bf16[288,2048]{1,0:T(8,128)(2,1)} %get-tuple-element.85.refs_0_.refs_4_.refs_1_, bf16[768,2048]{1,0:T(8,128)(2,1)} %bitcast.29), custom_call_target="tpu_custom_call" | custom-call | flops 3000000000 | bytes 10000000 | tf_op jit(solution)/shard_map/dh/pallas_call | solution.py:262
  75.5 2.2 collective-permute-done.6.refs_0_.refs_5_.refs_2_
  82.4 5.9 %dh.3 = (f32[288,768]{1,0:T(8,128)}, f32[288,768]{1,0:T(8,128)}) custom-call(bf16[288,2048]{1,0:T(8,128)(2,1)} %copy-done.4, bf16[288,2048]{1,0:T(8,128)(2,1)} %copy-done.5, bf16[768,2048]{1,0:T(8,128)(2,1)} %bitcast.30), custom_call_target="tpu_custom_call" | custom-call | flops 3000000000 | bytes 10000000 | tf_op jit(solution)/shard_map/dh/pallas_call | solution.py:262
  88.3 7.8 %up.4 = (f32[288,768]{1,0:T(8,128)}, bf16[288,768]{1,0:T(8,128)(2,1)}, bf16[288,768]{1,0:T(8,128)(2,1)}, f32[288,768]{1,0:T(8,128)}, bf16[288,768]{1,0:T(8,128)(2,1)}, /*index=5*/bf16[288,768]{1,0:T(8,128)(2,1)}) custom-call(bf16[288,2048]{1,0:T(8,128)(2,1)} %copy-done.2, bf16[288,2048]{1,0:T(8,128)(2,1)} %copy-done.3, bf16[2048,1536]{1,0:T(8,128)(2,1)} %bitcast.23, ...), custom_call_target="tpu_custom_call" | custom-call | flops 3000000000 | bytes 10000000 | tf_op jit(solution)/shard_map/up/pallas_call | solution.py:234
  96.1 11.1 %early_rows.1 = (bf16[16,72,2048]{2,1,0:T(8,128)(2,1)}, bf16[1152,768]{1,0:T(8,128)(2,1)}, bf16[1152,768]{1,0:T(8,128)(2,1)}) custom-call(s32[16]{0:T(128)} %add.106.to_ref, f32[288,768]{1,0:T(8,128)} %dh.2.refs_0_, f32[288,768]{1,0:T(8,128)} %get-tuple-element.120.refs_1_, f32[288,768]{1,0:T(8,128)} %get-tuple-element.121.refs_2_, ...), custom_call_target="tpu_custom_call" | custom-call | flops 3000000000 | bytes 10000000 | tf_op jit(solution)/shard_map/early_rows/pallas_call | solution.py:450
  107.2 6.3 %up.5 = (f32[288,768]{1,0:T(8,128)}, bf16[288,768]{1,0:T(8,128)(2,1)}, bf16[288,768]{1,0:T(8,128)(2,1)}) custom-call(bf16[288,2048]{1,0:T(8,128)(2,1)} %collective-permute-done.11.refs_0_.refs_7_.refs_3_, bf16[2048,1536]{1,0:T(8,128)(2,1)} %bitcast.26, bf16[2048,1536]{1,0:T(8,128)(2,1)} %bitcast.27), custom_call_target="tpu_custom_call" | custom-call | flops 3000000000 | bytes 10000000 | tf_op jit(solution)/shard_map/up/pallas_call | solution.py:234
  114.6 8.2 %down_parts.1 = (bf16[768,512]{1,0:T(8,128)(2,1)}, bf16[768,512]{1,0:T(8,128)(2,1)}, f32[768,512]{1,0:T(8,128)}, bf16[768,1152]{1,0:T(8,128)(2,1)}) custom-call(s32[1]{0:T(128)} %bitcast.8.place_ref, f32[288,768]{1,0:T(8,128)} %get-tuple-element.111.refs_0_, f32[288,768]{1,0:T(8,128)} %get-tuple-element.112.refs_1_, f32[288,768]{1,0:T(8,128)} %get-tuple-element.113.refs_2_, ...), custom_call_target="tpu_custom_call" | custom-call | flops 1 | bytes 1 | tf_op jit(solution)/shard_map/down_parts/pallas_call | solution.py:350
  126.1 16.5 %late_rows.1 = (bf16[16,72,2048]{2,1,0:T(8,128)(2,1)}, bf16[504,768]{1,0:T(8,128)(2,1)}, bf16[504,768]{1,0:T(8,128)(2,1)}) custom-call(s32[16]{0:T(128)} %add.106.to_ref, bf16[288,2048]{1,0:T(8,128)(2,1)} %copy-done, bf16[768,2048]{1,0:T(8,128)(2,1)} %bitcast.31, f32[288,768]{1,0:T(8,128)} %dh.2.refs_0_, ...), custom_call_target="tpu_custom_call", output_to_operand_aliasing={{0}: (15, {})} | custom-call | flops 1 | bytes 1 | tf_op jit(solution)/shard_map/late_rows/pallas_call | solution.py:528
  142.7 4.7 %all-to-all-start = ((bf16[16,72,2048]{2,1,0:T(8,128)(2,1)}), bf16[16,72,2048]{2,1,0:T(8,128)(2,1)}, u32[]{:S(2)}, u32[]{:S(2)}) async-start(bf16[16,72,2048]{2,1,0:T(8,128)(2,1)} %get-tuple-element.125), calls=%async_computation | async-start | bytes 9437184 | tf_op jit(solution)/shard_map/all_to_all | solution.py:711
  149.1 3.0 %collective-permute-start.20 = (bf16[384,512]{1,0:T(8,128)(2,1)}, bf16[384,512]{1,0:T(8,128)(2,1)}, u32[]{:S(2)}, u32[]{:S(2)}) collective-permute-start(bf16[384,512]{1,0:T(8,128)(2,1)} %get-tuple-element.158), channel_id=1, source_target_pairs={{0,48},{16,0},{32,16},{48,32},{1,49},{17,1},{33,17},{49,33},{2,50}... | collective-permute-start | bytes 1179656 | tf_op jit(solution)/shard_map/ppermute | solution.py:45
  152.1 11.6 %gate_up_parts.1 = (bf16[512,1536]{1,0:T(8,128)(2,1)}, bf16[512,1536]{1,0:T(8,128)(2,1)}, f32[512,1536]{1,0:T(8,128)}, bf16[1152,768]{1,0:T(8,128)(2,1)}, bf16[1152,768]{1,0:T(8,128)(2,1)}) custom-call(s32[1]{0:T(128)} %bitcast.8.place_ref, bf16[1152,768]{1,0:T(8,128)(2,1)} %get-tuple-element.126.refs_0_, bf16[1152,768]{1,0:T(8,128)(2,1)} %get-tuple-element.127.refs_1_, ...), custom_call_target="tpu_custom_call" | custom-call | flops 1 | bytes 1 | tf_op jit(solution)/shard_map/gate_up_parts/pallas_call | solution.py:601
  163.7 3.2 %collective-permute-start.16 = (bf16[512,1536]{1,0:T(8,128)(2,1)}, bf16[512,1536]{1,0:T(8,128)(2,1)}, u32[]{:S(2)}, u32[]{:S(2)}) collective-permute-start(bf16[512,1536]{1,0:T(8,128)(2,1)} %get-tuple-element.142), channel_id=1, source_target_pairs={{0,48},{16,0},{32,16},{48,32},{1,49},{17,1},{33,17},{49,33},{2,50}... | collective-permute-start | bytes 4718600 | tf_op jit(solution)/shard_map/ppermute | solution.py:45
  167.0 6.1 %gate_up_own.1 = f32[512,1536]{1,0:T(8,128)} custom-call(s32[1]{0:T(128)} %bitcast.8.place_ref, bf16[288,2048]{1,0:T(8,128)(2,1)} %get-tuple-element.95.refs_0_.refs_4_, bf16[288,2048]{1,0:T(8,128)(2,1)} %copy-done.2, bf16[288,2048]{1,0:T(8,128)(2,1)} %copy-done.3, bf16[288,2048]{1,0:T(8,128)(2,1)} %collective-permute-done.11.refs_0_.refs_7_.refs_3_, ...), custom_call_target="tpu_custom_call" | custom-call | flops 199999995904 | bytes 10000000 | tf_op jit(solution)/shard_map/gate_up_own/pallas_call | solution.py:630
  173.1 3.9 %down_own.1 = f32[768,512]{1,0:T(8,128)} custom-call(s32[1]{0:T(128)} %bitcast.8.place_ref, bf16[768,1152]{1,0:T(8,128)(2,1)} %get-tuple-element.138.refs_0_, bf16[288,2048]{1,0:T(8,128)(2,1)} %get-tuple-element.85.refs_0_.refs_4_.refs_1_, bf16[288,2048]{1,0:T(8,128)(2,1)} %copy-done.4, bf16[288,2048]{1,0:T(8,128)(2,1)} %copy-done.5, bf16[288,2048]{1,0:T(8,128)(2,1)} %copy-done), custom_call_target="tpu_custom_call" | custom-call | flops 1 | bytes 1 | tf_op jit(solution)/shard_map/down_own/pallas_call | solution.py:382
  177.0 22.5 %collective-permute-done.15 = bf16[512,1536]{1,0:T(8,128)(2,1)} collective-permute-done((bf16[512,1536]{1,0:T(8,128)(2,1)}, bf16[512,1536]{1,0:T(8,128)(2,1)}, u32[]{:S(2)}, u32[]{:S(2)}) %collective-permute-start.15) | collective-permute-done | bytes 1572896 | tf_op jit(solution)/shard_map/ppermute | solution.py:45
  201.4 3.2 %collective-permute-start.18 = (bf16[256,1536]{1,0:T(8,128)(2,1)S(1)}, bf16[256,1536]{1,0:T(8,128)(2,1)}, u32[]{:S(2)}, u32[]{:S(2)}) collective-permute-start(bf16[256,1536]{1,0:T(8,128)(2,1)S(1)} %get-tuple-element.154), channel_id=1, source_target_pairs={{0,48},{16,0},{32,16},{48,32},{1,49},{17,1},{33,17},{49,33},{2,50}... | collective-permute-start | bytes 2359304 | tf_op jit(solution)/shard_map/ppermute | solution.py:45
  207.8 5.2 %home.1 = bf16[128,2048]{1,0:T(8,128)(2,1)} custom-call(bf16[128,128]{1,0:T(8,128)(2,1)} %get-tuple-element.77.tail_ref, bf16[1152,2048]{1,0:T(8,128)(2,1)} %bitcast.9.rows_ref, bf16[128,2048]{1,0:T(8,128)(2,1)} %bitcast.34), custom_call_target="tpu_custom_call" | custom-call | flops 3000000000 | bytes 10000000 | tf_op jit(solution)/shard_map/home/pallas_call | solution.py:198
  213.0 6.1 %collective-permute-done.17 = bf16[256,1536]{1,0:T(8,128)(2,1)S(1)} collective-permute-done((bf16[256,1536]{1,0:T(8,128)(2,1)S(1)}, bf16[256,1536]{1,0:T(8,128)(2,1)S(1)}, u32[]{:S(2)}, u32[]{:S(2)}) %collective-permute-start.17) | collective-permute-done | bytes 786464 | tf_op jit(solution)/shard_map/ppermute | solution.py:45
  219.1 2.2 fusion
  (76 shorter events, 27.2 us)
Async XLA Ops:
  3.0 17.3 %collective-permute-start.2 = (bf16[128,2176]{1,0:T(8,128)(2,1)}, bf16[128,2176]{1,0:T(8,128)(2,1)S(1)}, u32[]{:S(2)}, u32[]{:S(2)}) collective-permute-start(bf16[128,2176]{1,0:T(8,128)(2,1)} %get-tuple-element.78.refs_0_), channel_id=1, source_target_pairs={{0,8},{1,9},{2,10},{3,11},{4,12},{5,13},{6,14},{7,15},{8,0},{9,1},... | collective-permute-start | bytes 1671176 | tf_op jit(solution)/shard_map/ppermute | solution.py:53
  6.1 25.1 %collective-permute-start.1 = (bf16[128,2176]{1,0:T(8,128)(2,1)}, bf16[128,2176]{1,0:T(8,128)(2,1)S(1)}, u32[]{:S(2)}, u32[]{:S(2)}) collective-permute-start(bf16[128,2176]{1,0:T(8,128)(2,1)} %get-tuple-element.78.refs_0_), channel_id=1, source_target_pairs={{0,12},{1,13},{2,14},{3,15},{4,0},{5,1},{6,2},{7,3},{8,4},{9,5},{1... | collective-permute-start | bytes 1671176 | tf_op jit(solution)/shard_map/ppermute | solution.py:53
  7.2 24.0 %collective-permute-start = (bf16[128,2176]{1,0:T(8,128)(2,1)}, bf16[128,2176]{1,0:T(8,128)(2,1)S(1)}, u32[]{:S(2)}, u32[]{:S(2)}) collective-permute-start(bf16[128,2176]{1,0:T(8,128)(2,1)} %get-tuple-element.78.refs_0_), channel_id=1, source_target_pairs={{0,4},{1,5},{2,6},{3,7},{4,8},{5,9},{6,10},{7,11},{8,12},{9,13},{1... | collective-permute-start | bytes 1671176 | tf_op jit(solution)/shard_map/ppermute | solution.py:53
  8.1 33.8 %collective-permute-start.5 = (bf16[128,2176]{1,0:T(8,128)(2,1)}, bf16[128,2176]{1,0:T(8,128)(2,1)S(1)}, u32[]{:S(2)}, u32[]{:S(2)}) collective-permute-start(bf16[128,2176]{1,0:T(8,128)(2,1)} %get-tuple-element.81.refs_0_), channel_id=1, source_target_pairs={{0,2},{1,3},{2,0},{3,1},{4,6},{5,7},{6,4},{7,5},{8,10},{9,11},{10,... | collective-permute-start | bytes 1671176 | tf_op jit(solution)/shard_map/ppermute | solution.py:53
  12.0 29.9 %collective-permute-start.4 = (bf16[128,2176]{1,0:T(8,128)(2,1)}, bf16[128,2176]{1,0:T(8,128)(2,1)S(1)}, u32[]{:S(2)}, u32[]{:S(2)}) collective-permute-start(bf16[128,2176]{1,0:T(8,128)(2,1)} %get-tuple-element.81.refs_0_), channel_id=1, source_target_pairs={{0,3},{1,0},{2,1},{3,2},{4,7},{5,4},{6,5},{7,6},{8,11},{9,8},{10,9... | collective-permute-start | bytes 1671176 | tf_op jit(solution)/shard_map/ppermute | solution.py:53
  20.3 10.9 %copy-start.16 = (bf16[128,2176]{1,0:T(8,128)(2,1)}, bf16[128,2176]{1,0:T(8,128)(2,1)S(1)}, u32[]{:S(2)}) copy-start(bf16[128,2176]{1,0:T(8,128)(2,1)S(1)} %collective-permute-done.2.refs_3_) | copy-start | bytes 1671172
  20.3 21.6 %collective-permute-start.3 = (bf16[128,2176]{1,0:T(8,128)(2,1)}, bf16[128,2176]{1,0:T(8,128)(2,1)}, u32[]{:S(2)}, u32[]{:S(2)}) collective-permute-start(bf16[128,2176]{1,0:T(8,128)(2,1)} %get-tuple-element.81.refs_0_), channel_id=1, source_target_pairs={{0,1},{1,2},{2,3},{3,0},{4,5},{5,6},{6,7},{7,4},{8,9},{9,10},{10,1... | collective-permute-start | bytes 1671176 | tf_op jit(solution)/shard_map/ppermute | solution.py:53
  37.7 30.1 %collective-permute-start.9 = (bf16[288,2048]{1,0:T(8,128)(2,1)}, bf16[288,2048]{1,0:T(8,128)(2,1)S(1)}, u32[]{:S(2)}, u32[]{:S(2)}) collective-permute-start(bf16[288,2048]{1,0:T(8,128)(2,1)} %get-tuple-element.93), channel_id=1, source_target_pairs={{0,1},{1,2},{2,3},{3,0},{4,5},{5,6},{6,7},{7,4},{8,9},{9,10},{10,1... | collective-permute-start | bytes 3538952 | tf_op jit(solution)/shard_map/ppermute | solution.py:53
  39.7 28.2 %collective-permute-start.10 = (bf16[288,2048]{1,0:T(8,128)(2,1)}, bf16[288,2048]{1,0:T(8,128)(2,1)S(1)}, u32[]{:S(2)}, u32[]{:S(2)}) collective-permute-start(bf16[288,2048]{1,0:T(8,128)(2,1)} %get-tuple-element.94), channel_id=1, source_target_pairs={{0,3},{1,0},{2,1},{3,2},{4,7},{5,4},{6,5},{7,6},{8,11},{9,8},{10,9... | collective-permute-start | bytes 3538952 | tf_op jit(solution)/shard_map/ppermute | solution.py:53
  42.9 9.3 %copy-start.13 = (s32[4]{0:T(128)S(1)}, s32[4]{0:T(128)}, u32[]{:S(2)}) copy-start(s32[4]{0:T(128)} %constant.75) | copy-start | bytes 52
  48.9 28.8 %collective-permute-start.6 = (bf16[288,2048]{1,0:T(8,128)(2,1)}, bf16[288,2048]{1,0:T(8,128)(2,1)S(1)}, u32[]{:S(2)}, u32[]{:S(2)}) collective-permute-start(bf16[288,2048]{1,0:T(8,128)(2,1)} %get-tuple-element.83), channel_id=1, source_target_pairs={{0,4},{1,5},{2,6},{3,7},{4,8},{5,9},{6,10},{7,11},{8,12},{9,13},{1... | collective-permute-start | bytes 3538952 | tf_op jit(solution)/shard_map/ppermute | solution.py:53
  50.3 27.6 %collective-permute-start.7 = (bf16[288,2048]{1,0:T(8,128)(2,1)}, bf16[288,2048]{1,0:T(8,128)(2,1)S(1)}, u32[]{:S(2)}, u32[]{:S(2)}) collective-permute-start(bf16[288,2048]{1,0:T(8,128)(2,1)} %get-tuple-element.84), channel_id=1, source_target_pairs={{0,12},{1,13},{2,14},{3,15},{4,0},{5,1},{6,2},{7,3},{8,4},{9,5},{1... | collective-permute-start | bytes 3538952 | tf_op jit(solution)/shard_map/ppermute | solution.py:53
  67.8 7.6 %copy-start.2 = (bf16[288,2048]{1,0:T(8,128)(2,1)}, bf16[288,2048]{1,0:T(8,128)(2,1)S(1)}, u32[]{:S(2)}) copy-start(bf16[288,2048]{1,0:T(8,128)(2,1)S(1)} %collective-permute-done.9.refs_0_.refs_5_.refs_1_) | copy-start | bytes 3538948
  67.9 7.6 %copy-start.3 = (bf16[288,2048]{1,0:T(8,128)(2,1)}, bf16[288,2048]{1,0:T(8,128)(2,1)S(1)}, u32[]{:S(2)}) copy-start(bf16[288,2048]{1,0:T(8,128)(2,1)S(1)} %collective-permute-done.10.refs_1_.refs_6_.refs_2_) | copy-start | bytes 3538948
  67.9 39.4 %collective-permute-start.11 = (bf16[288,2048]{1,0:T(8,128)(2,1)}, bf16[288,2048]{1,0:T(8,128)(2,1)}, u32[]{:S(2)}, u32[]{:S(2)}) collective-permute-start(bf16[288,2048]{1,0:T(8,128)(2,1)} %get-tuple-element.108), channel_id=1, source_target_pairs={{0,2},{1,3},{2,0},{3,1},{4,6},{5,7},{6,4},{7,5},{8,10},{9,11},{10,... | collective-permute-start | bytes 3538952 | tf_op jit(solution)/shard_map/ppermute | solution.py:53
  79.8 33.8 %collective-permute-start.8 = (bf16[288,2048]{1,0:T(8,128)(2,1)}, bf16[288,2048]{1,0:T(8,128)(2,1)S(1)}, u32[]{:S(2)}, u32[]{:S(2)}) collective-permute-start(bf16[288,2048]{1,0:T(8,128)(2,1)} %get-tuple-element.86), channel_id=1, source_target_pairs={{0,8},{1,9},{2,10},{3,11},{4,12},{5,13},{6,14},{7,15},{8,0},{9,1},... | collective-permute-start | bytes 3538952 | tf_op jit(solution)/shard_map/ppermute | solution.py:53
  122.7 24.7 %collective-permute-start.13 = (bf16[768,512]{1,0:T(8,128)(2,1)}, bf16[768,512]{1,0:T(8,128)(2,1)S(1)}, u32[]{:S(2)}, u32[]{:S(2)}) collective-permute-start(bf16[768,512]{1,0:T(8,128)(2,1)} %get-tuple-element.130), channel_id=1, source_target_pairs={{0,16},{16,32},{32,48},{48,0},{1,17},{17,33},{33,49},{49,1},{2,18}... | collective-permute-start | bytes 2359304 | tf_op jit(solution)/shard_map/ppermute | solution.py:45
  124.4 23.1 %collective-permute-start.14 = (bf16[768,512]{1,0:T(8,128)(2,1)}, bf16[768,512]{1,0:T(8,128)(2,1)S(1)}, u32[]{:S(2)}, u32[]{:S(2)}) collective-permute-start(bf16[768,512]{1,0:T(8,128)(2,1)} %get-tuple-element.131), channel_id=1, source_target_pairs={{0,48},{16,0},{32,16},{48,32},{1,49},{17,1},{33,17},{49,33},{2,50}... | collective-permute-start | bytes 2359304 | tf_op jit(solution)/shard_map/ppermute | solution.py:45
  142.7 4.8 %copy-start.8 = (f32[768,512]{1,0:T(8,128)S(1)}, f32[768,512]{1,0:T(8,128)}, u32[]{:S(2)}) copy-start(f32[768,512]{1,0:T(8,128)} %get-tuple-element.149) | copy-start | bytes 4718596
  142.7 65.1 %all-to-all-start = ((bf16[16,72,2048]{2,1,0:T(8,128)(2,1)}), bf16[16,72,2048]{2,1,0:T(8,128)(2,1)}, u32[]{:S(2)}, u32[]{:S(2)}) async-start(bf16[16,72,2048]{2,1,0:T(8,128)(2,1)} %get-tuple-element.125), calls=%async_computation | async-start | bytes 9437184 | tf_op jit(solution)/shard_map/all_to_all | solution.py:711
  148.8 55.8 %collective-permute-start.19 = (bf16[384,512]{1,0:T(8,128)(2,1)}, bf16[384,512]{1,0:T(8,128)(2,1)}, u32[]{:S(2)}, u32[]{:S(2)}) collective-permute-start(bf16[384,512]{1,0:T(8,128)(2,1)} %get-tuple-element.157), channel_id=1, source_target_pairs={{0,16},{16,32},{32,48},{48,0},{1,17},{17,33},{33,49},{49,1},{2,18}... | collective-permute-start | bytes 1179656 | tf_op jit(solution)/shard_map/ppermute | solution.py:45
  149.1 55.5 %collective-permute-start.20 = (bf16[384,512]{1,0:T(8,128)(2,1)}, bf16[384,512]{1,0:T(8,128)(2,1)}, u32[]{:S(2)}, u32[]{:S(2)}) collective-permute-start(bf16[384,512]{1,0:T(8,128)(2,1)} %get-tuple-element.158), channel_id=1, source_target_pairs={{0,48},{16,0},{32,16},{48,32},{1,49},{17,1},{33,17},{49,33},{2,50}... | collective-permute-start | bytes 1179656 | tf_op jit(solution)/shard_map/ppermute | solution.py:45
  163.7 35.8 %collective-permute-start.15 = (bf16[512,1536]{1,0:T(8,128)(2,1)}, bf16[512,1536]{1,0:T(8,128)(2,1)}, u32[]{:S(2)}, u32[]{:S(2)}) collective-permute-start(bf16[512,1536]{1,0:T(8,128)(2,1)} %get-tuple-element.141), channel_id=1, source_target_pairs={{0,16},{16,32},{32,48},{48,0},{1,17},{17,33},{33,49},{49,1},{2,18}... | collective-permute-start | bytes 4718600 | tf_op jit(solution)/shard_map/ppermute | solution.py:45
  163.7 35.7 %collective-permute-start.16 = (bf16[512,1536]{1,0:T(8,128)(2,1)}, bf16[512,1536]{1,0:T(8,128)(2,1)}, u32[]{:S(2)}, u32[]{:S(2)}) collective-permute-start(bf16[512,1536]{1,0:T(8,128)(2,1)} %get-tuple-element.142), channel_id=1, source_target_pairs={{0,48},{16,0},{32,16},{48,32},{1,49},{17,1},{33,17},{49,33},{2,50}... | collective-permute-start | bytes 4718600 | tf_op jit(solution)/shard_map/ppermute | solution.py:45
  173.1 26.4 %copy-start.6 = (f32[512,1536]{1,0:T(8,128)S(1)}, f32[512,1536]{1,0:T(8,128)}, u32[]{:S(2)}) copy-start(f32[512,1536]{1,0:T(8,128)} %get-tuple-element.145) | copy-start | bytes 9437188
  177.0 27.6 %copy-start.1 = (f32[768,512]{1,0:T(8,128)S(1)}, f32[768,512]{1,0:T(8,128)}, u32[]{:S(2)}) copy-start(f32[768,512]{1,0:T(8,128)} %down_own.1) | copy-start | bytes 4718596
  177.0 27.6 %copy-start.10 = (bf16[768,512]{1,0:T(8,128)(2,1)S(1)}, bf16[768,512]{1,0:T(8,128)(2,1)}, u32[]{:S(2)}) copy-start(bf16[768,512]{1,0:T(8,128)(2,1)} %copy-done.9) | copy-start | bytes 2359300
  177.0 27.6 %copy-start.12 = (bf16[768,512]{1,0:T(8,128)(2,1)S(1)}, bf16[768,512]{1,0:T(8,128)(2,1)}, u32[]{:S(2)}) copy-start(bf16[768,512]{1,0:T(8,128)(2,1)} %copy-done.11) | copy-start | bytes 2359300
  201.3 17.7 %collective-permute-start.17 = (bf16[256,1536]{1,0:T(8,128)(2,1)S(1)}, bf16[256,1536]{1,0:T(8,128)(2,1)S(1)}, u32[]{:S(2)}, u32[]{:S(2)}) collective-permute-start(bf16[256,1536]{1,0:T(8,128)(2,1)S(1)} %get-tuple-element.153), channel_id=1, source_target_pairs={{0,16},{16,32},{32,48},{48,0},{1,17},{17,33},{33,49},{49,1},{2,18}... | collective-permute-start | bytes 2359304 | tf_op jit(solution)/shard_map/ppermute | solution.py:45
  201.4 17.7 %collective-permute-start.18 = (bf16[256,1536]{1,0:T(8,128)(2,1)S(1)}, bf16[256,1536]{1,0:T(8,128)(2,1)}, u32[]{:S(2)}, u32[]{:S(2)}) collective-permute-start(bf16[256,1536]{1,0:T(8,128)(2,1)S(1)} %get-tuple-element.154), channel_id=1, source_target_pairs={{0,48},{16,0},{32,16},{48,32},{1,49},{17,1},{33,17},{49,33},{2,50}... | collective-permute-start | bytes 2359304 | tf_op jit(solution)/shard_map/ppermute | solution.py:45
  207.8 11.3 %copy-start.7 = (f32[512,1536]{1,0:T(8,128)S(1)}, f32[512,1536]{1,0:T(8,128)}, u32[]{:S(2)}) copy-start(f32[512,1536]{1,0:T(8,128)} %gate_up_own.1) | copy-start | bytes 9437188
  212.9 9.6 %collective-permute-start.12 = (bf16[128,2048]{1,0:T(8,128)(2,1)}, bf16[128,2048]{1,0:T(8,128)(2,1)S(1)}, u32[]{:S(2)}, u32[]{:S(2)}) collective-permute-start(bf16[128,2048]{1,0:T(8,128)(2,1)} %home.1), channel_id=1, source_target_pairs={{0,64},{64,0},{1,65},{65,1},{2,66},{66,2},{3,67},{67,3},{4,68},{68... | collective-permute-start | bytes 1572872 | tf_op jit(solution)/shard_map/ppermute | solution.py:45
  (9 other events, 9.5 us)
